TPU v7x, 32 devices: a whole 2x2x4 slice. The times are simulated.
32 devices in a mesh: patch: 8 (over z, y), mp: 4 (over x, core).
Axes of the slice: x: 2, y: 2, z: 4, core: 2. Of those that a mesh axis runs over, the one named last changes fastest.
Arguments:
- grid_latent: bfloat16 [8192, 512], P('patch'), may hold values from -6 to 6
- mesh_latent: bfloat16 [1024, 512], P('patch', 'mp'), may hold values from -6 to 6
- edge_weight: bfloat16 [96, 128, 128], P('patch'), may hold values from -0.15625 to 0.15625
- block_source: int32 [96], P('patch'), may hold values from 0 to 63, as said below
- block_live: int32 [96], P('patch'), may hold values from 0 to 1
- mlp_first: bfloat16 [512, 512], replicated, may hold values from -0.25 to 0.25
- mlp_second: bfloat16 [512, 512], P(None, 'mp'), may hold values from -0.25 to 0.25
- mesh_cotangent: bfloat16 [1024, 512], P('patch', 'mp'), may hold values from -6 to 6
Outputs:
- mesh_out: bfloat16 [1024, 512], P('patch', 'mp')
- grad_first: float32 [512, 512], P(None, 'mp')
- grad_second: float32 [512, 512], P(None, 'mp')
Inputs may be any that keep to these rules, and one draw needn't show every extreme that they name: `block_source`: grid patch g lies on the device of index g // 8 along patch, and slot b on the device of index b // 12. On every device at most 2 slots take their source from one device, and some device supplies exactly 2 slots to some device.
All inputs are finite; a program needn't handle non-finite values.
Results may differ from a plain program's by a relative error of at most 0.0058.
Values may be sent and summed in bfloat16 or wider, within the bound.
No kernel may reach another device: no remote copies, remote signals or barrier semaphores. Data moves between devices by JAX's collectives and lax.ppermute only.
A program may use at most 64 MiB of HBM per device.

v0:
```python
import math

import jax
import jax.numpy as jnp
from jax import lax
from jax.sharding import PartitionSpec as P

PATCH = 128
GPD = 8
BPM = 12
MPD = 1
EBD = 12


def silu_slope(values):
    sigmoid = jax.nn.sigmoid(values)
    return sigmoid * (1.0 + values * (1.0 - sigmoid))


def per_device(
    grid_latent,
    mesh_latent,
    edge_weight,
    block_source,
    block_live,
    mlp_first,
    mlp_second,
    mesh_cotangent,
):
    devices = lax.axis_size("patch")
    own_index = lax.axis_index("patch")
    column_index = lax.axis_index("mp")
    grid_rows = grid_latent.shape[0]
    width_local = mlp_second.shape[1]
    hidden_local = mlp_first.shape[1] // lax.axis_size("mp")
    block_width = PATCH * width_local
    slot_cap = (EBD + devices - 1) // devices
    pre_act = jnp.dot(grid_latent, mlp_first, preferred_element_type=jnp.float32)
    hidden = jax.nn.silu(pre_act).astype(jnp.bfloat16)
    message = jnp.dot(hidden, mlp_second, preferred_element_type=jnp.float32).astype(jnp.bfloat16)
    message_flat = message.reshape(GPD, block_width)
    live_local = block_live.astype(jnp.float32)[:, None, None]
    every_source, every_live = (
        lax.all_gather(block_source, "patch", axis=0, tiled=True),
        lax.all_gather(block_live, "patch", axis=0, tiled=True),
    )
    every_source = every_source.reshape(devices, EBD)
    every_live = every_live.reshape(devices, EBD)
    source_device = every_source // GPD
    source_patch = every_source % GPD
    slot_order = jnp.arange(EBD)
    same_source = (source_device[:, :, None] == source_device[:, None, :]) & (
        slot_order[None, None, :] < slot_order[None, :, None]
    )
    slot_rank = jnp.sum(same_source, axis=2)
    own_sources = source_device[own_index]
    own_ranks = slot_rank[own_index]
    wanted = (source_device == own_index) & (every_live == 1)
    matches = (
        wanted[:, :, None, None]
        & (slot_rank[:, :, None, None] == jnp.arange(slot_cap)[None, None, :, None])
        & (source_patch[:, :, None, None] == jnp.arange(GPD)[None, None, None, :])
    )
    picking = jnp.sum(matches, axis=1).reshape(devices * slot_cap, GPD).astype(jnp.bfloat16)
    outgoing = (
        jnp.dot(picking, message_flat, preferred_element_type=jnp.float32)
        .astype(jnp.bfloat16)
        .reshape(devices, slot_cap, block_width)
    )
    incoming = lax.all_to_all(outgoing, "patch", split_axis=0, concat_axis=0, tiled=True).reshape(
        devices * slot_cap, block_width
    )
    lookup = own_sources * slot_cap + own_ranks
    block_input = jnp.take(incoming, lookup, axis=0).reshape(EBD, PATCH, width_local)
    products = (
        jnp.einsum("bpq,bqc->bpc", edge_weight, block_input, preferred_element_type=jnp.float32)
        * live_local
    )
    summed = (
        products.reshape(MPD, BPM, PATCH, width_local).sum(axis=1).reshape(MPD * PATCH, width_local)
    )
    mesh_out = (mesh_latent.astype(jnp.float32) + summed).astype(jnp.bfloat16)
    cotangent_blocks = jnp.broadcast_to(
        mesh_cotangent.reshape(MPD, 1, PATCH, width_local), (MPD, BPM, PATCH, width_local)
    ).reshape(EBD, PATCH, width_local)
    adjoint = (
        jnp.einsum(
            "bqp,bqc->bpc", edge_weight, cotangent_blocks, preferred_element_type=jnp.float32
        )
        * live_local
    ).astype(jnp.bfloat16)
    adjoint = adjoint.reshape(EBD, block_width)
    slot_rows = devices * slot_cap
    scatter_table = (
        (jnp.arange(slot_rows)[:, None] == lookup[None, :]) & (block_live[None, :] == 1)
    ).astype(jnp.bfloat16)
    returning = jnp.dot(scatter_table, adjoint, preferred_element_type=jnp.float32).astype(
        jnp.bfloat16
    )
    back_flat = lax.all_to_all(
        returning.reshape(devices, slot_cap, block_width),
        "patch",
        split_axis=0,
        concat_axis=0,
        tiled=True,
    ).reshape(devices * slot_cap, block_width)
    grad_message = lax.dot_general(
        picking, back_flat, (((0,), (0,)), ((), ())), preferred_element_type=jnp.float32
    )
    grad_message = grad_message.astype(jnp.bfloat16).reshape(grid_rows, width_local)
    scaling = 1.0 / math.sqrt(grid_rows * devices)
    grad_second = (
        lax.dot_general(
            hidden, grad_message, (((0,), (0,)), ((), ())), preferred_element_type=jnp.float32
        )
        * scaling
    )
    grad_hidden = lax.psum_scatter(
        lax.dot_general(
            mlp_second, grad_message, (((1,), (1,)), ((), ())), preferred_element_type=jnp.float32
        ),
        "mp",
        scatter_dimension=0,
        tiled=True,
    )
    pre_slice = lax.dynamic_slice_in_dim(pre_act, column_index * hidden_local, hidden_local, 1).T
    grad_pre = (grad_hidden * silu_slope(pre_slice)).astype(jnp.bfloat16)
    grad_first = (
        lax.dot_general(
            grid_latent, grad_pre, (((0,), (1,)), ((), ())), preferred_element_type=jnp.float32
        )
        * scaling
    )
    grad_first, grad_second = lax.psum((grad_first, grad_second), "patch")
    return (mesh_out, grad_first, grad_second)


def solution(mesh):
    placed = (
        P("patch", None),
        P("patch", "mp"),
        P("patch", None, None),
        P("patch"),
        P("patch"),
        P(),
        P(None, "mp"),
        P("patch", "mp"),
    )
    return jax.shard_map(
        per_device,
        mesh=mesh,
        in_specs=placed,
        out_specs=(P("patch", "mp"), P(None, "mp"), P(None, "mp")),
        check_vma=False,
    )
```

profile of v0, /device:TPU:0, one launch (start us, length us, event | category | flops | bytes accessed | tf_op | source)
XLA Modules:
  0.0 164.8 jit_solution(12187376525085914817)
XLA Ops:
  7.2 0.0 copy-start
  7.2 0.7 convert_element_type.58
  7.9 0.7 broadcast_compare_fusion
  8.6 1.2 dynamic-slice
  10.5 0.9 dynamic-update-slice.1
  11.4 0.8 dynamic-update-slice
  12.2 13.1 %all-reduce.2 = (s32[96]{0:T(128)S(1)}, s32[96]{0:T(128)S(1)}) all-reduce(s32[96]{0:T(128)S(1)} %dynamic-update-slice, s32[96]{0:T(128)S(1)} %dynamic-update-slice.1), channel_id=1, replica_groups=mesh['patch'=8,'mp'=4] {'patch'}, use_global_device_ids=true, to_apply=%add | all-reduce | flops 192 | bytes 1536
  25.3 0.1 reshape.249
  25.3 0.1 eq.95
  25.5 0.1 copy.56
  25.5 0.3 convert_reduce_fusion.1
  25.9 0.1 copy.57
  26.0 1.3 fusion.1
  27.4 0.3 copy.67
  27.7 0.0 copy-start.1
  27.8 0.3 convolution_convert_fusion
  28.0 1.1 reshape.255
  29.2 3.5 %all-to-all-start.1 = ((bf16[8,2,16384]{2,1,0:T(2,128)(2,1)}), bf16[8,2,16384]{2,1,0:T(2,128)(2,1)S(1)}, u32[]{:S(2)}, u32[]{:S(2)}) async-start(bf16[8,2,16384]{2,1,0:T(2,128)(2,1)} %reshape.255), calls=%async_computation.1 | async-start | bytes 1048576 | tf_op jit(solution)/shard_map/all_to_all | solution.py:100
  32.7 0.0 reduce-scatter.2.cloned.1.call-start
  32.8 0.4 convert_reduce_fusion
  33.2 11.3 %all-to-all-done.1 = bf16[8,2,16384]{2,1,0:T(2,128)(2,1)S(1)} async-done(((bf16[8,2,16384]{2,1,0:T(2,128)(2,1)}), bf16[8,2,16384]{2,1,0:T(2,128)(2,1)S(1)}, u32[]{:S(2)}, u32[]{:S(2)}) %all-to-all-start.1) | async-done | bytes 524320 | tf_op jit(solution)/shard_map/all_to_all | solution.py:100
  44.5 0.4 fusion
  44.9 0.1 reshape.256
  45.0 0.0 copy-done.1
  45.0 0.0 copy-start.4
  45.0 1.7 %convolution_bitcast_fusion.1 = f32[512,1024]{0,1:T(8,128)} fusion(bf16[1024,128]{1,0:T(8,128)(2,1)S(1)} %reshape.256, bf16[512,128]{1,0:T(8,128)(2,1)S(1)} %copy-done.1), kind=kOutput, calls=%fused_computation.6 | convolution fusion | flops 134217728 | bytes 2490368 | tf_op jit(solution)/shard_map/dot_general | solution.py:119
  46.8 0.0 reduce-scatter.2.cloned.1.call-update
  46.8 0.0 copy-done
  46.8 0.0 copy-done.4
  46.8 2.2 %multiply_convert_fusion = (bf16[1024,512]{1,0:T(8,128)(2,1)S(1)}, f32[1024,512]{1,0:T(8,128)}) fusion(bf16[1024,512]{1,0:T(8,128)(2,1)S(1)} %copy-done, bf16[512,512]{1,0:T(8,128)(2,1)S(1)} %copy-done.4), kind=kOutput, calls=%fused_computation.5 | convolution fusion | flops 539492352 | bytes 4718592 | tf_op jit(solution)/shard_map/dot_general | solution.py:38
  49.1 0.4 convolution_convert_fusion.2
  49.5 0.1 reshape.250
  49.6 0.3 convolution_convert_fusion.1
  49.9 1.1 reshape.251
  51.1 3.7 %all-to-all-start = ((bf16[8,2,16384]{2,1,0:T(2,128)(2,1)}), bf16[8,2,16384]{2,1,0:T(2,128)(2,1)S(1)}, u32[]{:S(2)}, u32[]{:S(2)}) async-start(bf16[8,2,16384]{2,1,0:T(2,128)(2,1)} %reshape.251), calls=%async_computation | async-start | bytes 1048576 | tf_op jit(solution)/shard_map/all_to_all | solution.py:70
  54.7 0.0 all-reduce.6.cloned.1.call-start
  54.8 1.2 convolution_multiply_fusion.2
  55.9 21.5 %reduce-scatter.2.cloned.1.call-done = f32[128,1024]{0,1:T(8,128)} async-done(((f32[512,1024]{0,1:T(8,128)}), f32[128,1024]{0,1:T(8,128)}) %reduce-scatter.2.cloned.1.call-update) | async-done | bytes 524304 | tf_op jit(solution)/shard_map/reduce_scatter | solution.py:118
  77.4 0.0 copy-start.3
  77.4 2.3 %fusion.3 = f32[512,128]{0,1:T(8,128)} fusion(bf16[1024,512]{1,0:T(8,128)(2,1)S(1)} %copy-done, f32[128,1024]{0,1:T(8,128)} %reduce-scatter.2.cloned.1.call-done, f32[1024,512]{1,0:T(8,128)} %get-tuple-element.27, s32[]{:T(128)S(6)} %select_n.62), kind=kOutput, calls=%fused_computation.14 | convolution fusion | flops 135462912 | bytes 2359300 | tf_op jit(solution)/shard_map/dot_general | solution.py:129
  79.8 0.0 all-reduce.6.cloned.1.call-update
  79.8 0.0 copy-done.3
  79.8 0.1 copy.55
  80.0 0.0 all-to-all-done
  80.0 0.2 reshape.252
  80.2 0.8 gather_fusion
  81.0 0.0 copy-start.2
  81.0 0.1 copy.66
  81.1 0.2 copy.59
  81.4 0.6 copy-done.2
  82.0 0.4 fusion.2
  82.5 0.7 copy.63
  83.2 71.3 %all-reduce.6.cloned.1.call-done = (f32[512,128]{0,1:T(8,128)}, f32[512,128]{1,0:T(8,128)}) async-done(((f32[512,128]{0,1:T(8,128)}, f32[512,128]{1,0:T(8,128)}), (f32[512,128]{0,1:T(8,128)}, f32[512,128]{1,0:T(8,128)})) %all-reduce.6.cloned.1.call-update) | async-done | bytes 524304 | tf_op jit(solution)/shard_map/psum | solution.py:134
  154.5 1.8 %copy.64 = f32[512,128]{1,0:T(8,128)} copy(f32[512,128]{0,1:T(8,128)} %get-tuple-element.20) | data formatting | bytes 524288
  156.3 1.7 %copy.78 = f32[512,128]{1,0:T(8,128)} copy(f32[512,128]{1,0:T(8,128)} %get-tuple-element.30) | data formatting | bytes 524288
  (15 shorter events, 0.2 us)
Async XLA Ops:
  7.2 39.6 %copy-start = (bf16[1024,512]{1,0:T(8,128)(2,1)S(1)}, bf16[1024,512]{1,0:T(8,128)(2,1)}, u32[]{:S(2)}) copy-start(bf16[1024,512]{1,0:T(8,128)(2,1)} %param.8) | copy-start | bytes 3145732
  27.7 17.3 %copy-start.1 = (bf16[512,128]{1,0:T(8,128)(2,1)S(1)}, bf16[512,128]{1,0:T(8,128)(2,1)}, u32[]{:S(2)}) copy-start(bf16[512,128]{1,0:T(8,128)(2,1)} %param.14) | copy-start | bytes 393220
  29.2 15.3 %all-to-all-start.1 = ((bf16[8,2,16384]{2,1,0:T(2,128)(2,1)}), bf16[8,2,16384]{2,1,0:T(2,128)(2,1)S(1)}, u32[]{:S(2)}, u32[]{:S(2)}) async-start(bf16[8,2,16384]{2,1,0:T(2,128)(2,1)} %reshape.255), calls=%async_computation.1 | async-start | bytes 1048576 | tf_op jit(solution)/shard_map/all_to_all | solution.py:100
  32.7 44.8 %reduce-scatter.2.cloned.1.call-start = ((), (), s32[]{:S(2)}) async-start(), calls=%async_computation.3 | async-start | bytes 2621440 | tf_op jit(solution)/shard_map/reduce_scatter | solution.py:118
  45.0 1.8 %copy-start.4 = (bf16[512,512]{1,0:T(8,128)(2,1)S(1)}, bf16[512,512]{1,0:T(8,128)(2,1)}, u32[]{:S(2)}) copy-start(bf16[512,512]{1,0:T(8,128)(2,1)} %param.13) | copy-start | bytes 1572868
  51.1 28.9 %all-to-all-start = ((bf16[8,2,16384]{2,1,0:T(2,128)(2,1)}), bf16[8,2,16384]{2,1,0:T(2,128)(2,1)S(1)}, u32[]{:S(2)}, u32[]{:S(2)}) async-start(bf16[8,2,16384]{2,1,0:T(2,128)(2,1)} %reshape.251), calls=%async_computation | async-start | bytes 1048576 | tf_op jit(solution)/shard_map/all_to_all | solution.py:70
  54.7 99.8 %all-reduce.6.cloned.1.call-start = ((), (), s32[]{:S(2)}) async-start(), calls=%async_computation.4 | async-start | bytes 1048576 | tf_op jit(solution)/shard_map/psum | solution.py:134
  77.4 2.4 %copy-start.3 = (bf16[128,128]{1,0:T(8,128)(2,1)S(1)}, bf16[128,128]{1,0:T(8,128)(2,1)}, u32[]{:S(2)}) copy-start(bf16[128,128]{1,0:T(8,128)(2,1)} %param.9) | copy-start | bytes 98308
  81.0 1.0 copy-start.2
Sparse Core Ops, SparseCore 0:
  46.9 30.4 reduce-scatter.1
  81.9 72.5 all-reduce.5
where the time goes:
time: 165 us
  waiting for transfers between devices  104 us (63%)
  between operations  15 us (9%)
  blocking collectives  13.1 us (8%)
  local copies, waits for them, and re-layouts  12.5 us (8%)
  matrix products  10.7 us (6%)
  starting transfers between devices  7.22 us (4%)
  other arithmetic  2.22 us (1%)
    psum x1, waiting for transfers between devices, per_device(): grad_first, grad_second = lax.psum((grad_first, grad_second), 'patch')  71.3 us
    reduce_scatter x1, waiting for transfers between devices, per_device(): lax.psum_scatter(lax.dot_general(mlp_second, grad_message, (((1,), (1,)),...  21.5 us
    unnamed x1, blocking collectives  13.1 us
    all_to_all x1, waiting for transfers between devices, per_device(): lax.all_to_all(returning.reshape(devices, slot_cap, block_width), 'patch'...  11.3 us
    unnamed x22, local copies, waits for them, and re-layouts  8.34 us
    all_to_all x1, starting transfers between devices, per_device(): lax.all_to_all(outgoing, 'patch', split_axis=0, concat_axis=0, tiled=True)  3.66 us
    all_to_all x1, starting transfers between devices, per_device(): lax.all_to_all(returning.reshape(devices, slot_cap, block_width), 'patch'...  3.49 us
  transfers between devices with their start and end apart: 4, of which 3 were waited for; matrix products, arithmetic and copies ran while one was open for 7% of the time, Pallas kernels for 0%

commit v1 on v0

v1 whole, which is shorter than its diff:
```python
import functools
import math

import jax
import jax.numpy as jnp
from jax import lax
from jax.experimental import pallas as pl
from jax.experimental.pallas import tpu as pltpu
from jax.sharding import PartitionSpec as P

BF16 = jnp.bfloat16
F32 = jnp.float32
INDEX_ROWS = 16
UNROLL = 8
VMEM_BYTES = 40 * 1024 * 1024


def dot(left, right):
    return jnp.dot(left, right, preferred_element_type=F32)


def whole(space=pltpu.VMEM):
    return pl.BlockSpec(memory_space=space)


def params():
    return pltpu.CompilerParams(vmem_limit_bytes=VMEM_BYTES)


def swap(value, axis, offset):
    size = lax.axis_size(axis)
    return lax.ppermute(value, axis, [(i, i ^ offset) for i in range(size)])


def each_device(count, body):
    group = min(count, UNROLL)
    if count == group:
        for step in range(count):
            body(step)
        return

    @pl.loop(0, count // group)
    def _(outer):
        for step in range(group):
            body(outer * group + step)


def pack_kernel(
    patches, cap, source, live, weight, cotangent, second, payload, kept, sent
):
    column = lax.axis_index("mp")
    slots, rows, width = weight.shape
    half = rows // 2
    devices = payload.shape[0]
    first_row = pl.multiple_of((column % 2) * half, half)
    turned = cotangent[...].T
    blank = jnp.zeros((cap * half, width), BF16)
    blank_index = jnp.zeros((INDEX_ROWS, width), BF16)

    def fill(device):
        payload[device, : cap * half] = blank
        payload[device, cap * half : cap * half + turned.shape[0]] = turned
        payload[device, cap * half + turned.shape[0] :] = blank_index

    each_device(devices, fill)
    row = lax.broadcasted_iota(jnp.int32, (INDEX_ROWS, width), 0)
    for slot in range(slots):
        device = source[slot] // patches
        place = source[slot] % patches
        rank = jnp.int32(0)
        for other in range(slot):
            same = (source[other] // patches == device) & (live[other] == 1)
            rank = rank + same.astype(jnp.int32)

        @pl.when(live[slot] == 1)
        def _():
            start = pl.multiple_of(rank * half, half)
            payload[device, pl.ds(start, half)] = weight[slot, pl.ds(first_row, half)]
            tail = pl.ds(cap * half + turned.shape[0], INDEX_ROWS)
            old = payload[device, tail].astype(F32)
            payload[device, tail] = jnp.where(row == rank, place.astype(F32), old).astype(BF16)

    term = lax.dot_general(
        second[...], cotangent[...], (((1,), (1,)), ((), ())), preferred_element_type=F32
    )
    block = term.shape[0] // 2
    upper = column >= lax.axis_size("mp") // 2
    kept[...] = jnp.where(upper, term[block:], term[:block])
    sent[...] = jnp.where(upper, term[:block], term[block:]).astype(BF16)


def local_kernel(latent, first, second, hidden, message, slope, scratch):
    column = lax.axis_index("mp")
    rows = latent.shape[0]
    own = slope.shape[0]
    tile = min(256, rows)
    for start in range(0, rows, tile):
        here = pl.ds(start, tile)
        pre = dot(latent[here], first[...])
        scratch[...] = pre
        value = (pre * jax.nn.sigmoid(pre)).astype(BF16)
        hidden[here] = value
        message[here] = dot(value, second[...]).astype(BF16)
        mine = scratch[:, pl.ds(pl.multiple_of(column * own, own), own)]
        gate = jax.nn.sigmoid(mine)
        slope[:, here] = (gate * (1.0 + mine * (1.0 - gate))).T


def adjoint_kernel(
    cap, scaling, places, received, other, message, hidden, forward, weights, second, total
):
    column = lax.axis_index("mp")
    devices, _, width = received.shape
    half = other.shape[1] // cap
    rows = 2 * half
    patches = message.shape[0] // rows
    mine = pl.ds(pl.multiple_of((column % 2) * half, half), half)
    theirs = pl.ds(pl.multiple_of((1 - column % 2) * half, half), half)
    total[...] = jnp.zeros_like(total)

    def one(device):
        turned = received[device, cap * half : cap * half + width]
        summed = None
        for rank in range(cap):
            slot = device * cap + rank
            place = places[slot]
            weights[slot, mine] = received[device, rank * half : (rank + 1) * half]
            weights[slot, theirs] = other[device, rank * half : (rank + 1) * half]
            block = weights[slot]
            start = pl.multiple_of(place * rows, rows)
            product = dot(block, message[pl.ds(start, rows)])
            summed = product if summed is None else summed + product
            total[place] += dot(turned, block).astype(BF16).astype(F32)
        forward[device] = summed.astype(BF16)

    each_device(devices, one)
    turned_message = jnp.concatenate(
        [total[place].astype(BF16) for place in range(patches)], axis=1
    )
    second[...] = (dot(turned_message, hidden[...]) * scaling).T.astype(BF16)


def first_kernel(cap, scaling, places, weights, carried, slope, latent, first, total):
    own = lax.axis_index("patch")
    devices = carried.shape[0]
    rows = weights.shape[1]
    patches = latent.shape[0] // rows
    total[...] = jnp.zeros_like(total)

    def one(offset):
        turned = carried[offset]
        device = jnp.bitwise_xor(own, offset)
        for rank in range(cap):
            slot = device * cap + rank
            total[places[slot]] += dot(turned, weights[slot])

    each_device(devices, one)
    grad_pre = jnp.concatenate(
        [
            (total[place] * slope[:, place * rows : (place + 1) * rows]).astype(BF16)
            for place in range(patches)
        ],
        axis=1,
    )
    first[...] = (dot(grad_pre, latent[...]) * scaling).T.astype(BF16)


def per_device(
    grid_latent,
    mesh_latent,
    edge_weight,
    block_source,
    block_live,
    mlp_first,
    mlp_second,
    mesh_cotangent,
):
    devices = lax.axis_size("patch")
    parts = lax.axis_size("mp")
    slots, rows, _ = edge_weight.shape
    grid_rows, depth = grid_latent.shape
    patches = grid_rows // rows
    hidden_width, width = mlp_second.shape
    hidden_local = hidden_width // parts
    cap = -(-slots // devices)
    half = rows // 2
    column = lax.axis_index("mp")
    scaling = 1.0 / math.sqrt(grid_rows * devices)
    payload_rows = cap * half + width + INDEX_ROWS

    payload, kept, sent = pl.pallas_call(
        functools.partial(pack_kernel, patches, cap),
        out_shape=(
            jax.ShapeDtypeStruct((devices, payload_rows, rows), BF16),
            jax.ShapeDtypeStruct((hidden_width // 2, rows), F32),
            jax.ShapeDtypeStruct((hidden_width // 2, rows), BF16),
        ),
        in_specs=[whole(pltpu.SMEM)] * 2 + [whole()] * 3,
        out_specs=(whole(),) * 3,
        compiler_params=params(),
        name="pack",
    )(block_source, block_live, edge_weight, mesh_cotangent, mlp_second)

    received = lax.all_to_all(payload, "patch", split_axis=0, concat_axis=0, tiled=True)

    carried = kept + swap(sent, "mp", parts // 2).astype(F32)
    offset = parts // 4
    while offset:
        size = carried.shape[0] // 2
        upper = (column // offset) % 2
        away = lax.dynamic_slice_in_dim(carried, (1 - upper) * size, size, 0)
        stay = lax.dynamic_slice_in_dim(carried, upper * size, size, 0)
        carried = stay + swap(away, "mp", offset)
        offset //= 2
    carried = carried.astype(BF16)[None]
    offset = 1
    while offset < devices:
        carried = jnp.concatenate([carried, swap(carried, "patch", offset)])
        offset *= 2

    hidden, message, slope = pl.pallas_call(
        local_kernel,
        out_shape=(
            jax.ShapeDtypeStruct((grid_rows, hidden_width), BF16),
            jax.ShapeDtypeStruct((grid_rows, width), BF16),
            jax.ShapeDtypeStruct((hidden_local, grid_rows), F32),
        ),
        in_specs=[whole()] * 3,
        out_specs=(whole(),) * 3,
        scratch_shapes=[pltpu.VMEM((min(256, grid_rows), hidden_width), F32)],
        compiler_params=params(),
        cost_estimate=pl.CostEstimate(
            flops=2 * grid_rows * hidden_width * (depth + width),
            bytes_accessed=4 * grid_rows * hidden_width,
            transcendentals=grid_rows * hidden_width,
        ),
        name="local",
    )(grid_latent, mlp_first, mlp_second)

    other = swap(received[:, : cap * half], "mp", 1)
    index_row = cap * half + width
    places = received[:, index_row : index_row + cap, 0].astype(jnp.int32).reshape(-1)

    forward, weights, grad_second = pl.pallas_call(
        functools.partial(adjoint_kernel, cap, scaling),
        out_shape=(
            jax.ShapeDtypeStruct((devices, rows, width), BF16),
            jax.ShapeDtypeStruct((devices * cap, rows, rows), BF16),
            jax.ShapeDtypeStruct((hidden_width, width), BF16),
        ),
        in_specs=[whole(pltpu.SMEM)] + [whole()] * 4,
        out_specs=(whole(),) * 3,
        scratch_shapes=[pltpu.VMEM((patches, width, rows), F32)],
        compiler_params=params(),
        name="adjoint",
    )(places, received, other, message, hidden)

    arrived = lax.all_to_all(forward, "patch", split_axis=0, concat_axis=0, tiled=True)
    mesh_out = (mesh_latent.astype(F32) + jnp.sum(arrived.astype(F32), axis=0)).astype(BF16)

    grad_first = pl.pallas_call(
        functools.partial(first_kernel, cap, scaling),
        out_shape=jax.ShapeDtypeStruct((depth, hidden_local), BF16),
        in_specs=[whole(pltpu.SMEM)] + [whole()] * 4,
        out_specs=whole(),
        scratch_shapes=[pltpu.VMEM((patches, hidden_local, rows), F32)],
        compiler_params=params(),
        name="first",
    )(places, weights, carried, slope, grid_latent)

    both = jnp.stack([grad_first, grad_second])
    offset = 1
    while offset < devices:
        both = both.astype(BF16)
        both = both.astype(F32) + swap(both, "patch", offset).astype(F32)
        offset *= 2
    return (mesh_out, both[0], both[1])


def solution(mesh):
    placed = (
        P("patch", None),
        P("patch", "mp"),
        P("patch", None, None),
        P("patch"),
        P("patch"),
        P(),
        P(None, "mp"),
        P("patch", "mp"),
    )
    return jax.shard_map(
        per_device,
        mesh=mesh,
        in_specs=placed,
        out_specs=(P("patch", "mp"), P(None, "mp"), P(None, "mp")),
        check_vma=False,
    )
```

time: 165 us -> 77.4 us (0.47)
  waiting for transfers between devices: 104 us -> 35.2 us
  starting transfers between devices: 7.22 us -> 22.2 us
  between operations: 15 us -> 0.83 us
  blocking collectives: 13.1 us -> 0 us
  matrix products: 10.7 us -> 0 us
  Pallas kernels: 0 us -> 6.69 us
  local copies, waits for them, and re-layouts: 12.5 us -> 9.1 us
    psum x1 -> x0, waiting for transfers between devices: 71.3 us -> none  [per_device(): grad_first, grad_second = lax.psum((grad_first, grad_second), 'patch')]
    ppermute x0 -> x9, waiting for transfers between devices: none -> 23.2 us  [swap(): return lax.ppermute(value, axis, [(i, i ^ offset) for i in range(size)])]
    reduce_scatter x1 -> x0, waiting for transfers between devices: 21.5 us -> none  [per_device(): lax.psum_scatter(lax.dot_general(mlp_second, grad_message, (((1,), (1,)),...]
    unnamed x1 -> x0, blocking collectives: 13.1 us -> none
    ppermute x0 -> x9, starting transfers between devices: none -> 13 us  [swap(): return lax.ppermute(value, axis, [(i, i ^ offset) for i in range(size)])]
    dot_general x10 -> x0, matrix products: 10.7 us -> none  [the longest x1 2.34 us: per_device(): lax.dot_general(grid_latent, grad_pre, (((0,), (1,)), ((), ())), preferre...]
    pallas_call x0 -> x4, Pallas kernels: none -> 6.69 us  [the longest x1 2.02 us: per_device(): pl.pallas_call(functools.partial(pack_kernel, patches, cap), out_shape=(j...]
    reshape x6 -> x0, local copies, waits for them, and re-layouts: 2.8 us -> none  [the longest x1 1.15 us: per_device(): outgoing = jnp.dot(picking, message_flat, preferred_element_type=jnp.floa...]
  transfers between devices with their start and end apart: 4 -> 11, of which waited for: 3 -> 7; matrix products, arithmetic and copies ran while one was open for 7% -> 4% of each run, Pallas kernels for 0% -> 2%
where the time goes in v1:
time: 77.4 us; the launch traced here: 76.8 us
  waiting for transfers between devices  35.2 us (45%)
  starting transfers between devices  22.2 us (29%)
  local copies, waits for them, and re-layouts  9.1 us (12%)
  Pallas kernels  6.69 us (9%)
  other arithmetic  2.77 us (4%)
  between operations  0.83 us (1%)
    ppermute x9, waiting for transfers between devices, swap(): return lax.ppermute(value, axis, [(i, i ^ offset) for i in range(size)])  23.2 us
    ppermute x9, starting transfers between devices, swap(): return lax.ppermute(value, axis, [(i, i ^ offset) for i in range(size)])  13 us
    all_to_all x1, waiting for transfers between devices, per_device(): lax.all_to_all(forward, 'patch', split_axis=0, concat_axis=0, tiled=True)  12 us
    unnamed x26, local copies, waits for them, and re-layouts  7.46 us
    all_to_all x1, starting transfers between devices, per_device(): lax.all_to_all(payload, 'patch', split_axis=0, concat_axis=0, tiled=True)  5.83 us
    all_to_all x1, starting transfers between devices, per_device(): lax.all_to_all(forward, 'patch', split_axis=0, concat_axis=0, tiled=True)  3.41 us
    pallas_call x1, Pallas kernels, per_device(): pl.pallas_call(functools.partial(pack_kernel, patches, cap), out_shape=(j...  2.02 us
    pallas_call x1, Pallas kernels, per_device(): pl.pallas_call(functools.partial(adjoint_kernel, cap, scaling), out_shape...  1.92 us
  transfers between devices with their start and end apart: 11, of which 7 were waited for; matrix products, arithmetic and copies ran while one was open for 4% of the time, Pallas kernels for 2%

profile of v1, /device:TPU:0, one launch (start us, length us, event | category | flops | bytes accessed | tf_op | source)
XLA Modules:
  0.0 76.8 jit_solution(6800197462799309033)
XLA Ops:
  0.6 0.0 copy-start.3
  0.6 1.0 %copy-done.3 = bf16[12,128,128]{2,1,0:T(8,128)(2,1)S(1)} copy-done((bf16[12,128,128]{2,1,0:T(8,128)(2,1)S(1)}, bf16[12,128,128]{2,1,0:T(8,128)(2,1)}, u32[]{:S(2)}) %copy-start.3) | copy-done | bytes 393240
  1.6 0.0 copy-start.6
  1.6 0.9 %copy-done.6 = bf16[512,128]{1,0:T(8,128)(2,1)S(1)} copy-done((bf16[512,128]{1,0:T(8,128)(2,1)S(1)}, bf16[512,128]{1,0:T(8,128)(2,1)}, u32[]{:S(2)}) %copy-start.6) | copy-done | bytes 131096
  2.5 0.0 copy-start.8
  2.5 0.8 copy-done.8
  3.3 0.0 copy-start.9
  3.3 0.7 copy-done.9
  3.9 0.0 copy-start.10
  3.9 0.7 copy-done.10
  4.6 2.0 %pack.1 = (bf16[8,272,128]{2,1,0:T(8,128)(2,1)}, f32[256,128]{1,0:T(8,128)S(1)}, bf16[256,128]{1,0:T(8,128)(2,1)S(1)}) custom-call(s32[12]{0:T(128)S(1)} %copy-done.9, s32[12]{0:T(128)S(1)} %copy-done.10, bf16[12,128,128]{2,1,0:T(8,128)(2,1)S(1)} %copy-done.3, bf16[128,128]{1,0:T(8,128)(2,1)S(1)} %copy-done.8, bf16[512,128]{1,0:T(8,128)(2,1)S(1)} %copy-done.6), custom_call_target="tpu_custom_call" | custom-call | tf_op jit(solution)/shard_map/pack/pallas_call | solution.py:191
  6.6 2.9 %collective-permute-start.1 = (bf16[256,128]{1,0:T(8,128)(2,1)S(1)}, bf16[256,128]{1,0:T(8,128)(2,1)S(1)}, u32[]{:S(2)}, u32[]{:S(2)}) collective-permute-start(bf16[256,128]{1,0:T(8,128)(2,1)S(1)} %get-tuple-element.18), channel_id=1, source_target_pairs={{0,2},{1,3},{2,0},{3,1},{4,6},{5,7},{6,4},{7,5},{8,10},{9,11},{10,... | collective-permute-start | bytes 196616 | tf_op jit(solution)/shard_map/ppermute | solution.py:32
  9.6 5.8 %all-to-all-start = ((bf16[8,272,128]{2,1,0:T(8,128)(2,1)}), bf16[8,272,128]{2,1,0:T(8,128)(2,1)S(1)}, u32[]{:S(2)}, u32[]{:S(2)}) async-start(bf16[8,272,128]{2,1,0:T(8,128)(2,1)} %get-tuple-element.12), calls=%async_computation | async-start | bytes 1114112 | tf_op jit(solution)/shard_map/all_to_all | solution.py:204
  15.4 0.0 copy-start
  15.4 0.0 collective-permute-done.1
  15.5 0.1 collective-permute-start.2
  15.6 1.2 %collective-permute-done.2 = f32[128,128]{1,0:T(8,128)S(1)} collective-permute-done((f32[128,128]{1,0:T(8,128)S(1)}, f32[128,128]{1,0:T(8,128)S(1)}, u32[]{:S(2)}, u32[]{:S(2)}) %collective-permute-start.2) | collective-permute-done | bytes 65568 | tf_op jit(solution)/shard_map/ppermute | solution.py:32
  16.8 2.1 %collective-permute-start.3 = (bf16[1,128,128]{2,1,0:T(8,128)(2,1)S(1)}, bf16[1,128,128]{2,1,0:T(8,128)(2,1)S(1)}, u32[]{:S(2)}, u32[]{:S(2)}) collective-permute-start(bf16[1,128,128]{2,1,0:T(8,128)(2,1)S(1)} %fusion), channel_id=1, source_target_pairs={{0,4},{4,0},{8,12},{12,8},{16,20},{20,16},{24,28},{28,24},{1,5},{5... | collective-permute-start | bytes 98312 | tf_op jit(solution)/shard_map/ppermute | solution.py:32
  18.9 4.0 %collective-permute-done.3 = bf16[1,128,128]{2,1,0:T(8,128)(2,1)S(1)} collective-permute-done((bf16[1,128,128]{2,1,0:T(8,128)(2,1)S(1)}, bf16[1,128,128]{2,1,0:T(8,128)(2,1)S(1)}, u32[]{:S(2)}, u32[]{:S(2)}) %collective-permute-start.3) | collective-permute-done | bytes 32800 | tf_op jit(solution)/shard_map/ppermute | solution.py:32
  22.9 0.2 collective-permute-start.4
  23.1 4.5 %collective-permute-done.4 = bf16[2,128,128]{2,1,0:T(8,128)(2,1)S(1)} collective-permute-done((bf16[2,128,128]{2,1,0:T(8,128)(2,1)S(1)}, bf16[2,128,128]{2,1,0:T(8,128)(2,1)S(1)}, u32[]{:S(2)}, u32[]{:S(2)}) %collective-permute-start.4) | collective-permute-done | bytes 65568 | tf_op jit(solution)/shard_map/ppermute | solution.py:32
  27.6 0.7 pad_maximum_fusion.2
  28.3 0.0 copy-start.7
  28.3 2.7 %collective-permute-start.5 = (bf16[4,128,128]{2,1,0:T(8,128)(2,1)}, bf16[4,128,128]{2,1,0:T(8,128)(2,1)}, u32[]{:S(2)}, u32[]{:S(2)}) collective-permute-start(bf16[4,128,128]{2,1,0:T(8,128)(2,1)} %pad_maximum_fusion.2), channel_id=1, source_target_pairs={{0,16},{4,20},{8,24},{12,28},{16,0},{20,4},{24,8},{28,12},{1,17},{... | collective-permute-start | bytes 393224 | tf_op jit(solution)/shard_map/ppermute | solution.py:32
  31.0 0.0 all-to-all-done.received
  31.0 0.7 slice.17
  31.7 0.0 collective-permute-start
  31.7 0.0 copy-done
  31.7 0.0 copy-done.7
  31.7 0.0 copy-start.11
  31.7 1.0 %copy-done.11 = bf16[512,512]{1,0:T(8,128)(2,1)S(1)} copy-done((bf16[512,512]{1,0:T(8,128)(2,1)S(1)}, bf16[512,512]{1,0:T(8,128)(2,1)}, u32[]{:S(2)}) %copy-start.11) | copy-done | bytes 524312
  32.8 1.5 %local.1 = (bf16[1024,512]{1,0:T(8,128)(2,1)S(1)}, bf16[1024,128]{1,0:T(8,128)(2,1)S(1)}, f32[128,1024]{1,0:T(8,128)S(1)}) custom-call(bf16[1024,512]{1,0:T(8,128)(2,1)S(1)} %copy-done, bf16[512,512]{1,0:T(8,128)(2,1)S(1)} %copy-done.11, bf16[512,128]{1,0:T(8,128)(2,1)S(1)} %copy-done.7), custom_call_target="tpu_custom_call" | custom-call | flops 671088640 | bytes 2097152 | tf_op jit(solution)/shard_map/local/pallas_call | solution.py:221
  34.3 0.0 copy-start.1
  34.3 0.8 %copy-done.1 = f32[128,1024]{1,0:T(8,128)} copy-done((f32[128,1024]{1,0:T(8,128)}, f32[128,1024]{1,0:T(8,128)S(1)}, u32[]{:S(2)}) %copy-start.1) | copy-done | bytes 524312
  35.1 0.0 copy-start.4
  35.1 0.7 copy-done.4
  35.8 0.0 collective-permute-done.5
  35.8 0.9 %pad_maximum_fusion.carried = bf16[8,128,128]{2,1,0:T(8,128)(2,1)S(1)} fusion(bf16[4,128,128]{2,1,0:T(8,128)(2,1)} %collective-permute-done.5, bf16[2,128,128]{2,1,0:T(8,128)(2,1)S(1)} %collective-permute-done.4, bf16[1,128,128]{2,1,0:T(8,128)(2,1)S(1)} %collective-permute-done.3, bf16[1,128,128]{2,1,0:T(8,128)(2,1)S(1)} %fusion), kind=kLoop, calls=%fused_computation.6 | loop fusion | flops 393216 | bytes 524288 | tf_op jit(solution)/shard_map/concatenate | solution.py:218
  36.7 0.2 convert_reduce_fusion.1
  37.0 0.1 reshape.10.places
  37.0 0.0 collective-permute-done.other
  37.1 0.0 copy-start.5
  37.1 0.9 %copy-done.5 = bf16[1024,128]{1,0:T(8,128)(2,1)S(1)} copy-done((bf16[1024,128]{1,0:T(8,128)(2,1)S(1)}, bf16[1024,128]{1,0:T(8,128)(2,1)}, u32[]{:S(2)}) %copy-start.5) | copy-done | bytes 262168
  38.0 0.0 copy-start.2
  38.0 1.9 %adjoint.1 = (bf16[8,128,128]{2,1,0:T(8,128)(2,1)}, bf16[16,128,128]{2,1,0:T(8,128)(2,1)S(1)}, bf16[512,128]{1,0:T(8,128)(2,1)S(1)}) custom-call(s32[16]{0:T(128)S(1)} %reshape.10.places, bf16[8,272,128]{2,1,0:T(8,128)(2,1)S(1)} %all-to-all-done.received, bf16[8,128,128]{2,1,0:T(8,128)(2,1)S(1)} %collective-permute-done.other, ...), custom_call_target="tpu_custom_call" | custom-call | tf_op jit(solution)/shard_map/adjoint/pallas_call | solution.py:244
  39.9 0.0 copy-done.2
  39.9 1.2 %first.3 = bf16[512,128]{1,0:T(8,128)(2,1)S(1)} custom-call(s32[16]{0:T(128)S(1)} %reshape.10.places, bf16[16,128,128]{2,1,0:T(8,128)(2,1)S(1)} %get-tuple-element.16.weights, bf16[8,128,128]{2,1,0:T(8,128)(2,1)S(1)} %pad_maximum_fusion.carried, f32[128,1024]{1,0:T(8,128)S(1)} %copy-done.2, bf16[1024,512]{1,0:T(8,128)(2,1)S(1)} %copy-done), custom_call_target="tpu_custom_call" | custom-call | tf_op jit(solution)/shard_map/first/pallas_call | solution.py:261
  41.2 2.5 %collective-permute-start.6 = (bf16[2,512,128]{2,1,0:T(8,128)(2,1)S(1)}, bf16[2,512,128]{2,1,0:T(8,128)(2,1)S(1)}, u32[]{:S(2)}, u32[]{:S(2)}) collective-permute-start(bf16[2,512,128]{2,1,0:T(8,128)(2,1)S(1)} %pad_maximum_fusion.1), channel_id=1, source_target_pairs={{0,4},{4,0},{8,12},{12,8},{16,20},{20,16},{24,28},{28,24},{1,5},{5... | collective-permute-start | bytes 786440 | tf_op jit(solution)/shard_map/ppermute | solution.py:32
  43.7 6.3 %collective-permute-done.6 = bf16[2,512,128]{2,1,0:T(8,128)(2,1)S(1)} collective-permute-done((bf16[2,512,128]{2,1,0:T(8,128)(2,1)S(1)}, bf16[2,512,128]{2,1,0:T(8,128)(2,1)S(1)}, u32[]{:S(2)}, u32[]{:S(2)}) %collective-permute-start.6) | collective-permute-done | bytes 262176 | tf_op jit(solution)/shard_map/ppermute | solution.py:32
  50.0 0.1 add_convert_fusion.1
  50.1 2.5 %collective-permute-start.7 = (bf16[2,512,128]{2,1,0:T(8,128)(2,1)S(1)}, bf16[2,512,128]{2,1,0:T(8,128)(2,1)S(1)}, u32[]{:S(2)}, u32[]{:S(2)}) collective-permute-start(bf16[2,512,128]{2,1,0:T(8,128)(2,1)S(1)} %add_convert_fusion.1), channel_id=1, source_target_pairs={{0,8},{4,12},{8,0},{12,4},{16,24},{20,28},{24,16},{28,20},{1,9},{5... | collective-permute-start | bytes 786440 | tf_op jit(solution)/shard_map/ppermute | solution.py:32
  52.6 3.4 %all-to-all-start.1 = ((bf16[8,128,128]{2,1,0:T(8,128)(2,1)}), bf16[8,128,128]{2,1,0:T(8,128)(2,1)S(1)}, u32[]{:S(2)}, u32[]{:S(2)}) async-start(bf16[8,128,128]{2,1,0:T(8,128)(2,1)} %get-tuple-element.15), calls=%async_computation.1 | async-start | bytes 524288 | tf_op jit(solution)/shard_map/all_to_all | solution.py:258
  56.0 3.3 %collective-permute-done.7 = bf16[2,512,128]{2,1,0:T(8,128)(2,1)S(1)} collective-permute-done((bf16[2,512,128]{2,1,0:T(8,128)(2,1)S(1)}, bf16[2,512,128]{2,1,0:T(8,128)(2,1)S(1)}, u32[]{:S(2)}, u32[]{:S(2)}) %collective-permute-start.7) | collective-permute-done | bytes 262176 | tf_op jit(solution)/shard_map/ppermute | solution.py:32
  59.3 0.1 add_convert_fusion
  59.4 0.0 copy-start.12
  59.5 0.1 collective-permute-start.8
  59.5 12.0 %all-to-all-done.1 = bf16[8,128,128]{2,1,0:T(8,128)(2,1)S(1)} async-done(((bf16[8,128,128]{2,1,0:T(8,128)(2,1)}), bf16[8,128,128]{2,1,0:T(8,128)(2,1)S(1)}, u32[]{:S(2)}, u32[]{:S(2)}) %all-to-all-start.1) | async-done | bytes 262176 | tf_op jit(solution)/shard_map/all_to_all | solution.py:258
  71.6 0.0 copy-done.12
  71.6 0.6 add_convert_fusion.3
  72.2 3.7 %collective-permute-done.8 = bf16[2,512,128]{2,1,0:T(8,128)(2,1)S(1)} collective-permute-done((bf16[2,512,128]{2,1,0:T(8,128)(2,1)S(1)}, bf16[2,512,128]{2,1,0:T(8,128)(2,1)S(1)}, u32[]{:S(2)}, u32[]{:S(2)}) %collective-permute-start.8) | collective-permute-done | bytes 262176 | tf_op jit(solution)/shard_map/ppermute | solution.py:32
  76.0 0.1 convert_add_fusion
  76.0 0.8 %slice_bitcast_fusion = (f32[512,128]{1,0:T(8,128)}, f32[512,128]{1,0:T(8,128)}) fusion(f32[2,512,128]{2,1,0:T(8,128)S(1)} %convert_add_fusion), kind=kLoop, calls=%fused_computation.4 | loop fusion | bytes 1048576 | tf_op jit(solution)/shard_map/squeeze | solution.py:277
  (6 shorter events, 0.1 us)
Async XLA Ops:
  0.6 1.0 %copy-start.3 = (bf16[12,128,128]{2,1,0:T(8,128)(2,1)S(1)}, bf16[12,128,128]{2,1,0:T(8,128)(2,1)}, u32[]{:S(2)}) copy-start(bf16[12,128,128]{2,1,0:T(8,128)(2,1)} %weight.1) | copy-start | bytes 1179652
  1.6 0.9 %copy-start.6 = (bf16[512,128]{1,0:T(8,128)(2,1)S(1)}, bf16[512,128]{1,0:T(8,128)(2,1)}, u32[]{:S(2)}) copy-start(bf16[512,128]{1,0:T(8,128)(2,1)} %second.3) | copy-start | bytes 393220
  2.5 0.8 copy-start.8
  3.3 0.7 copy-start.9
  3.9 0.7 copy-start.10
  6.6 8.8 %collective-permute-start.1 = (bf16[256,128]{1,0:T(8,128)(2,1)S(1)}, bf16[256,128]{1,0:T(8,128)(2,1)S(1)}, u32[]{:S(2)}, u32[]{:S(2)}) collective-permute-start(bf16[256,128]{1,0:T(8,128)(2,1)S(1)} %get-tuple-element.18), channel_id=1, source_target_pairs={{0,2},{1,3},{2,0},{3,1},{4,6},{5,7},{6,4},{7,5},{8,10},{9,11},{10,... | collective-permute-start | bytes 196616 | tf_op jit(solution)/shard_map/ppermute | solution.py:32
  9.6 21.4 %all-to-all-start = ((bf16[8,272,128]{2,1,0:T(8,128)(2,1)}), bf16[8,272,128]{2,1,0:T(8,128)(2,1)S(1)}, u32[]{:S(2)}, u32[]{:S(2)}) async-start(bf16[8,272,128]{2,1,0:T(8,128)(2,1)} %get-tuple-element.12), calls=%async_computation | async-start | bytes 1114112 | tf_op jit(solution)/shard_map/all_to_all | solution.py:204
  15.4 16.3 %copy-start = (bf16[1024,512]{1,0:T(8,128)(2,1)S(1)}, bf16[1024,512]{1,0:T(8,128)(2,1)}, u32[]{:S(2)}) copy-start(bf16[1024,512]{1,0:T(8,128)(2,1)} %latent.3) | copy-start | bytes 3145732
  15.5 1.3 %collective-permute-start.2 = (f32[128,128]{1,0:T(8,128)S(1)}, f32[128,128]{1,0:T(8,128)S(1)}, u32[]{:S(2)}, u32[]{:S(2)}) collective-permute-start(f32[128,128]{1,0:T(8,128)S(1)} %constant_dynamic-slice_fusion), channel_id=1, source_target_pairs={{0,1},{1,0},{2,3},{3,2},{4,5},{5,4},{6,7},{7,6},{8,9},{9,8},{10,11... | collective-permute-start | bytes 196616 | tf_op jit(solution)/shard_map/ppermute | solution.py:32
  16.8 6.1 %collective-permute-start.3 = (bf16[1,128,128]{2,1,0:T(8,128)(2,1)S(1)}, bf16[1,128,128]{2,1,0:T(8,128)(2,1)S(1)}, u32[]{:S(2)}, u32[]{:S(2)}) collective-permute-start(bf16[1,128,128]{2,1,0:T(8,128)(2,1)S(1)} %fusion), channel_id=1, source_target_pairs={{0,4},{4,0},{8,12},{12,8},{16,20},{20,16},{24,28},{28,24},{1,5},{5... | collective-permute-start | bytes 98312 | tf_op jit(solution)/shard_map/ppermute | solution.py:32
  22.9 4.7 %collective-permute-start.4 = (bf16[2,128,128]{2,1,0:T(8,128)(2,1)S(1)}, bf16[2,128,128]{2,1,0:T(8,128)(2,1)S(1)}, u32[]{:S(2)}, u32[]{:S(2)}) collective-permute-start(bf16[2,128,128]{2,1,0:T(8,128)(2,1)S(1)} %pad_maximum_fusion.3), channel_id=1, source_target_pairs={{0,8},{4,12},{8,0},{12,4},{16,24},{20,28},{24,16},{28,20},{1,9},{5... | collective-permute-start | bytes 196616 | tf_op jit(solution)/shard_map/ppermute | solution.py:32
  28.3 3.4 %copy-start.7 = (bf16[512,128]{1,0:T(8,128)(2,1)S(1)}, bf16[512,128]{1,0:T(8,128)(2,1)}, u32[]{:S(2)}) copy-start(bf16[512,128]{1,0:T(8,128)(2,1)} %second.3) | copy-start | bytes 393220
  28.3 7.5 %collective-permute-start.5 = (bf16[4,128,128]{2,1,0:T(8,128)(2,1)}, bf16[4,128,128]{2,1,0:T(8,128)(2,1)}, u32[]{:S(2)}, u32[]{:S(2)}) collective-permute-start(bf16[4,128,128]{2,1,0:T(8,128)(2,1)} %pad_maximum_fusion.2), channel_id=1, source_target_pairs={{0,16},{4,20},{8,24},{12,28},{16,0},{20,4},{24,8},{28,12},{1,17},{... | collective-permute-start | bytes 393224 | tf_op jit(solution)/shard_map/ppermute | solution.py:32
  31.7 5.3 %collective-permute-start = (bf16[8,128,128]{2,1,0:T(8,128)(2,1)}, bf16[8,128,128]{2,1,0:T(8,128)(2,1)S(1)}, u32[]{:S(2)}, u32[]{:S(2)}) collective-permute-start(bf16[8,128,128]{2,1,0:T(8,128)(2,1)} %slice.17), channel_id=1, source_target_pairs={{0,1},{1,0},{2,3},{3,2},{4,5},{5,4},{6,7},{7,6},{8,9},{9,8},{10,11... | collective-permute-start | bytes 786440 | tf_op jit(solution)/shard_map/ppermute | solution.py:32
  31.7 1.0 %copy-start.11 = (bf16[512,512]{1,0:T(8,128)(2,1)S(1)}, bf16[512,512]{1,0:T(8,128)(2,1)}, u32[]{:S(2)}) copy-start(bf16[512,512]{1,0:T(8,128)(2,1)} %first.2) | copy-start | bytes 1572868
  34.3 0.8 %copy-start.1 = (f32[128,1024]{1,0:T(8,128)}, f32[128,1024]{1,0:T(8,128)S(1)}, u32[]{:S(2)}) copy-start(f32[128,1024]{1,0:T(8,128)S(1)} %get-tuple-element.19.slope) | copy-start | bytes 1572868
  35.1 0.7 copy-start.4
  37.1 1.0 %copy-start.5 = (bf16[1024,128]{1,0:T(8,128)(2,1)S(1)}, bf16[1024,128]{1,0:T(8,128)(2,1)}, u32[]{:S(2)}) copy-start(bf16[1024,128]{1,0:T(8,128)(2,1)} %copy-done.4) | copy-start | bytes 786436
  38.0 1.9 %copy-start.2 = (f32[128,1024]{1,0:T(8,128)S(1)}, f32[128,1024]{1,0:T(8,128)}, u32[]{:S(2)}) copy-start(f32[128,1024]{1,0:T(8,128)} %copy-done.1) | copy-start | bytes 1572868
  41.2 8.8 %collective-permute-start.6 = (bf16[2,512,128]{2,1,0:T(8,128)(2,1)S(1)}, bf16[2,512,128]{2,1,0:T(8,128)(2,1)S(1)}, u32[]{:S(2)}, u32[]{:S(2)}) collective-permute-start(bf16[2,512,128]{2,1,0:T(8,128)(2,1)S(1)} %pad_maximum_fusion.1), channel_id=1, source_target_pairs={{0,4},{4,0},{8,12},{12,8},{16,20},{20,16},{24,28},{28,24},{1,5},{5... | collective-permute-start | bytes 786440 | tf_op jit(solution)/shard_map/ppermute | solution.py:32
  50.1 9.3 %collective-permute-start.7 = (bf16[2,512,128]{2,1,0:T(8,128)(2,1)S(1)}, bf16[2,512,128]{2,1,0:T(8,128)(2,1)S(1)}, u32[]{:S(2)}, u32[]{:S(2)}) collective-permute-start(bf16[2,512,128]{2,1,0:T(8,128)(2,1)S(1)} %add_convert_fusion.1), channel_id=1, source_target_pairs={{0,8},{4,12},{8,0},{12,4},{16,24},{20,28},{24,16},{28,20},{1,9},{5... | collective-permute-start | bytes 786440 | tf_op jit(solution)/shard_map/ppermute | solution.py:32
  52.6 19.0 %all-to-all-start.1 = ((bf16[8,128,128]{2,1,0:T(8,128)(2,1)}), bf16[8,128,128]{2,1,0:T(8,128)(2,1)S(1)}, u32[]{:S(2)}, u32[]{:S(2)}) async-start(bf16[8,128,128]{2,1,0:T(8,128)(2,1)} %get-tuple-element.15), calls=%async_computation.1 | async-start | bytes 524288 | tf_op jit(solution)/shard_map/all_to_all | solution.py:258
  59.4 12.1 %copy-start.12 = (bf16[128,128]{1,0:T(8,128)(2,1)S(1)}, bf16[128,128]{1,0:T(8,128)(2,1)}, u32[]{:S(2)}) copy-start(bf16[128,128]{1,0:T(8,128)(2,1)} %param.9) | copy-start | bytes 98308
  59.5 16.5 %collective-permute-start.8 = (bf16[2,512,128]{2,1,0:T(8,128)(2,1)S(1)}, bf16[2,512,128]{2,1,0:T(8,128)(2,1)S(1)}, u32[]{:S(2)}, u32[]{:S(2)}) collective-permute-start(bf16[2,512,128]{2,1,0:T(8,128)(2,1)S(1)} %add_convert_fusion), channel_id=1, source_target_pairs={{0,16},{4,20},{8,24},{12,28},{16,0},{20,4},{24,8},{28,12},{1,17},{... | collective-permute-start | bytes 786440 | tf_op jit(solution)/shard_map/ppermute | solution.py:32

commit v2 on v1

v2 whole, which is shorter than its diff:
```python
import functools
import math

import jax
import jax.numpy as jnp
from jax import lax
from jax.experimental import pallas as pl
from jax.experimental.pallas import tpu as pltpu
from jax.sharding import PartitionSpec as P

BF16 = jnp.bfloat16
F32 = jnp.float32
INDEX_ROWS = 16
UNROLL = 8
VMEM_BYTES = 16 * 1024 * 1024
VMEM = pltpu.VMEM
SMEM = pltpu.SMEM
HBM = pltpu.HBM


def dot(left, right):
    return jnp.dot(left, right, preferred_element_type=F32)


def call(kernel, name, placed, outputs, scratch=(), cost=None):
    return pl.pallas_call(
        kernel,
        out_shape=[VMEM(shape, dtype) for shape, dtype in outputs],
        in_specs=[pl.BlockSpec(memory_space=space) for space, _ in placed],
        out_specs=[pl.BlockSpec(memory_space=VMEM) for _ in outputs],
        scratch_shapes=list(scratch),
        compiler_params=pltpu.CompilerParams(vmem_limit_bytes=VMEM_BYTES),
        cost_estimate=cost,
        name=name,
    )(
        *[
            operand if space is SMEM else pltpu.with_memory_space_constraint(operand, space)
            for space, operand in placed
        ]
    )


def fetch(pairs, arrivals):
    copies = [
        pltpu.make_async_copy(source, target, arrivals.at[place])
        for place, (source, target) in enumerate(pairs)
    ]
    for copy in copies:
        copy.start()
    return copies


def after(value, *others):
    return lax.optimization_barrier((value, *others))[0]


def swap(value, axis, offset):
    size = lax.axis_size(axis)
    return lax.ppermute(value, axis, [(i, i ^ offset) for i in range(size)])


def each_device(count, body):
    group = min(count, UNROLL)
    if count == group:
        for step in range(count):
            body(step)
        return

    @pl.loop(0, count // group)
    def _(outer):
        for step in range(group):
            body(outer * group + step)


def term_kernel(
    cotangent_hbm, second_hbm, kept, sent, turned, cotangent, second, arrivals
):
    for copy in fetch([(cotangent_hbm, cotangent), (second_hbm, second)], arrivals):
        copy.wait()
    turned[...] = cotangent[...].T
    column = lax.axis_index("mp")
    term = lax.dot_general(
        second[...], cotangent[...], (((1,), (1,)), ((), ())), preferred_element_type=F32
    )
    block = term.shape[0] // 2
    upper = column >= lax.axis_size("mp") // 2
    kept[...] = jnp.where(upper, term[block:], term[:block])
    sent[...] = jnp.where(upper, term[:block], term[block:]).astype(BF16)


def pack_kernel(
    patches, cap, source_hbm, live_hbm, weight_hbm, payload, source, live, weight, arrivals
):
    column = lax.axis_index("mp")
    slots, half, width = weight.shape
    devices = payload.shape[0]
    first_row = pl.multiple_of((column % 2) * half, half)
    copies = fetch(
        [
            (source_hbm, source),
            (live_hbm, live),
            (weight_hbm.at[:, pl.ds(first_row, half)], weight),
        ],
        arrivals,
    )
    blank = jnp.zeros(payload.shape[1:], BF16)
    tail = cap * half
    row = lax.broadcasted_iota(jnp.int32, (INDEX_ROWS, width), 0)

    def clear(device):
        payload[device] = blank

    each_device(devices, clear)
    for copy in copies:
        copy.wait()
    for slot in range(slots):
        device = source[slot] // patches
        place = source[slot] % patches
        rank = jnp.int32(0)
        for other in range(slot):
            same = (source[other] // patches == device) & (live[other] == 1)
            rank = rank + same.astype(jnp.int32)

        @pl.when(live[slot] == 1)
        def _():
            payload[device, pl.ds(pl.multiple_of(rank * half, half), half)] = weight[slot]
            old = payload[device, tail:].astype(F32)
            payload[device, tail:] = jnp.where(row == rank, place.astype(F32), old).astype(BF16)


def local_kernel(latent, first, second, hidden, message, slope, scratch):
    column = lax.axis_index("mp")
    rows = latent.shape[0]
    own = slope.shape[0]
    tile = min(256, rows)
    for start in range(0, rows, tile):
        here = pl.ds(start, tile)
        pre = dot(latent[here], first[...])
        scratch[...] = pre
        value = (pre * jax.nn.sigmoid(pre)).astype(BF16)
        hidden[here] = value
        message[here] = dot(value, second[...]).astype(BF16)
        mine = scratch[:, pl.ds(pl.multiple_of(column * own, own), own)]
        gate = jax.nn.sigmoid(mine)
        slope[:, here] = (gate * (1.0 + mine * (1.0 - gate))).T


def carried_device(step, held_near, offsets):
    device = lax.axis_index("patch")
    if not held_near:
        device = device ^ offsets[-1]
    for place, offset in enumerate(offsets[:-1]):
        device = device ^ (((step >> place) & 1) * offset)
    return device


def adjoint_kernel(
    cap,
    gather_order,
    sum_order,
    scaling,
    places,
    received,
    other,
    near,
    far,
    message,
    hidden,
    sent,
    kept,
    weights,
    total,
):
    column = lax.axis_index("mp")
    own = lax.axis_index("patch")
    devices, _, rows = received.shape
    half = other.shape[1] // cap
    width = message.shape[1]
    patches = message.shape[0] // rows
    mine = pl.ds(pl.multiple_of((column % 2) * half, half), half)
    theirs = pl.ds(pl.multiple_of((1 - column % 2) * half, half), half)
    total[...] = jnp.zeros_like(total)

    def one(step, held, is_near):
        device = carried_device(step, is_near, gather_order)
        turned = held[step, :width]
        summed = None
        for rank in range(cap):
            slot = device * cap + rank
            place = places[slot]
            weights[slot, mine] = received[device, rank * half : (rank + 1) * half]
            weights[slot, theirs] = other[device, rank * half : (rank + 1) * half]
            block = weights[slot]
            start = pl.multiple_of(place * rows, rows)
            product = dot(block, message[pl.ds(start, rows)])
            summed = product if summed is None else summed + product
            total[place] += dot(turned, block).astype(BF16).astype(F32)
        apart = device ^ own
        away = (apart // sum_order[0]) & 1
        block = jnp.int32(0)
        for offset in sum_order[1:]:
            block = 2 * block + ((apart // offset) & 1)

        @pl.when(away == 1)
        def _():
            start = pl.multiple_of(hidden.shape[1] + block * rows, rows)
            sent[pl.ds(start, rows)] = summed.astype(BF16)

        @pl.when(away == 0)
        def _():
            kept[pl.ds(pl.multiple_of(block * rows, rows), rows)] = summed

    each_device(devices // 2, lambda step: one(step, near, True))
    each_device(devices // 2, lambda step: one(step, far, False))
    turned_message = jnp.concatenate(
        [total[place].astype(BF16) for place in range(patches)], axis=1
    )
    second = dot(turned_message, hidden[...]) * scaling
    sent[: hidden.shape[1]] = second.T.astype(BF16)


def first_kernel(
    cap, gather_order, scaling, places, weights, near, far, slope, latent, first, total
):
    devices = 2 * near.shape[0]
    rows = weights.shape[1]
    width = near.shape[1] - slope.shape[0]
    patches = latent.shape[0] // rows
    total[...] = jnp.zeros_like(total)

    def one(step, held, is_near):
        device = carried_device(step, is_near, gather_order)
        turned = held[step, width:]
        for rank in range(cap):
            slot = device * cap + rank
            total[places[slot]] += dot(turned, weights[slot])

    each_device(devices // 2, lambda step: one(step, near, True))
    each_device(devices // 2, lambda step: one(step, far, False))
    grad_pre = jnp.concatenate(
        [
            (total[place] * slope[:, place * rows : (place + 1) * rows]).astype(BF16)
            for place in range(patches)
        ],
        axis=1,
    )
    first[...] = (dot(grad_pre, latent[...]) * scaling).T.astype(BF16)


def per_device(
    grid_latent,
    mesh_latent,
    edge_weight,
    block_source,
    block_live,
    mlp_first,
    mlp_second,
    mesh_cotangent,
):
    devices = lax.axis_size("patch")
    parts = lax.axis_size("mp")
    slots, rows, _ = edge_weight.shape
    grid_rows, depth = grid_latent.shape
    patches = grid_rows // rows
    hidden_width, width = mlp_second.shape
    hidden_local = hidden_width // parts
    cap = -(-slots // devices)
    half = rows // 2
    column = lax.axis_index("mp")
    scaling = 1.0 / math.sqrt(grid_rows * devices)
    payload_rows = cap * half + INDEX_ROWS

    slot_bytes = ((slots,), jnp.int32)
    kept, sent, turned = call(
        term_kernel,
        "term",
        [(HBM, mesh_cotangent), (HBM, mlp_second)],
        [
            ((hidden_width // 2, rows), F32),
            ((hidden_width // 2, rows), BF16),
            ((width, rows), BF16),
        ],
        scratch=[
            VMEM(mesh_cotangent.shape, BF16),
            VMEM(mlp_second.shape, BF16),
            pltpu.SemaphoreType.DMA((2,)),
        ],
    )
    (payload,) = call(
        functools.partial(pack_kernel, patches, cap),
        "pack",
        [(HBM, block_source), (HBM, block_live), (HBM, edge_weight)],
        [((devices, payload_rows, rows), BF16)],
        scratch=[
            SMEM(*slot_bytes),
            SMEM(*slot_bytes),
            VMEM((slots, half, rows), BF16),
            pltpu.SemaphoreType.DMA((3,)),
        ],
    )

    carried = after(kept, payload) + swap(sent, "mp", parts // 2).astype(F32)
    offset = parts // 4
    while offset:
        size = carried.shape[0] // 2
        upper = (column // offset) % 2
        away = lax.dynamic_slice_in_dim(carried, (1 - upper) * size, size, 0)
        stay = lax.dynamic_slice_in_dim(carried, upper * size, size, 0)
        carried = stay + swap(away, "mp", offset)
        offset //= 2
    carried = jnp.concatenate([turned, carried.astype(BF16)])[None]
    hidden, message, slope = call(
        local_kernel,
        "local",
        [(VMEM, grid_latent), (VMEM, mlp_first), (VMEM, mlp_second)],
        [
            ((grid_rows, hidden_width), BF16),
            ((grid_rows, width), BF16),
            ((hidden_local, grid_rows), F32),
        ],
        scratch=[VMEM((min(256, grid_rows), hidden_width), F32)],
    )

    steps = devices.bit_length() - 1
    up = [1 << place for place in range(steps)]
    down = up[::-1]
    gather_order, second_order, first_order = down[:1] + up[:-1], up, up[1:] + up[:1]
    near = carried
    for offset in gather_order:
        if offset != gather_order[0]:
            near = jnp.concatenate([near, far])
        far = swap(near, "patch", offset)
        if offset == gather_order[min(1, steps - 1)]:
            far = after(far, hidden)
        if offset == gather_order[0]:
            payload = after(payload, far)
            received = lax.all_to_all(payload, "patch", split_axis=0, concat_axis=0, tiled=True)
    other = swap(received[:, : cap * half], "mp", 1)
    index_row = cap * half
    places = received[:, index_row : index_row + cap, 0].astype(jnp.int32).reshape(-1)

    sent, kept, weights = call(
        functools.partial(adjoint_kernel, cap, gather_order, second_order, scaling),
        "adjoint",
        [
            (SMEM, places),
            (VMEM, received),
            (VMEM, other),
            (VMEM, near),
            (VMEM, far),
            (VMEM, message),
            (VMEM, hidden),
        ],
        [
            ((hidden_width + devices // 2 * rows, width), BF16),
            ((devices // 2 * rows, width), F32),
            ((devices * cap, rows, rows), BF16),
        ],
        scratch=[VMEM((patches, width, rows), F32)],
    )
    (grad_first,) = call(
        functools.partial(first_kernel, cap, gather_order, scaling),
        "first",
        [
            (SMEM, places),
            (VMEM, weights),
            (VMEM, near),
            (VMEM, far),
            (VMEM, slope),
            (VMEM, grid_latent),
        ],
        [((depth, hidden_local), BF16)],
        scratch=[VMEM((patches, hidden_local, rows), F32)],
    )

    first = grad_first
    for step in range(steps):
        if step:
            size = kept.shape[0] // 2
            sent = jnp.concatenate([second, kept[size:]]).astype(BF16)
            kept = kept[:size]
            first = first.astype(BF16)
        got = swap(sent, "patch", second_order[step]).astype(F32)
        second = sent[:hidden_width].astype(F32) + got[:hidden_width]
        kept = kept + got[hidden_width:]
        if step == steps - 1:
            mesh_out = (mesh_latent.astype(F32) + kept).astype(BF16)
        first = first.astype(F32) + swap(first, "patch", first_order[step]).astype(F32)
    return (mesh_out, first, second)


def solution(mesh):
    placed = (
        P("patch", None),
        P("patch", "mp"),
        P("patch", None, None),
        P("patch"),
        P("patch"),
        P(),
        P(None, "mp"),
        P("patch", "mp"),
    )
    return jax.shard_map(
        per_device,
        mesh=mesh,
        in_specs=placed,
        out_specs=(P("patch", "mp"), P(None, "mp"), P(None, "mp")),
        check_vma=False,
    )
```

time: 77.4 us -> 63.8 us (0.82)
  waiting for transfers between devices: 35.2 us -> 22.4 us
  local copies, waits for them, and re-layouts: 9.1 us -> 0.89 us
  starting transfers between devices: 22.2 us -> 29.1 us
  Pallas kernels: 6.69 us -> 7.5 us
    all_to_all x1 -> x0, waiting for transfers between devices: 12 us -> none  [per_device(): lax.all_to_all(forward, 'patch', split_axis=0, concat_axis=0, tiled=True)]
    ppermute x9 -> x12, starting transfers between devices: 13 us -> 23.3 us  [swap(): return lax.ppermute(value, axis, [(i, i ^ offset) for i in range(size)])]
    unnamed x26 -> x16, local copies, waits for them, and re-layouts: 7.46 us -> 0.06 us
    all_to_all x1 -> x0, starting transfers between devices: 3.41 us -> none  [per_device(): lax.all_to_all(forward, 'patch', split_axis=0, concat_axis=0, tiled=True)]
    concatenate x3 -> x4, other arithmetic: 1.62 us -> 0.07 us  [the longest x2 0.04 us: per_device(): near = jnp.concatenate([near, far])]
    add x2 -> x4, other arithmetic: 0.07 us -> 1.49 us  [the longest x1 0.73 us: per_device(): first.astype(F32) + swap(first, 'patch', first_order[step]).astype(F32)]
    ppermute x9 -> x12, waiting for transfers between devices: 23.2 us -> 22.2 us  [swap(): return lax.ppermute(value, axis, [(i, i ^ offset) for i in range(size)])]
    squeeze x1 -> x0, local copies, waits for them, and re-layouts: 0.82 us -> none  [per_device(): return (mesh_out, both[0], both[1])]
  transfers between devices with their start and end apart: 11 -> 13, of which waited for: 7 -> 9; matrix products, arithmetic and copies ran while one was open for 4% -> 3% of each run, Pallas kernels for 2% -> 6%
where the time goes in v2:
time: 63.8 us; the launch traced here: 63.5 us
  starting transfers between devices  29.1 us (46%)
  waiting for transfers between devices  22.4 us (35%)
  Pallas kernels  7.5 us (12%)
  other arithmetic  2.69 us (4%)
  local copies, waits for them, and re-layouts  0.89 us (1%)
  between operations  0.88 us (1%)
    ppermute x12, starting transfers between devices, swap(): return lax.ppermute(value, axis, [(i, i ^ offset) for i in range(size)])  23.3 us
    ppermute x12, waiting for transfers between devices, swap(): return lax.ppermute(value, axis, [(i, i ^ offset) for i in range(size)])  22.2 us
    pallas_call x5, Pallas kernels, call(): pl.pallas_call(kernel, out_shape=[VMEM(shape, dtype) for shape, dtype in...  7.5 us
    all_to_all x1, starting transfers between devices, per_device(): lax.all_to_all(payload, 'patch', split_axis=0, concat_axis=0, tiled=True)  5.77 us
  transfers between devices with their start and end apart: 13, of which 9 were waited for; matrix products, arithmetic and copies ran while one was open for 3% of the time, Pallas kernels for 6%

profile of v2, /device:TPU:0, one launch (start us, length us, event | category | flops | bytes accessed | tf_op | source)
XLA Modules:
  0.0 63.5 jit_solution(2571625346892097281)
XLA Ops:
  0.6 1.1 %term.1 = (f32[256,128]{1,0:T(8,128)S(1)}, bf16[256,128]{1,0:T(8,128)(2,1)S(1)}, bf16[128,128]{1,0:T(8,128)(2,1)S(1)}) custom-call(bf16[128,128]{1,0:T(8,128)(2,1)} %cotangent_hbm.1, bf16[512,128]{1,0:T(8,128)(2,1)} %second.1), custom_call_target="tpu_custom_call" | custom-call | tf_op jit(solution)/shard_map/term/pallas_call | solution.py:26
  1.8 3.0 %collective-permute-start = (bf16[256,128]{1,0:T(8,128)(2,1)S(1)}, bf16[256,128]{1,0:T(8,128)(2,1)S(1)}, u32[]{:S(2)}, u32[]{:S(2)}) collective-permute-start(bf16[256,128]{1,0:T(8,128)(2,1)S(1)} %get-tuple-element.18), channel_id=1, source_target_pairs={{0,2},{1,3},{2,0},{3,1},{4,6},{5,7},{6,4},{7,5},{8,10},{9,11},{10,... | collective-permute-start | bytes 196616 | tf_op jit(solution)/shard_map/ppermute | solution.py:59
  4.8 0.0 copy-start
  4.8 2.2 %pack.1 = bf16[8,144,128]{2,1,0:T(8,128)(2,1)} custom-call(s32[12]{0:T(128)} %source_hbm.1, s32[12]{0:T(128)} %live_hbm.1, bf16[12,128,128]{2,1,0:T(8,128)(2,1)} %weight_hbm.1), custom_call_target="tpu_custom_call" | custom-call | tf_op jit(solution)/shard_map/pack/pallas_call | solution.py:26
  7.0 0.0 collective-permute-done
  7.1 0.1 collective-permute-start.1
  7.2 1.2 %collective-permute-done.1 = f32[128,128]{1,0:T(8,128)S(1)} collective-permute-done((f32[128,128]{1,0:T(8,128)S(1)}, f32[128,128]{1,0:T(8,128)S(1)}, u32[]{:S(2)}, u32[]{:S(2)}) %collective-permute-start.1) | collective-permute-done | bytes 65568 | tf_op jit(solution)/shard_map/ppermute | solution.py:59
  8.4 0.0 copy-start.1
  8.5 3.1 %collective-permute-start.2 = (bf16[1,256,128]{2,1,0:T(8,128)(2,1)S(1)}, bf16[1,256,128]{2,1,0:T(8,128)(2,1)S(1)}, u32[]{:S(2)}, u32[]{:S(2)}) collective-permute-start(bf16[1,256,128]{2,1,0:T(8,128)(2,1)S(1)} %maximum_bitcast_fusion), channel_id=1, source_target_pairs={{0,16},{4,20},{8,24},{12,28},{16,0},{20,4},{24,8},{28,12},{1,17},{... | collective-permute-start | bytes 196616 | tf_op jit(solution)/shard_map/ppermute | solution.py:59
  11.6 3.8 %collective-permute-done.2 = bf16[1,256,128]{2,1,0:T(8,128)(2,1)S(1)} collective-permute-done((bf16[1,256,128]{2,1,0:T(8,128)(2,1)S(1)}, bf16[1,256,128]{2,1,0:T(8,128)(2,1)S(1)}, u32[]{:S(2)}, u32[]{:S(2)}) %collective-permute-start.2) | collective-permute-done | bytes 65568 | tf_op jit(solution)/shard_map/ppermute | solution.py:59
  15.4 0.0 copy-start.5
  15.4 5.8 %all-to-all-start = ((bf16[8,144,128]{2,1,0:T(8,128)(2,1)}), bf16[8,144,128]{2,1,0:T(8,128)(2,1)S(1)}, u32[]{:S(2)}, u32[]{:S(2)}) async-start(bf16[8,144,128]{2,1,0:T(8,128)(2,1)} %pack.1), calls=%async_computation | async-start | bytes 589824 | tf_op jit(solution)/shard_map/all_to_all | solution.py:337
  21.2 0.0 copy-done.5
  21.2 0.0 copy-start.4
  21.2 0.0 copy-start.6
  21.3 2.1 %collective-permute-start.4 = (bf16[2,256,128]{2,1,0:T(8,128)(2,1)S(1)}, bf16[2,256,128]{2,1,0:T(8,128)(2,1)S(1)}, u32[]{:S(2)}, u32[]{:S(2)}) collective-permute-start(bf16[2,256,128]{2,1,0:T(8,128)(2,1)S(1)} %pad_maximum_fusion.3), channel_id=1, source_target_pairs={{0,4},{4,0},{8,12},{12,8},{16,20},{20,16},{24,28},{28,24},{1,5},{5... | collective-permute-start | bytes 393224 | tf_op jit(solution)/shard_map/ppermute | solution.py:59
  23.3 0.0 copy-done
  23.3 0.0 copy-done.1
  23.3 0.0 copy-done.4
  23.3 1.5 %local.1 = (bf16[1024,512]{1,0:T(8,128)(2,1)S(1)}, bf16[1024,128]{1,0:T(8,128)(2,1)S(1)}, f32[128,1024]{1,0:T(8,128)S(1)}) custom-call(bf16[1024,512]{1,0:T(8,128)(2,1)S(1)} %copy-done, bf16[512,512]{1,0:T(8,128)(2,1)S(1)} %copy-done.1, bf16[512,128]{1,0:T(8,128)(2,1)S(1)} %copy-done.4), custom_call_target="tpu_custom_call" | custom-call | tf_op jit(solution)/shard_map/local/pallas_call | solution.py:26
  24.9 0.0 copy-start.2
  24.9 4.4 %collective-permute-done.4 = bf16[2,256,128]{2,1,0:T(8,128)(2,1)S(1)} collective-permute-done((bf16[2,256,128]{2,1,0:T(8,128)(2,1)S(1)}, bf16[2,256,128]{2,1,0:T(8,128)(2,1)S(1)}, u32[]{:S(2)}, u32[]{:S(2)}) %collective-permute-start.4) | collective-permute-done | bytes 131104 | tf_op jit(solution)/shard_map/ppermute | solution.py:59
  29.3 0.0 copy-done.6
  29.3 0.0 copy-done.2
  29.3 1.5 %collective-permute-start.5 = (bf16[4,256,128]{2,1,0:T(8,128)(2,1)S(1)}, bf16[4,256,128]{2,1,0:T(8,128)(2,1)S(1)}, u32[]{:S(2)}, u32[]{:S(2)}) collective-permute-start(bf16[4,256,128]{2,1,0:T(8,128)(2,1)S(1)} %pad_maximum_fusion.near), channel_id=1, source_target_pairs={{0,8},{4,12},{8,0},{12,4},{16,24},{20,28},{24,16},{28,20},{1,9},{5... | collective-permute-start | bytes 786440 | tf_op jit(solution)/shard_map/ppermute | solution.py:59
  30.9 0.2 all-to-all-done.received
  31.0 0.7 %slice.63 = bf16[8,128,128]{2,1,0:T(8,128)(2,1)} slice(bf16[8,144,128]{2,1,0:T(8,128)(2,1)S(1)} %all-to-all-done.received), slice={[0:8], [0:128], [0:128]} | slice | bytes 524288 | tf_op jit(solution)/shard_map/slice | solution.py:338
  31.8 0.0 collective-permute-start.3
  31.8 0.2 convert_reduce_fusion
  32.0 0.1 reshape.10.places
  32.1 4.4 %collective-permute-done.5.far = bf16[4,256,128]{2,1,0:T(8,128)(2,1)S(1)} collective-permute-done((bf16[4,256,128]{2,1,0:T(8,128)(2,1)S(1)}, bf16[4,256,128]{2,1,0:T(8,128)(2,1)S(1)}, u32[]{:S(2)}, u32[]{:S(2)}) %collective-permute-start.5) | collective-permute-done | bytes 262176 | tf_op jit(solution)/shard_map/ppermute | solution.py:59
  36.5 0.0 collective-permute-done.3.other
  36.5 0.0 copy-start.3
  36.5 1.4 %adjoint.1 = (bf16[1024,128]{1,0:T(8,128)(2,1)S(1)}, f32[512,128]{1,0:T(8,128)S(1)}, bf16[16,128,128]{2,1,0:T(8,128)(2,1)S(1)}) custom-call(s32[16]{0:T(128)S(1)} %reshape.10.places, bf16[8,144,128]{2,1,0:T(8,128)(2,1)S(1)} %all-to-all-done.received, bf16[8,128,128]{2,1,0:T(8,128)(2,1)S(1)} %collective-permute-done.3.other, ...), custom_call_target="tpu_custom_call" | custom-call | tf_op jit(solution)/shard_map/adjoint/pallas_call | solution.py:26
  37.8 0.0 copy-done.3
  37.9 1.2 %first.3 = bf16[512,128]{1,0:T(8,128)(2,1)S(1)} custom-call(s32[16]{0:T(128)S(1)} %reshape.10.places, bf16[16,128,128]{2,1,0:T(8,128)(2,1)S(1)} %get-tuple-element.25.weights, bf16[4,256,128]{2,1,0:T(8,128)(2,1)S(1)} %pad_maximum_fusion.near, bf16[4,256,128]{2,1,0:T(8,128)(2,1)S(1)} %collective-permute-done.5.far, f32[128,1024]{1,0:T(8,128)S(1)} %copy-done.3, ...), custom_call_target="tpu_custom_call" | custom-call | tf_op jit(solution)/shard_map/first/pallas_call | solution.py:26
  39.1 1.1 %collective-permute-start.9 = (bf16[512,128]{1,0:T(8,128)(2,1)S(1)}, bf16[512,128]{1,0:T(8,128)(2,1)S(1)}, u32[]{:S(2)}, u32[]{:S(2)}) collective-permute-start(bf16[512,128]{1,0:T(8,128)(2,1)S(1)} %first.3), channel_id=1, source_target_pairs={{0,8},{4,12},{8,0},{12,4},{16,24},{20,28},{24,16},{28,20},{1,9},{5... | collective-permute-start | bytes 393224 | tf_op jit(solution)/shard_map/ppermute | solution.py:59
  40.2 1.8 %collective-permute-start.6 = (bf16[1024,128]{1,0:T(8,128)(2,1)S(1)}, bf16[1024,128]{1,0:T(8,128)(2,1)S(1)}, u32[]{:S(2)}, u32[]{:S(2)}) collective-permute-start(bf16[1024,128]{1,0:T(8,128)(2,1)S(1)} %get-tuple-element.24), channel_id=1, source_target_pairs={{0,4},{4,0},{8,12},{12,8},{16,20},{20,16},{24,28},{28,24},{1,5},{5... | collective-permute-start | bytes 786440 | tf_op jit(solution)/shard_map/ppermute | solution.py:59
  42.0 2.1 %collective-permute-done.9 = bf16[512,128]{1,0:T(8,128)(2,1)S(1)} collective-permute-done((bf16[512,128]{1,0:T(8,128)(2,1)S(1)}, bf16[512,128]{1,0:T(8,128)(2,1)S(1)}, u32[]{:S(2)}, u32[]{:S(2)}) %collective-permute-start.9) | collective-permute-done | bytes 131104 | tf_op jit(solution)/shard_map/ppermute | solution.py:59
  44.2 3.0 %collective-permute-start.10 = (bf16[512,128]{1,0:T(8,128)(2,1)S(1)}, bf16[512,128]{1,0:T(8,128)(2,1)S(1)}, u32[]{:S(2)}, u32[]{:S(2)}) collective-permute-start(bf16[512,128]{1,0:T(8,128)(2,1)S(1)} %add_convert_fusion.1), channel_id=1, source_target_pairs={{0,16},{4,20},{8,24},{12,28},{16,0},{20,4},{24,8},{28,12},{1,17},{... | collective-permute-start | bytes 393224 | tf_op jit(solution)/shard_map/ppermute | solution.py:59
  47.1 0.0 collective-permute-done.6
  47.2 0.1 fusion.1
  47.3 1.8 %collective-permute-start.7 = (bf16[768,128]{1,0:T(8,128)(2,1)S(1)}, bf16[768,128]{1,0:T(8,128)(2,1)S(1)}, u32[]{:S(2)}, u32[]{:S(2)}) collective-permute-start(bf16[768,128]{1,0:T(8,128)(2,1)S(1)} %pad_maximum_fusion.1), channel_id=1, source_target_pairs={{0,8},{4,12},{8,0},{12,4},{16,24},{20,28},{24,16},{28,20},{1,9},{5... | collective-permute-start | bytes 589832 | tf_op jit(solution)/shard_map/ppermute | solution.py:59
  49.1 1.5 %collective-permute-done.10 = bf16[512,128]{1,0:T(8,128)(2,1)S(1)} collective-permute-done((bf16[512,128]{1,0:T(8,128)(2,1)S(1)}, bf16[512,128]{1,0:T(8,128)(2,1)S(1)}, u32[]{:S(2)}, u32[]{:S(2)}) %collective-permute-start.10) | collective-permute-done | bytes 131104 | tf_op jit(solution)/shard_map/ppermute | solution.py:59
  50.6 2.0 %collective-permute-start.11 = (bf16[512,128]{1,0:T(8,128)(2,1)S(1)}, bf16[512,128]{1,0:T(8,128)(2,1)S(1)}, u32[]{:S(2)}, u32[]{:S(2)}) collective-permute-start(bf16[512,128]{1,0:T(8,128)(2,1)S(1)} %add_convert_fusion), channel_id=1, source_target_pairs={{0,4},{4,0},{8,12},{12,8},{16,20},{20,16},{24,28},{28,24},{1,5},{5... | collective-permute-start | bytes 393224 | tf_op jit(solution)/shard_map/ppermute | solution.py:59
  52.6 0.5 collective-permute-done.7
  53.2 3.8 %collective-permute-start.8 = (bf16[640,128]{1,0:T(8,128)(2,1)S(1)}, bf16[640,128]{1,0:T(8,128)(2,1)S(1)}, u32[]{:S(2)}, u32[]{:S(2)}) collective-permute-start(bf16[640,128]{1,0:T(8,128)(2,1)S(1)} %pad_maximum_fusion.2), channel_id=1, source_target_pairs={{0,16},{4,20},{8,24},{12,28},{16,0},{20,4},{24,8},{28,12},{1,17},{... | collective-permute-start | bytes 491528 | tf_op jit(solution)/shard_map/ppermute | solution.py:59
  57.0 0.0 collective-permute-done.11
  57.0 0.7 %convert_add_fusion = f32[512,128]{1,0:T(8,128)} fusion(bf16[512,128]{1,0:T(8,128)(2,1)S(1)} %collective-permute-done.11, bf16[512,128]{1,0:T(8,128)(2,1)S(1)} %add_convert_fusion), kind=kLoop, calls=%fused_computation.7 | loop fusion | flops 196608 | bytes 524288 | tf_op jit(solution)/shard_map/add | solution.py:388
  57.7 4.3 %collective-permute-done.8 = bf16[640,128]{1,0:T(8,128)(2,1)S(1)} collective-permute-done((bf16[640,128]{1,0:T(8,128)(2,1)S(1)}, bf16[640,128]{1,0:T(8,128)(2,1)S(1)}, u32[]{:S(2)}, u32[]{:S(2)}) %collective-permute-start.8) | collective-permute-done | bytes 163872 | tf_op jit(solution)/shard_map/ppermute | solution.py:59
  62.1 0.0 copy-start.7
  62.1 0.7 %slice_add_fusion = f32[512,128]{1,0:T(8,128)} fusion(f32[640,128]{1,0:T(8,128)S(1)} %convert_element_type.72, bf16[512,128]{1,0:T(8,128)(2,1)S(1)} %fusion), kind=kLoop, calls=%fused_computation | loop fusion | flops 131072 | bytes 655360 | tf_op jit(solution)/shard_map/add | solution.py:384
  62.8 0.0 copy-done.7
  62.8 0.6 fusion.3
  (17 shorter events, 0.3 us)
Async XLA Ops:
  1.8 5.3 %collective-permute-start = (bf16[256,128]{1,0:T(8,128)(2,1)S(1)}, bf16[256,128]{1,0:T(8,128)(2,1)S(1)}, u32[]{:S(2)}, u32[]{:S(2)}) collective-permute-start(bf16[256,128]{1,0:T(8,128)(2,1)S(1)} %get-tuple-element.18), channel_id=1, source_target_pairs={{0,2},{1,3},{2,0},{3,1},{4,6},{5,7},{6,4},{7,5},{8,10},{9,11},{10,... | collective-permute-start | bytes 196616 | tf_op jit(solution)/shard_map/ppermute | solution.py:59
  4.8 18.5 %copy-start = (bf16[1024,512]{1,0:T(8,128)(2,1)S(1)}, bf16[1024,512]{1,0:T(8,128)(2,1)}, u32[]{:S(2)}) copy-start(bf16[1024,512]{1,0:T(8,128)(2,1)} %latent.3) | copy-start | bytes 3145732
  7.1 1.3 %collective-permute-start.1 = (f32[128,128]{1,0:T(8,128)S(1)}, f32[128,128]{1,0:T(8,128)S(1)}, u32[]{:S(2)}, u32[]{:S(2)}) collective-permute-start(f32[128,128]{1,0:T(8,128)S(1)} %constant_dynamic-slice_fusion), channel_id=1, source_target_pairs={{0,1},{1,0},{2,3},{3,2},{4,5},{5,4},{6,7},{7,6},{8,9},{9,8},{10,11... | collective-permute-start | bytes 196616 | tf_op jit(solution)/shard_map/ppermute | solution.py:59
  8.4 14.9 %copy-start.1 = (bf16[512,512]{1,0:T(8,128)(2,1)S(1)}, bf16[512,512]{1,0:T(8,128)(2,1)}, u32[]{:S(2)}) copy-start(bf16[512,512]{1,0:T(8,128)(2,1)} %first.2) | copy-start | bytes 1572868
  8.5 7.0 %collective-permute-start.2 = (bf16[1,256,128]{2,1,0:T(8,128)(2,1)S(1)}, bf16[1,256,128]{2,1,0:T(8,128)(2,1)S(1)}, u32[]{:S(2)}, u32[]{:S(2)}) collective-permute-start(bf16[1,256,128]{2,1,0:T(8,128)(2,1)S(1)} %maximum_bitcast_fusion), channel_id=1, source_target_pairs={{0,16},{4,20},{8,24},{12,28},{16,0},{20,4},{24,8},{28,12},{1,17},{... | collective-permute-start | bytes 196616 | tf_op jit(solution)/shard_map/ppermute | solution.py:59
  15.4 5.8 %copy-start.5 = (bf16[1,256,128]{2,1,0:T(8,128)(2,1)}, bf16[1,256,128]{2,1,0:T(8,128)(2,1)S(1)}, u32[]{:S(2)}) copy-start(bf16[1,256,128]{2,1,0:T(8,128)(2,1)S(1)} %collective-permute-done.2) | copy-start | bytes 196612
  15.4 15.6 %all-to-all-start = ((bf16[8,144,128]{2,1,0:T(8,128)(2,1)}), bf16[8,144,128]{2,1,0:T(8,128)(2,1)S(1)}, u32[]{:S(2)}, u32[]{:S(2)}) async-start(bf16[8,144,128]{2,1,0:T(8,128)(2,1)} %pack.1), calls=%async_computation | async-start | bytes 589824 | tf_op jit(solution)/shard_map/all_to_all | solution.py:337
  21.2 2.1 %copy-start.4 = (bf16[512,128]{1,0:T(8,128)(2,1)S(1)}, bf16[512,128]{1,0:T(8,128)(2,1)}, u32[]{:S(2)}) copy-start(bf16[512,128]{1,0:T(8,128)(2,1)} %second.1) | copy-start | bytes 393220
  21.2 8.1 %copy-start.6 = (bf16[1,256,128]{2,1,0:T(8,128)(2,1)S(1)}, bf16[1,256,128]{2,1,0:T(8,128)(2,1)}, u32[]{:S(2)}) copy-start(bf16[1,256,128]{2,1,0:T(8,128)(2,1)} %copy-done.5) | copy-start | bytes 196612
  21.3 8.0 %collective-permute-start.4 = (bf16[2,256,128]{2,1,0:T(8,128)(2,1)S(1)}, bf16[2,256,128]{2,1,0:T(8,128)(2,1)S(1)}, u32[]{:S(2)}, u32[]{:S(2)}) collective-permute-start(bf16[2,256,128]{2,1,0:T(8,128)(2,1)S(1)} %pad_maximum_fusion.3), channel_id=1, source_target_pairs={{0,4},{4,0},{8,12},{12,8},{16,20},{20,16},{24,28},{28,24},{1,5},{5... | collective-permute-start | bytes 393224 | tf_op jit(solution)/shard_map/ppermute | solution.py:59
  24.9 4.5 %copy-start.2 = (f32[128,1024]{1,0:T(8,128)}, f32[128,1024]{1,0:T(8,128)S(1)}, u32[]{:S(2)}) copy-start(f32[128,1024]{1,0:T(8,128)S(1)} %get-tuple-element.26.slope) | copy-start | bytes 1572868
  29.3 7.1 %collective-permute-start.5 = (bf16[4,256,128]{2,1,0:T(8,128)(2,1)S(1)}, bf16[4,256,128]{2,1,0:T(8,128)(2,1)S(1)}, u32[]{:S(2)}, u32[]{:S(2)}) collective-permute-start(bf16[4,256,128]{2,1,0:T(8,128)(2,1)S(1)} %pad_maximum_fusion.near), channel_id=1, source_target_pairs={{0,8},{4,12},{8,0},{12,4},{16,24},{20,28},{24,16},{28,20},{1,9},{5... | collective-permute-start | bytes 786440 | tf_op jit(solution)/shard_map/ppermute | solution.py:59
  31.8 4.7 %collective-permute-start.3 = (bf16[8,128,128]{2,1,0:T(8,128)(2,1)}, bf16[8,128,128]{2,1,0:T(8,128)(2,1)S(1)}, u32[]{:S(2)}, u32[]{:S(2)}) collective-permute-start(bf16[8,128,128]{2,1,0:T(8,128)(2,1)} %slice.63), channel_id=1, source_target_pairs={{0,1},{1,0},{2,3},{3,2},{4,5},{5,4},{6,7},{7,6},{8,9},{9,8},{10,11... | collective-permute-start | bytes 786440 | tf_op jit(solution)/shard_map/ppermute | solution.py:59
  36.5 1.4 %copy-start.3 = (f32[128,1024]{1,0:T(8,128)S(1)}, f32[128,1024]{1,0:T(8,128)}, u32[]{:S(2)}) copy-start(f32[128,1024]{1,0:T(8,128)} %copy-done.2) | copy-start | bytes 1572868
  39.1 5.0 %collective-permute-start.9 = (bf16[512,128]{1,0:T(8,128)(2,1)S(1)}, bf16[512,128]{1,0:T(8,128)(2,1)S(1)}, u32[]{:S(2)}, u32[]{:S(2)}) collective-permute-start(bf16[512,128]{1,0:T(8,128)(2,1)S(1)} %first.3), channel_id=1, source_target_pairs={{0,8},{4,12},{8,0},{12,4},{16,24},{20,28},{24,16},{28,20},{1,9},{5... | collective-permute-start | bytes 393224 | tf_op jit(solution)/shard_map/ppermute | solution.py:59
  40.2 7.0 %collective-permute-start.6 = (bf16[1024,128]{1,0:T(8,128)(2,1)S(1)}, bf16[1024,128]{1,0:T(8,128)(2,1)S(1)}, u32[]{:S(2)}, u32[]{:S(2)}) collective-permute-start(bf16[1024,128]{1,0:T(8,128)(2,1)S(1)} %get-tuple-element.24), channel_id=1, source_target_pairs={{0,4},{4,0},{8,12},{12,8},{16,20},{20,16},{24,28},{28,24},{1,5},{5... | collective-permute-start | bytes 786440 | tf_op jit(solution)/shard_map/ppermute | solution.py:59
  44.2 6.4 %collective-permute-start.10 = (bf16[512,128]{1,0:T(8,128)(2,1)S(1)}, bf16[512,128]{1,0:T(8,128)(2,1)S(1)}, u32[]{:S(2)}, u32[]{:S(2)}) collective-permute-start(bf16[512,128]{1,0:T(8,128)(2,1)S(1)} %add_convert_fusion.1), channel_id=1, source_target_pairs={{0,16},{4,20},{8,24},{12,28},{16,0},{20,4},{24,8},{28,12},{1,17},{... | collective-permute-start | bytes 393224 | tf_op jit(solution)/shard_map/ppermute | solution.py:59
  47.3 5.7 %collective-permute-start.7 = (bf16[768,128]{1,0:T(8,128)(2,1)S(1)}, bf16[768,128]{1,0:T(8,128)(2,1)S(1)}, u32[]{:S(2)}, u32[]{:S(2)}) collective-permute-start(bf16[768,128]{1,0:T(8,128)(2,1)S(1)} %pad_maximum_fusion.1), channel_id=1, source_target_pairs={{0,8},{4,12},{8,0},{12,4},{16,24},{20,28},{24,16},{28,20},{1,9},{5... | collective-permute-start | bytes 589832 | tf_op jit(solution)/shard_map/ppermute | solution.py:59
  50.6 6.4 %collective-permute-start.11 = (bf16[512,128]{1,0:T(8,128)(2,1)S(1)}, bf16[512,128]{1,0:T(8,128)(2,1)S(1)}, u32[]{:S(2)}, u32[]{:S(2)}) collective-permute-start(bf16[512,128]{1,0:T(8,128)(2,1)S(1)} %add_convert_fusion), channel_id=1, source_target_pairs={{0,4},{4,0},{8,12},{12,8},{16,20},{20,16},{24,28},{28,24},{1,5},{5... | collective-permute-start | bytes 393224 | tf_op jit(solution)/shard_map/ppermute | solution.py:59
  53.2 8.9 %collective-permute-start.8 = (bf16[640,128]{1,0:T(8,128)(2,1)S(1)}, bf16[640,128]{1,0:T(8,128)(2,1)S(1)}, u32[]{:S(2)}, u32[]{:S(2)}) collective-permute-start(bf16[640,128]{1,0:T(8,128)(2,1)S(1)} %pad_maximum_fusion.2), channel_id=1, source_target_pairs={{0,16},{4,20},{8,24},{12,28},{16,0},{20,4},{24,8},{28,12},{1,17},{... | collective-permute-start | bytes 491528 | tf_op jit(solution)/shard_map/ppermute | solution.py:59
  62.1 0.8 %copy-start.7 = (bf16[128,128]{1,0:T(8,128)(2,1)S(1)}, bf16[128,128]{1,0:T(8,128)(2,1)}, u32[]{:S(2)}) copy-start(bf16[128,128]{1,0:T(8,128)(2,1)} %param.9) | copy-start | bytes 98308

commit v3 on v2

v3 whole, which is shorter than its diff:
```python
import functools
import math

import jax
import jax.numpy as jnp
from jax import lax
from jax.experimental import pallas as pl
from jax.experimental.pallas import tpu as pltpu
from jax.sharding import PartitionSpec as P

BF16 = jnp.bfloat16
F32 = jnp.float32
INDEX_ROWS = 16
UNROLL = 8
VMEM_BYTES = 16 * 1024 * 1024
VMEM = pltpu.VMEM
SMEM = pltpu.SMEM
HBM = pltpu.HBM


def dot(left, right):
    return jnp.dot(left, right, preferred_element_type=F32)


def call(kernel, name, placed, outputs, scratch=(), cost=None):
    return pl.pallas_call(
        kernel,
        out_shape=[space(shape, dtype) for space, shape, dtype in outputs],
        in_specs=[pl.BlockSpec(memory_space=space) for space, _ in placed],
        out_specs=[pl.BlockSpec(memory_space=space) for space, _, _ in outputs],
        scratch_shapes=list(scratch),
        compiler_params=pltpu.CompilerParams(vmem_limit_bytes=VMEM_BYTES),
        cost_estimate=cost,
        name=name,
    )(
        *[
            operand if space is SMEM else pltpu.with_memory_space_constraint(operand, space)
            for space, operand in placed
        ]
    )


def fetch(pairs, arrivals):
    copies = [
        pltpu.make_async_copy(source, target, arrivals.at[place])
        for place, (source, target) in enumerate(pairs)
    ]
    for copy in copies:
        copy.start()
    return copies


def after(value, *others):
    return lax.optimization_barrier((value, *others))[0]


def swap(value, axis, offset):
    size = lax.axis_size(axis)
    return lax.ppermute(value, axis, [(i, i ^ offset) for i in range(size)])


def spread(value, group):
    devices, parts = lax.axis_size("patch"), lax.axis_size("mp")
    pairs = [
        (device * parts + column, (device ^ (column + parts * group)) * parts + column)
        for device in range(devices)
        for column in range(parts)
    ]
    return lax.ppermute(value, ("patch", "mp"), pairs)


def swap_both(value, offset, column_offset):
    devices, parts = lax.axis_size("patch"), lax.axis_size("mp")
    pairs = [
        (device * parts + column, (device ^ offset) * parts + (column ^ column_offset))
        for device in range(devices)
        for column in range(parts)
    ]
    return lax.ppermute(value, ("patch", "mp"), pairs)


def each_device(count, body):
    group = min(count, UNROLL)
    if count == group:
        for step in range(count):
            body(step)
        return

    @pl.loop(0, count // group)
    def _(outer):
        for step in range(group):
            body(outer * group + step)


def term_kernel(
    cotangent_hbm, second_hbm, kept, sent, turned, cotangent, second, arrivals
):
    for copy in fetch([(cotangent_hbm, cotangent), (second_hbm, second)], arrivals):
        copy.wait()
    turned[...] = cotangent[...].T
    parts = lax.axis_size("mp")
    odd = lax.axis_index("mp") % 2 == 1
    term = lax.dot_general(
        second[...], cotangent[...], (((1,), (1,)), ((), ())), preferred_element_type=F32
    )
    size = term.shape[0] // parts
    for pair in range(parts // 2):
        even_block = term[2 * pair * size : (2 * pair + 1) * size]
        odd_block = term[(2 * pair + 1) * size : (2 * pair + 2) * size]
        kept[pair] = jnp.where(odd, odd_block, even_block)
        sent[pair] = jnp.where(odd, even_block, odd_block)


def pack_kernel(
    patches, cap, source_hbm, live_hbm, weight_hbm, payload, source, live, weight, arrivals
):
    own, column = lax.axis_index("patch"), lax.axis_index("mp")
    parts = lax.axis_size("mp")
    slots, rows, width = weight.shape
    copies = fetch([(source_hbm, source), (live_hbm, live), (weight_hbm, weight)], arrivals)
    tail = cap * rows
    row = lax.broadcasted_iota(jnp.int32, (INDEX_ROWS, width), 0)
    payload[...] = jnp.zeros_like(payload)
    for copy in copies:
        copy.wait()
    for slot in range(slots):
        device = source[slot] // patches
        place = source[slot] % patches
        rank = jnp.int32(0)
        for other in range(slot):
            same = (source[other] // patches == device) & (live[other] == 1)
            rank = rank + same.astype(jnp.int32)
        apart = device ^ own

        @pl.when((live[slot] == 1) & (apart % parts == column))
        def _():
            group = apart // parts
            payload[group, pl.ds(pl.multiple_of(rank * rows, rows), rows)] = weight[slot]
            old = payload[group, tail:].astype(F32)
            payload[group, tail:] = jnp.where(row == rank, place.astype(F32), old).astype(BF16)


def local_kernel(latent, first, second, hidden, message, slope, scratch):
    column = lax.axis_index("mp")
    rows = latent.shape[0]
    own = slope.shape[0]
    tile = min(256, rows)
    for start in range(0, rows, tile):
        here = pl.ds(start, tile)
        pre = dot(latent[here], first[...])
        scratch[...] = pre
        value = (pre * jax.nn.sigmoid(pre)).astype(BF16)
        hidden[here] = value
        message[here] = dot(value, second[...]).astype(BF16)
        mine = scratch[:, pl.ds(pl.multiple_of(column * own, own), own)]
        gate = jax.nn.sigmoid(mine)
        slope[:, here] = (gate * (1.0 + mine * (1.0 - gate))).T


def each_block(near, far, gather_order, body):
    own, column = lax.axis_index("patch"), lax.axis_index("mp")
    sides, groups = near.shape[:2]
    for turn in range(2 * sides):
        held = far if turn % 2 else near

        def one(group):
            apart = (column ^ turn) + 2 * sides * group
            position = jnp.int32(0)
            for place, offset in enumerate(gather_order):
                position = position + (((apart // offset) & 1) << place)
            number = turn * groups + group
            body(held.at[turn // 2, group], own ^ apart, position, number)

        each_device(groups, one)


def spot(apart, order):
    number = jnp.int32(0)
    for offset in order:
        number = 2 * number + ((apart // offset) & 1)
    return number


def halve(value, offset, sent, kept):
    half = value.shape[0] // 2
    upper = (lax.axis_index("patch") // offset) % 2 == 1
    kept[...] = jnp.where(upper, value[half:], value[:half])
    sent[:half] = jnp.where(upper, value[:half], value[half:]).astype(BF16)


def gradient_kernel(
    cap,
    gather_order,
    second_order,
    first_order,
    scaling,
    places,
    near,
    far,
    carried,
    message,
    hidden,
    slope_hbm,
    latent,
    sent_second,
    kept_second,
    forward,
    sent_first,
    kept_first,
    terms,
    forwards,
    total,
    slope,
    arrivals,
):
    copies = fetch([(slope_hbm, slope)], arrivals)
    own = lax.axis_index("patch")
    width = message.shape[1]
    rows = near.shape[3]
    patches = message.shape[0] // rows

    def one(held, device, position, number):
        turned = carried[position]
        summed = None
        for rank in range(cap):
            place = places[number * cap + rank]
            block = held[rank * rows : (rank + 1) * rows]
            start = pl.multiple_of(place * rows, rows)
            product = dot(block, message[pl.ds(start, rows)])
            summed = product if summed is None else summed + product
            terms[number * cap + rank] = dot(turned, block)
        forwards[spot(device ^ own, second_order)] = summed

    each_block(near, far, gather_order, one)
    total[...] = jnp.zeros_like(total)

    def add(slot):
        place = places[slot]
        term = terms[slot]
        total[place, :width] += term[:width].astype(BF16).astype(F32)
        total[place, width:] += term[width:]

    each_device(terms.shape[0], add)
    turned_message = jnp.concatenate(
        [total[place, :width].astype(BF16) for place in range(patches)], axis=1
    )
    second = dot(turned_message, hidden[...]) * scaling
    halve(second.T, second_order[0], sent_second, kept_second)
    for copy in copies:
        copy.wait()
    grad_pre = jnp.concatenate(
        [
            (total[place, width:] * slope[:, place * rows : (place + 1) * rows]).astype(BF16)
            for place in range(patches)
        ],
        axis=1,
    )
    first = dot(grad_pre, latent[...]) * scaling
    halve(first.T, first_order[0], sent_first, kept_first)
    devices = forwards.shape[0]
    split = kept_second.shape[0]
    for device in range(devices // 2):
        here = device * rows
        forward[here : here + rows] = forwards[device]
        sent_second[split + here : split + here + rows] = forwards[
            devices // 2 + device
        ].astype(BF16)


def finish_kernel(
    second_offset,
    first_offset,
    mesh_latent,
    forward,
    own_second,
    got_second,
    own_first,
    got_first,
    mesh_hbm,
    first_hbm,
    second_hbm,
    mesh,
    first,
    second,
    departures,
):
    mesh[...] = (mesh_latent[...].astype(F32) + forward[...]).astype(BF16)
    copies = []
    for place, offset, own, got, whole, target in (
        (0, second_offset, own_second, got_second, second, second_hbm),
        (1, first_offset, own_first, got_first, first, first_hbm),
    ):
        half = own.shape[0]
        upper = (lax.axis_index("patch") // offset) % 2
        whole[pl.ds(pl.multiple_of(upper * half, half), half)] = own[...].astype(F32)
        whole[pl.ds(pl.multiple_of((1 - upper) * half, half), half)] = got[...].astype(F32)
        copies.append(pltpu.make_async_copy(whole, target, departures.at[place]))
        copies[-1].start()
    copies.append(pltpu.make_async_copy(mesh, mesh_hbm, departures.at[2]))
    copies[-1].start()
    for copy in copies:
        copy.wait()


def per_device(
    grid_latent,
    mesh_latent,
    edge_weight,
    block_source,
    block_live,
    mlp_first,
    mlp_second,
    mesh_cotangent,
):
    devices = lax.axis_size("patch")
    parts = lax.axis_size("mp")
    slots, rows, _ = edge_weight.shape
    grid_rows, depth = grid_latent.shape
    patches = grid_rows // rows
    hidden_width, width = mlp_second.shape
    hidden_local = hidden_width // parts
    cap = -(-slots // devices)
    column = lax.axis_index("mp")
    scaling = 1.0 / math.sqrt(grid_rows * devices)
    payload_rows = cap * rows + INDEX_ROWS
    groups = devices // parts

    slot_bytes = ((slots,), jnp.int32)
    kept, sent, turned = call(
        term_kernel,
        "term",
        [(HBM, mesh_cotangent), (HBM, mlp_second)],
        [
            (VMEM, (parts // 2, hidden_local, rows), F32),
            (VMEM, (parts // 2, hidden_local, rows), F32),
            (VMEM, (width, rows), BF16),
        ],
        scratch=[
            VMEM(mesh_cotangent.shape, BF16),
            VMEM(mlp_second.shape, BF16),
            pltpu.SemaphoreType.DMA((2,)),
        ],
    )
    (payload,) = call(
        functools.partial(pack_kernel, patches, cap),
        "pack",
        [(HBM, block_source), (HBM, block_live), (HBM, edge_weight)],
        [(VMEM, (groups, payload_rows, rows), BF16)],
        scratch=[
            SMEM(*slot_bytes),
            SMEM(*slot_bytes),
            VMEM(edge_weight.shape, BF16),
            pltpu.SemaphoreType.DMA((3,)),
        ],
    )

    summed = after(kept, payload) + swap(sent, "mp", 1)
    offset = 2
    while summed.shape[0] > 2:
        pairs = summed.reshape(-1, 2, *summed.shape[1:])
        bit = (column // offset) % 2
        stay = lax.dynamic_index_in_dim(pairs, bit, 1, keepdims=False)
        away = lax.dynamic_index_in_dim(pairs, 1 - bit, 1, keepdims=False)
        summed = stay + swap(away, "mp", offset)
        offset *= 2
    bit = (column // offset) % 2
    stay = lax.dynamic_index_in_dim(summed, bit, 0, keepdims=False)
    away = lax.dynamic_index_in_dim(summed, 1 - bit, 0, keepdims=False).astype(BF16)
    steps = devices.bit_length() - 1
    up = [1 << place for place in range(steps)]
    down = up[::-1]
    gather_order, second_order, first_order = down[:1] + up[:-1], [*up[1::-1], *up[2:]], up
    across = gather_order[0]
    beside = swap(away, "mp", offset)
    facing = swap(jnp.concatenate([turned, stay.astype(BF16)]), "patch", across)
    corner = swap_both(away, across, offset)
    here = jnp.concatenate([turned, (stay + beside.astype(F32)).astype(BF16)])
    there = facing[width:].astype(F32) + corner.astype(F32)
    there = jnp.concatenate([facing[:width], there.astype(BF16)])
    carried = jnp.stack([here, there])

    latent = after(grid_latent, carried)
    hidden, message, slope = call(
        local_kernel,
        "local",
        [(VMEM, latent), (VMEM, mlp_first), (VMEM, mlp_second)],
        [
            (VMEM, (grid_rows, hidden_width), BF16),
            (VMEM, (grid_rows, width), BF16),
            (VMEM, (hidden_local, grid_rows), F32),
        ],
        scratch=[VMEM((min(256, grid_rows), hidden_width), F32)],
    )

    payload = after(payload, beside)
    spreads = [spread(payload[group], group) for group in range(groups)]
    for place in range(1, steps, 2):
        moves = gather_order[place : place + 2]
        offsets = [moves[0]] if len(moves) == 1 else [moves[0], moves[1], moves[0] ^ moves[1]]
        arriving = [swap(carried, "patch", offset) for offset in offsets]
        if place == 1:
            arriving[0] = after(arriving[0], hidden)
        carried = jnp.concatenate([carried, *arriving])

    blocks = after(jnp.stack(spreads), hidden)
    near = blocks[None]
    offset = parts // 2
    while offset > 1:
        near = jnp.concatenate([near, swap(near, "mp", offset)])
        offset //= 2
    far = swap(near, "mp", 1)
    index_row = cap * rows
    places = jnp.stack([near, far], axis=1)[..., index_row : index_row + cap, 0]
    places = places.astype(jnp.int32).reshape(-1)

    sent_second, kept_second, forward, sent_first, kept_first = call(
        functools.partial(
            gradient_kernel, cap, gather_order, second_order, first_order, scaling
        ),
        "gradients",
        [
            (SMEM, places),
            (VMEM, near),
            (VMEM, far),
            (VMEM, carried),
            (VMEM, message),
            (VMEM, hidden),
            (HBM, slope),
            (VMEM, latent),
        ],
        [
            (VMEM, (hidden_width // 2 + devices // 2 * rows, width), BF16),
            (VMEM, (hidden_width // 2, width), F32),
            (VMEM, (devices // 2 * rows, width), F32),
            (VMEM, (depth // 2, hidden_local), BF16),
            (VMEM, (depth // 2, hidden_local), F32),
        ],
        scratch=[
            VMEM((devices * cap, width + hidden_local, rows), F32),
            VMEM((devices, rows, width), F32),
            VMEM((patches, width + hidden_local, rows), F32),
            VMEM(slope.shape, F32),
            pltpu.SemaphoreType.DMA((1,)),
        ],
    )

    split = hidden_width // 2
    for step in range(steps):
        got_second = swap(sent_second, "patch", second_order[step]).astype(F32)
        got_first = swap(sent_first, "patch", first_order[step]).astype(F32)
        second = kept_second + got_second[:split]
        forward = forward + got_second[split:]
        sent_first = (kept_first + got_first).astype(BF16)
        if step < steps - 1:
            size = forward.shape[0] // 2
            sent_second = jnp.concatenate([second, forward[size:]]).astype(BF16)
            forward = forward[:size]
            kept_second = sent_second[:split].astype(F32)
            kept_first = sent_first.astype(F32)
    second = second.astype(BF16)
    mesh_out, first, second = call(
        functools.partial(finish_kernel, second_order[0], first_order[0]),
        "finish",
        [
            (VMEM, mesh_latent),
            (VMEM, forward),
            (VMEM, second),
            (VMEM, swap(second, "patch", second_order[0])),
            (VMEM, sent_first),
            (VMEM, swap(sent_first, "patch", first_order[0])),
        ],
        [
            (HBM, (rows, width), BF16),
            (HBM, (depth, hidden_local), F32),
            (HBM, (hidden_width, width), F32),
        ],
        scratch=[
            VMEM((rows, width), BF16),
            VMEM((depth, hidden_local), F32),
            VMEM((hidden_width, width), F32),
            pltpu.SemaphoreType.DMA((3,)),
        ],
    )
    return (mesh_out, first, second)


def solution(mesh):
    placed = (
        P("patch", None),
        P("patch", "mp"),
        P("patch", None, None),
        P("patch"),
        P("patch"),
        P(),
        P(None, "mp"),
        P("patch", "mp"),
    )
    return jax.shard_map(
        per_device,
        mesh=mesh,
        in_specs=placed,
        out_specs=(P("patch", "mp"), P(None, "mp"), P(None, "mp")),
        check_vma=False,
    )
```

time: 63.8 us -> 58 us (0.909)
  starting transfers between devices: 29.1 us -> 23.7 us
  waiting for transfers between devices: 22.4 us -> 25.2 us
  other arithmetic: 2.69 us -> 0.41 us
    all_to_all x1 -> x0, starting transfers between devices: 5.77 us -> none  [per_device(): lax.all_to_all(payload, 'patch', split_axis=0, concat_axis=0, tiled=True)]
    ppermute x0 -> x3, starting transfers between devices: none -> 3.7 us  [the longest x1 2.49 us: swap_both(): return lax.ppermute(value, ('patch', 'mp'), pairs)]
    ppermute x12 -> x16, starting transfers between devices: 23.3 us -> 20 us  [swap(): return lax.ppermute(value, axis, [(i, i ^ offset) for i in range(size)])]
    ppermute x12 -> x16, waiting for transfers between devices: 22.2 us -> 25.2 us  [swap(): return lax.ppermute(value, axis, [(i, i ^ offset) for i in range(size)])]
    add x4 -> x3, other arithmetic: 1.49 us -> 0.06 us  [the longest x2 0.04 us: per_device(): forward = forward + got_second[split:]]
    convert_element_type x8 -> x10, other arithmetic: 1.01 us -> 0.18 us  [the longest x3 0.06 us: per_device(): got_second = swap(sent_second, 'patch', second_order[step]).astype(F32)]
    slice x3, local copies, waits for them, and re-layouts: 0.73 us -> 0.02 us  [the longest x2 0.02 us: per_device(): sent_second = jnp.concatenate([second, forward[size:]]).astype(BF16)]
  transfers between devices with their start and end apart: 13 -> 19, of which waited for: 9 -> 11; matrix products, arithmetic and copies ran while one was open for 3% -> 1% of each run, Pallas kernels for 6% -> 5%
where the time goes in v3:
time: 58 us; the launch traced here: 58.2 us
  waiting for transfers between devices  25.2 us (43%)
  starting transfers between devices  23.7 us (41%)
  Pallas kernels  7.55 us (13%)
  between operations  0.96 us (2%)
    ppermute x16, waiting for transfers between devices, swap(): return lax.ppermute(value, axis, [(i, i ^ offset) for i in range(size)])  25.2 us
    ppermute x16, starting transfers between devices, swap(): return lax.ppermute(value, axis, [(i, i ^ offset) for i in range(size)])  20 us
    pallas_call x5, Pallas kernels, call(): pl.pallas_call(kernel, out_shape=[space(shape, dtype) for space, shape, d...  7.55 us
    ppermute x1, starting transfers between devices, swap_both(): return lax.ppermute(value, ('patch', 'mp'), pairs)  2.49 us
    ppermute x2, starting transfers between devices, spread(): return lax.ppermute(value, ('patch', 'mp'), pairs)  1.21 us
  transfers between devices with their start and end apart: 19, of which 11 were waited for; matrix products, arithmetic and copies ran while one was open for 1% of the time, Pallas kernels for 5%

profile of v3, /device:TPU:0, one launch (start us, length us, event | category | flops | bytes accessed | tf_op | source)
XLA Modules:
  0.0 58.2 jit_solution(11342984044808758676)
XLA Ops:
  0.6 1.1 %term.1 = (f32[2,128,128]{2,1,0:T(8,128)S(1)}, f32[2,128,128]{2,1,0:T(8,128)S(1)}, bf16[128,128]{1,0:T(8,128)(2,1)S(1)}) custom-call(bf16[128,128]{1,0:T(8,128)(2,1)} %cotangent_hbm.1, bf16[512,128]{1,0:T(8,128)(2,1)} %second.1), custom_call_target="tpu_custom_call" | custom-call | tf_op jit(solution)/shard_map/term/pallas_call | solution.py:26
  1.8 0.5 collective-permute-start
  2.3 0.0 copy-start
  2.3 1.6 %pack.1 = bf16[2,272,128]{2,1,0:T(8,128)(2,1)S(1)} custom-call(s32[12]{0:T(128)} %source_hbm.1, s32[12]{0:T(128)} %live_hbm.1, bf16[12,128,128]{2,1,0:T(8,128)(2,1)} %weight_hbm.1), custom_call_target="tpu_custom_call" | custom-call | tf_op jit(solution)/shard_map/pack/pallas_call | solution.py:26
  3.9 0.0 collective-permute-done
  4.0 2.5 %collective-permute-start.1 = (bf16[128,128]{1,0:T(8,128)(2,1)S(1)}, bf16[128,128]{1,0:T(8,128)(2,1)S(1)}, u32[]{:S(2)}, u32[]{:S(2)}) collective-permute-start(bf16[128,128]{1,0:T(8,128)(2,1)S(1)} %get-tuple-element.42), channel_id=1, source_target_pairs={{0,2},{1,3},{2,0},{3,1},{4,6},{5,7},{6,4},{7,5},{8,10},{9,11},{10,... | collective-permute-start | bytes 98312 | tf_op jit(solution)/shard_map/ppermute | solution.py:59
  6.5 2.5 %collective-permute-start.5 = (bf16[128,128]{1,0:T(8,128)(2,1)S(1)}, bf16[128,128]{1,0:T(8,128)(2,1)S(1)}, u32[]{:S(2)}, u32[]{:S(2)}) collective-permute-start(bf16[128,128]{1,0:T(8,128)(2,1)S(1)} %get-tuple-element.42), channel_id=1, source_target_pairs={{0,18},{1,19},{2,16},{3,17},{4,22},{5,23},{6,20},{7,21},{8,26},{9,... | collective-permute-start | bytes 98312 | tf_op jit(solution)/shard_map/ppermute | solution.py:79
  9.0 0.0 collective-permute-done.1
  9.0 0.0 copy-start.2
  9.1 2.5 %collective-permute-start.4 = (bf16[256,128]{1,0:T(8,128)(2,1)S(1)}, bf16[256,128]{1,0:T(8,128)(2,1)S(1)}, u32[]{:S(2)}, u32[]{:S(2)}) collective-permute-start(bf16[256,128]{1,0:T(8,128)(2,1)S(1)} %get-tuple-element.44), channel_id=1, source_target_pairs={{0,16},{4,20},{8,24},{12,28},{16,0},{20,4},{24,8},{28,12},{1,17},{... | collective-permute-start | bytes 196616 | tf_op jit(solution)/shard_map/ppermute | solution.py:59
  11.6 0.7 %collective-permute-start.2 = (bf16[272,128]{1,0:T(8,128)(2,1)S(1)}, bf16[272,128]{1,0:T(8,128)(2,1)S(1)}, u32[]{:S(2)}, u32[]{:S(2)}) collective-permute-start(bf16[272,128]{1,0:T(8,128)(2,1)S(1)} %get-tuple-element.39), channel_id=1, source_target_pairs={{0,0},{1,5},{2,10},{3,15},{4,4},{5,1},{6,14},{7,11},{8,8},{9,13},{... | collective-permute-start | bytes 208904 | tf_op jit(solution)/shard_map/ppermute | solution.py:69
  12.3 0.5 collective-permute-start.3
  12.8 2.9 %collective-permute-done.4 = bf16[256,128]{1,0:T(8,128)(2,1)S(1)} collective-permute-done((bf16[256,128]{1,0:T(8,128)(2,1)S(1)}, bf16[256,128]{1,0:T(8,128)(2,1)S(1)}, u32[]{:S(2)}, u32[]{:S(2)}) %collective-permute-start.4) | collective-permute-done | bytes 65568 | tf_op jit(solution)/shard_map/ppermute | solution.py:59
  15.7 0.0 collective-permute-done.5
  15.7 0.0 copy-start.3
  15.8 1.6 %collective-permute-start.8 = (bf16[2,256,128]{2,1,0:T(8,128)(2,1)S(1)}, bf16[2,256,128]{2,1,0:T(8,128)(2,1)S(1)}, u32[]{:S(2)}, u32[]{:S(2)}) collective-permute-start(bf16[2,256,128]{2,1,0:T(8,128)(2,1)S(1)} %pad_maximum_fusion.2), channel_id=1, source_target_pairs={{0,4},{4,0},{8,12},{12,8},{16,20},{20,16},{24,28},{28,24},{1,5},{5... | collective-permute-start | bytes 393224 | tf_op jit(solution)/shard_map/ppermute | solution.py:59
  17.3 0.0 copy-done
  17.3 0.0 copy-done.2
  17.3 0.0 copy-done.3
  17.3 1.5 %local.1 = (bf16[1024,512]{1,0:T(8,128)(2,1)S(1)}, bf16[1024,128]{1,0:T(8,128)(2,1)S(1)}, f32[128,1024]{1,0:T(8,128)S(1)}) custom-call(bf16[1024,512]{1,0:T(8,128)(2,1)S(1)} %copy-done, bf16[512,512]{1,0:T(8,128)(2,1)S(1)} %copy-done.2, bf16[512,128]{1,0:T(8,128)(2,1)S(1)} %copy-done.3), custom_call_target="tpu_custom_call" | custom-call | tf_op jit(solution)/shard_map/local/pallas_call | solution.py:26
  18.9 0.0 copy-start.1
  18.9 0.0 collective-permute-done.2
  18.9 0.0 collective-permute-done.3
  18.9 3.9 %collective-permute-start.6 = (bf16[1,2,272,128]{3,2,1,0:T(8,128)(2,1)S(1)}, bf16[1,2,272,128]{3,2,1,0:T(8,128)(2,1)S(1)}, u32[]{:S(2)}, u32[]{:S(2)}) collective-permute-start(bf16[1,2,272,128]{3,2,1,0:T(8,128)(2,1)S(1)} %bitcast.28), channel_id=1, source_target_pairs={{0,2},{1,3},{2,0},{3,1},{4,6},{5,7},{6,4},{7,5},{8,10},{9,11},{10,... | collective-permute-start | bytes 417800 | tf_op jit(solution)/shard_map/ppermute | solution.py:59
  22.8 0.0 collective-permute-start.10
  22.8 3.0 %collective-permute-start.9 = (bf16[2,256,128]{2,1,0:T(8,128)(2,1)S(1)}, bf16[2,256,128]{2,1,0:T(8,128)(2,1)S(1)}, u32[]{:S(2)}, u32[]{:S(2)}) collective-permute-start(bf16[2,256,128]{2,1,0:T(8,128)(2,1)S(1)} %pad_maximum_fusion.2), channel_id=1, source_target_pairs={{0,8},{4,12},{8,0},{12,4},{16,24},{20,28},{24,16},{28,20},{1,9},{5... | collective-permute-start | bytes 393224 | tf_op jit(solution)/shard_map/ppermute | solution.py:59
  25.8 0.0 collective-permute-done.8
  25.9 0.0 copy-done.1
  25.9 0.9 %collective-permute-done.6 = bf16[1,2,272,128]{3,2,1,0:T(8,128)(2,1)S(1)} collective-permute-done((bf16[1,2,272,128]{3,2,1,0:T(8,128)(2,1)S(1)}, bf16[1,2,272,128]{3,2,1,0:T(8,128)(2,1)S(1)}, u32[]{:S(2)}, u32[]{:S(2)}) %collective-permute-start.6) | collective-permute-done | bytes 139296 | tf_op jit(solution)/shard_map/ppermute | solution.py:59
  26.8 0.1 collective-permute-start.7
  26.9 3.4 %collective-permute-done.9 = bf16[2,256,128]{2,1,0:T(8,128)(2,1)S(1)} collective-permute-done((bf16[2,256,128]{2,1,0:T(8,128)(2,1)S(1)}, bf16[2,256,128]{2,1,0:T(8,128)(2,1)S(1)}, u32[]{:S(2)}, u32[]{:S(2)}) %collective-permute-start.9) | collective-permute-done | bytes 131104 | tf_op jit(solution)/shard_map/ppermute | solution.py:59
  30.3 0.0 collective-permute-done.10
  30.3 0.0 collective-permute-done.7.far
  30.4 0.1 copy.12
  30.5 0.1 reshape.11.places
  30.6 2.4 %gradients.1 = (bf16[768,128]{1,0:T(8,128)(2,1)S(1)}, f32[256,128]{1,0:T(8,128)S(1)}, f32[512,128]{1,0:T(8,128)S(1)}, bf16[256,128]{1,0:T(8,128)(2,1)S(1)}, f32[256,128]{1,0:T(8,128)S(1)}) custom-call(s32[16]{0:T(128)S(1)} %reshape.11.places, bf16[2,2,272,128]{3,2,1,0:T(8,128)(2,1)S(1)} %get-tuple-element.36.near, ...), custom_call_target="tpu_custom_call" | custom-call | tf_op jit(solution)/shard_map/gradients/pallas_call | solution.py:26
  33.0 2.1 %collective-permute-start.15 = (bf16[256,128]{1,0:T(8,128)(2,1)S(1)}, bf16[256,128]{1,0:T(8,128)(2,1)S(1)}, u32[]{:S(2)}, u32[]{:S(2)}) collective-permute-start(bf16[256,128]{1,0:T(8,128)(2,1)S(1)} %get-tuple-element.34), channel_id=1, source_target_pairs={{0,4},{4,0},{8,12},{12,8},{16,20},{20,16},{24,28},{28,24},{1,5},{5... | collective-permute-start | bytes 196616 | tf_op jit(solution)/shard_map/ppermute | solution.py:59
  35.0 0.0 collective-permute-start.11
  35.1 2.3 %collective-permute-done.15 = bf16[256,128]{1,0:T(8,128)(2,1)S(1)} collective-permute-done((bf16[256,128]{1,0:T(8,128)(2,1)S(1)}, bf16[256,128]{1,0:T(8,128)(2,1)S(1)}, u32[]{:S(2)}, u32[]{:S(2)}) %collective-permute-start.15) | collective-permute-done | bytes 65568 | tf_op jit(solution)/shard_map/ppermute | solution.py:59
  37.3 0.9 %collective-permute-start.16 = (bf16[256,128]{1,0:T(8,128)(2,1)S(1)}, bf16[256,128]{1,0:T(8,128)(2,1)S(1)}, u32[]{:S(2)}, u32[]{:S(2)}) collective-permute-start(bf16[256,128]{1,0:T(8,128)(2,1)S(1)} %add_convert_fusion.2), channel_id=1, source_target_pairs={{0,8},{4,12},{8,0},{12,4},{16,24},{20,28},{24,16},{28,20},{1,9},{5... | collective-permute-start | bytes 196616 | tf_op jit(solution)/shard_map/ppermute | solution.py:59
  38.2 3.0 %collective-permute-done.11 = bf16[768,128]{1,0:T(8,128)(2,1)S(1)} collective-permute-done((bf16[768,128]{1,0:T(8,128)(2,1)S(1)}, bf16[768,128]{1,0:T(8,128)(2,1)S(1)}, u32[]{:S(2)}, u32[]{:S(2)}) %collective-permute-start.11) | collective-permute-done | bytes 196640 | tf_op jit(solution)/shard_map/ppermute | solution.py:59
  41.3 0.4 collective-permute-start.12
  41.7 0.1 collective-permute-done.16
  41.9 1.2 %collective-permute-start.17 = (bf16[256,128]{1,0:T(8,128)(2,1)S(1)}, bf16[256,128]{1,0:T(8,128)(2,1)S(1)}, u32[]{:S(2)}, u32[]{:S(2)}) collective-permute-start(bf16[256,128]{1,0:T(8,128)(2,1)S(1)} %add_convert_fusion.1), channel_id=1, source_target_pairs={{0,16},{4,20},{8,24},{12,28},{16,0},{20,4},{24,8},{28,12},{1,17},{... | collective-permute-start | bytes 196616 | tf_op jit(solution)/shard_map/ppermute | solution.py:59
  43.1 3.3 %collective-permute-done.12 = bf16[512,128]{1,0:T(8,128)(2,1)S(1)} collective-permute-done((bf16[512,128]{1,0:T(8,128)(2,1)S(1)}, bf16[512,128]{1,0:T(8,128)(2,1)S(1)}, u32[]{:S(2)}, u32[]{:S(2)}) %collective-permute-start.12) | collective-permute-done | bytes 131104 | tf_op jit(solution)/shard_map/ppermute | solution.py:59
  46.4 0.1 collective-permute-start.13
  46.6 2.3 %collective-permute-done.17 = bf16[256,128]{1,0:T(8,128)(2,1)S(1)} collective-permute-done((bf16[256,128]{1,0:T(8,128)(2,1)S(1)}, bf16[256,128]{1,0:T(8,128)(2,1)S(1)}, u32[]{:S(2)}, u32[]{:S(2)}) %collective-permute-start.17) | collective-permute-done | bytes 65568 | tf_op jit(solution)/shard_map/ppermute | solution.py:59
  48.9 1.1 %collective-permute-start.18 = (bf16[256,128]{1,0:T(8,128)(2,1)S(1)}, bf16[256,128]{1,0:T(8,128)(2,1)S(1)}, u32[]{:S(2)}, u32[]{:S(2)}) collective-permute-start(bf16[256,128]{1,0:T(8,128)(2,1)S(1)} %add_convert_fusion.own_first), channel_id=1, source_target_pairs={{0,4},{4,0},{8,12},{12,8},{16,20},{20,16},{24,28},{28,24},{1,5},{5... | collective-permute-start | bytes 196616 | tf_op jit(solution)/shard_map/ppermute | solution.py:59
  50.0 2.9 %collective-permute-done.13 = bf16[384,128]{1,0:T(8,128)(2,1)S(1)} collective-permute-done((bf16[384,128]{1,0:T(8,128)(2,1)S(1)}, bf16[384,128]{1,0:T(8,128)(2,1)S(1)}, u32[]{:S(2)}, u32[]{:S(2)}) %collective-permute-start.13) | collective-permute-done | bytes 98336 | tf_op jit(solution)/shard_map/ppermute | solution.py:59
  53.0 0.0 copy-start.4
  53.0 0.2 collective-permute-start.14
  53.1 0.1 collective-permute-done.18.got_first
  53.3 4.0 %collective-permute-done.14.got_second = bf16[256,128]{1,0:T(8,128)(2,1)S(1)} collective-permute-done((bf16[256,128]{1,0:T(8,128)(2,1)S(1)}, bf16[256,128]{1,0:T(8,128)(2,1)S(1)}, u32[]{:S(2)}, u32[]{:S(2)}) %collective-permute-start.14) | collective-permute-done | bytes 65568 | tf_op jit(solution)/shard_map/ppermute | solution.py:59
  57.3 0.0 copy-done.4
  57.3 0.9 %finish.1 = (bf16[128,128]{1,0:T(8,128)(2,1)}, f32[512,128]{1,0:T(8,128)}, f32[512,128]{1,0:T(8,128)}) custom-call(bf16[128,128]{1,0:T(8,128)(2,1)S(1)} %copy-done.4, f32[128,128]{1,0:T(8,128)S(1)} %slice_add_fusion.5.forward, bf16[256,128]{1,0:T(8,128)(2,1)S(1)} %fusion.own_second, bf16[256,128]{1,0:T(8,128)(2,1)S(1)} %collective-permute-done.14.got_second, ...), custom_call_target="tpu_custom_call" | custom-call | tf_op jit(solution)/shard_map/finish/pallas_call | solution.py:26
  (32 shorter events, 0.5 us)
Async XLA Ops:
  1.8 2.2 %collective-permute-start = (f32[2,128,128]{2,1,0:T(8,128)S(1)}, f32[2,128,128]{2,1,0:T(8,128)S(1)}, u32[]{:S(2)}, u32[]{:S(2)}) collective-permute-start(f32[2,128,128]{2,1,0:T(8,128)S(1)} %get-tuple-element.21), channel_id=1, source_target_pairs={{0,1},{1,0},{2,3},{3,2},{4,5},{5,4},{6,7},{7,6},{8,9},{9,8},{10,11... | collective-permute-start | bytes 393224 | tf_op jit(solution)/shard_map/ppermute | solution.py:59
  2.3 15.0 %copy-start = (bf16[1024,512]{1,0:T(8,128)(2,1)S(1)}, bf16[1024,512]{1,0:T(8,128)(2,1)}, u32[]{:S(2)}) copy-start(bf16[1024,512]{1,0:T(8,128)(2,1)} %latent.1) | copy-start | bytes 3145732
  4.0 5.0 %collective-permute-start.1 = (bf16[128,128]{1,0:T(8,128)(2,1)S(1)}, bf16[128,128]{1,0:T(8,128)(2,1)S(1)}, u32[]{:S(2)}, u32[]{:S(2)}) collective-permute-start(bf16[128,128]{1,0:T(8,128)(2,1)S(1)} %get-tuple-element.42), channel_id=1, source_target_pairs={{0,2},{1,3},{2,0},{3,1},{4,6},{5,7},{6,4},{7,5},{8,10},{9,11},{10,... | collective-permute-start | bytes 98312 | tf_op jit(solution)/shard_map/ppermute | solution.py:59
  6.5 9.2 %collective-permute-start.5 = (bf16[128,128]{1,0:T(8,128)(2,1)S(1)}, bf16[128,128]{1,0:T(8,128)(2,1)S(1)}, u32[]{:S(2)}, u32[]{:S(2)}) collective-permute-start(bf16[128,128]{1,0:T(8,128)(2,1)S(1)} %get-tuple-element.42), channel_id=1, source_target_pairs={{0,18},{1,19},{2,16},{3,17},{4,22},{5,23},{6,20},{7,21},{8,26},{9,... | collective-permute-start | bytes 98312 | tf_op jit(solution)/shard_map/ppermute | solution.py:79
  9.0 8.3 %copy-start.2 = (bf16[512,512]{1,0:T(8,128)(2,1)S(1)}, bf16[512,512]{1,0:T(8,128)(2,1)}, u32[]{:S(2)}) copy-start(bf16[512,512]{1,0:T(8,128)(2,1)} %first.1) | copy-start | bytes 1572868
  9.1 6.6 %collective-permute-start.4 = (bf16[256,128]{1,0:T(8,128)(2,1)S(1)}, bf16[256,128]{1,0:T(8,128)(2,1)S(1)}, u32[]{:S(2)}, u32[]{:S(2)}) collective-permute-start(bf16[256,128]{1,0:T(8,128)(2,1)S(1)} %get-tuple-element.44), channel_id=1, source_target_pairs={{0,16},{4,20},{8,24},{12,28},{16,0},{20,4},{24,8},{28,12},{1,17},{... | collective-permute-start | bytes 196616 | tf_op jit(solution)/shard_map/ppermute | solution.py:59
  11.6 7.3 %collective-permute-start.2 = (bf16[272,128]{1,0:T(8,128)(2,1)S(1)}, bf16[272,128]{1,0:T(8,128)(2,1)S(1)}, u32[]{:S(2)}, u32[]{:S(2)}) collective-permute-start(bf16[272,128]{1,0:T(8,128)(2,1)S(1)} %get-tuple-element.39), channel_id=1, source_target_pairs={{0,0},{1,5},{2,10},{3,15},{4,4},{5,1},{6,14},{7,11},{8,8},{9,13},{... | collective-permute-start | bytes 208904 | tf_op jit(solution)/shard_map/ppermute | solution.py:69
  12.3 6.6 %collective-permute-start.3 = (bf16[272,128]{1,0:T(8,128)(2,1)S(1)}, bf16[272,128]{1,0:T(8,128)(2,1)S(1)}, u32[]{:S(2)}, u32[]{:S(2)}) collective-permute-start(bf16[272,128]{1,0:T(8,128)(2,1)S(1)} %get-tuple-element.40), channel_id=1, source_target_pairs={{0,16},{1,21},{2,26},{3,31},{4,20},{5,17},{6,30},{7,27},{8,24},{9,... | collective-permute-start | bytes 208904 | tf_op jit(solution)/shard_map/ppermute | solution.py:69
  15.7 1.6 %copy-start.3 = (bf16[512,128]{1,0:T(8,128)(2,1)S(1)}, bf16[512,128]{1,0:T(8,128)(2,1)}, u32[]{:S(2)}) copy-start(bf16[512,128]{1,0:T(8,128)(2,1)} %second.1) | copy-start | bytes 393220
  15.8 10.1 %collective-permute-start.8 = (bf16[2,256,128]{2,1,0:T(8,128)(2,1)S(1)}, bf16[2,256,128]{2,1,0:T(8,128)(2,1)S(1)}, u32[]{:S(2)}, u32[]{:S(2)}) collective-permute-start(bf16[2,256,128]{2,1,0:T(8,128)(2,1)S(1)} %pad_maximum_fusion.2), channel_id=1, source_target_pairs={{0,4},{4,0},{8,12},{12,8},{16,20},{20,16},{24,28},{28,24},{1,5},{5... | collective-permute-start | bytes 393224 | tf_op jit(solution)/shard_map/ppermute | solution.py:59
  18.9 7.0 %copy-start.1 = (f32[128,1024]{1,0:T(8,128)}, f32[128,1024]{1,0:T(8,128)S(1)}, u32[]{:S(2)}) copy-start(f32[128,1024]{1,0:T(8,128)S(1)} %get-tuple-element.29.slope_hbm) | copy-start | bytes 1572868
  18.9 7.8 %collective-permute-start.6 = (bf16[1,2,272,128]{3,2,1,0:T(8,128)(2,1)S(1)}, bf16[1,2,272,128]{3,2,1,0:T(8,128)(2,1)S(1)}, u32[]{:S(2)}, u32[]{:S(2)}) collective-permute-start(bf16[1,2,272,128]{3,2,1,0:T(8,128)(2,1)S(1)} %bitcast.28), channel_id=1, source_target_pairs={{0,2},{1,3},{2,0},{3,1},{4,6},{5,7},{6,4},{7,5},{8,10},{9,11},{10,... | collective-permute-start | bytes 417800 | tf_op jit(solution)/shard_map/ppermute | solution.py:59
  22.8 7.5 %collective-permute-start.10 = (bf16[2,256,128]{2,1,0:T(8,128)(2,1)S(1)}, bf16[2,256,128]{2,1,0:T(8,128)(2,1)S(1)}, u32[]{:S(2)}, u32[]{:S(2)}) collective-permute-start(bf16[2,256,128]{2,1,0:T(8,128)(2,1)S(1)} %pad_maximum_fusion.2), channel_id=1, source_target_pairs={{0,12},{4,8},{8,4},{12,0},{16,28},{20,24},{24,20},{28,16},{1,13},{... | collective-permute-start | bytes 393224 | tf_op jit(solution)/shard_map/ppermute | solution.py:59
  22.8 7.5 %collective-permute-start.9 = (bf16[2,256,128]{2,1,0:T(8,128)(2,1)S(1)}, bf16[2,256,128]{2,1,0:T(8,128)(2,1)S(1)}, u32[]{:S(2)}, u32[]{:S(2)}) collective-permute-start(bf16[2,256,128]{2,1,0:T(8,128)(2,1)S(1)} %pad_maximum_fusion.2), channel_id=1, source_target_pairs={{0,8},{4,12},{8,0},{12,4},{16,24},{20,28},{24,16},{28,20},{1,9},{5... | collective-permute-start | bytes 393224 | tf_op jit(solution)/shard_map/ppermute | solution.py:59
  26.8 3.6 %collective-permute-start.7 = (bf16[2,2,272,128]{3,2,1,0:T(8,128)(2,1)S(1)}, bf16[2,2,272,128]{3,2,1,0:T(8,128)(2,1)S(1)}, u32[]{:S(2)}, u32[]{:S(2)}) collective-permute-start(bf16[2,2,272,128]{3,2,1,0:T(8,128)(2,1)S(1)} %get-tuple-element.36.near), channel_id=1, source_target_pairs={{0,1},{1,0},{2,3},{3,2},{4,5},{5,4},{6,7},{7,6},{8,9},{9,8},{10,11... | collective-permute-start | bytes 835592 | tf_op jit(solution)/shard_map/ppermute | solution.py:59
  33.0 4.3 %collective-permute-start.15 = (bf16[256,128]{1,0:T(8,128)(2,1)S(1)}, bf16[256,128]{1,0:T(8,128)(2,1)S(1)}, u32[]{:S(2)}, u32[]{:S(2)}) collective-permute-start(bf16[256,128]{1,0:T(8,128)(2,1)S(1)} %get-tuple-element.34), channel_id=1, source_target_pairs={{0,4},{4,0},{8,12},{12,8},{16,20},{20,16},{24,28},{28,24},{1,5},{5... | collective-permute-start | bytes 196616 | tf_op jit(solution)/shard_map/ppermute | solution.py:59
  35.0 6.1 %collective-permute-start.11 = (bf16[768,128]{1,0:T(8,128)(2,1)S(1)}, bf16[768,128]{1,0:T(8,128)(2,1)S(1)}, u32[]{:S(2)}, u32[]{:S(2)}) collective-permute-start(bf16[768,128]{1,0:T(8,128)(2,1)S(1)} %get-tuple-element.31), channel_id=1, source_target_pairs={{0,8},{4,12},{8,0},{12,4},{16,24},{20,28},{24,16},{28,20},{1,9},{5... | collective-permute-start | bytes 589832 | tf_op jit(solution)/shard_map/ppermute | solution.py:59
  37.3 4.6 %collective-permute-start.16 = (bf16[256,128]{1,0:T(8,128)(2,1)S(1)}, bf16[256,128]{1,0:T(8,128)(2,1)S(1)}, u32[]{:S(2)}, u32[]{:S(2)}) collective-permute-start(bf16[256,128]{1,0:T(8,128)(2,1)S(1)} %add_convert_fusion.2), channel_id=1, source_target_pairs={{0,8},{4,12},{8,0},{12,4},{16,24},{20,28},{24,16},{28,20},{1,9},{5... | collective-permute-start | bytes 196616 | tf_op jit(solution)/shard_map/ppermute | solution.py:59
  41.3 5.0 %collective-permute-start.12 = (bf16[512,128]{1,0:T(8,128)(2,1)S(1)}, bf16[512,128]{1,0:T(8,128)(2,1)S(1)}, u32[]{:S(2)}, u32[]{:S(2)}) collective-permute-start(bf16[512,128]{1,0:T(8,128)(2,1)S(1)} %pad_maximum_fusion.3), channel_id=1, source_target_pairs={{0,4},{4,0},{8,12},{12,8},{16,20},{20,16},{24,28},{28,24},{1,5},{5... | collective-permute-start | bytes 393224 | tf_op jit(solution)/shard_map/ppermute | solution.py:59
  41.9 7.0 %collective-permute-start.17 = (bf16[256,128]{1,0:T(8,128)(2,1)S(1)}, bf16[256,128]{1,0:T(8,128)(2,1)S(1)}, u32[]{:S(2)}, u32[]{:S(2)}) collective-permute-start(bf16[256,128]{1,0:T(8,128)(2,1)S(1)} %add_convert_fusion.1), channel_id=1, source_target_pairs={{0,16},{4,20},{8,24},{12,28},{16,0},{20,4},{24,8},{28,12},{1,17},{... | collective-permute-start | bytes 196616 | tf_op jit(solution)/shard_map/ppermute | solution.py:59
  46.4 6.5 %collective-permute-start.13 = (bf16[384,128]{1,0:T(8,128)(2,1)S(1)}, bf16[384,128]{1,0:T(8,128)(2,1)S(1)}, u32[]{:S(2)}, u32[]{:S(2)}) collective-permute-start(bf16[384,128]{1,0:T(8,128)(2,1)S(1)} %pad_maximum_fusion.4), channel_id=1, source_target_pairs={{0,16},{4,20},{8,24},{12,28},{16,0},{20,4},{24,8},{28,12},{1,17},{... | collective-permute-start | bytes 294920 | tf_op jit(solution)/shard_map/ppermute | solution.py:59
  48.9 4.3 %collective-permute-start.18 = (bf16[256,128]{1,0:T(8,128)(2,1)S(1)}, bf16[256,128]{1,0:T(8,128)(2,1)S(1)}, u32[]{:S(2)}, u32[]{:S(2)}) collective-permute-start(bf16[256,128]{1,0:T(8,128)(2,1)S(1)} %add_convert_fusion.own_first), channel_id=1, source_target_pairs={{0,4},{4,0},{8,12},{12,8},{16,20},{20,16},{24,28},{28,24},{1,5},{5... | collective-permute-start | bytes 196616 | tf_op jit(solution)/shard_map/ppermute | solution.py:59
  53.0 4.3 %copy-start.4 = (bf16[128,128]{1,0:T(8,128)(2,1)S(1)}, bf16[128,128]{1,0:T(8,128)(2,1)}, u32[]{:S(2)}) copy-start(bf16[128,128]{1,0:T(8,128)(2,1)} %mesh_latent.1) | copy-start | bytes 98308
  53.0 4.3 %collective-permute-start.14 = (bf16[256,128]{1,0:T(8,128)(2,1)S(1)}, bf16[256,128]{1,0:T(8,128)(2,1)S(1)}, u32[]{:S(2)}, u32[]{:S(2)}) collective-permute-start(bf16[256,128]{1,0:T(8,128)(2,1)S(1)} %fusion.own_second), channel_id=1, source_target_pairs={{0,8},{4,12},{8,0},{12,4},{16,24},{20,28},{24,16},{28,20},{1,9},{5... | collective-permute-start | bytes 196616 | tf_op jit(solution)/shard_map/ppermute | solution.py:59

commit v4 on v3

--- a/solution.py
+++ b/solution.py
@@ -402,13 +402,13 @@
             arriving[0] = after(arriving[0], hidden)
         carried = jnp.concatenate([carried, *arriving])
 
-    blocks = after(jnp.stack(spreads), hidden)
+    blocks = jnp.stack(spreads)
     near = blocks[None]
     offset = parts // 2
     while offset > 1:
         near = jnp.concatenate([near, swap(near, "mp", offset)])
         offset //= 2
-    far = swap(near, "mp", 1)
+    far = swap(after(near, carried), "mp", 1)
     index_row = cap * rows
     places = jnp.stack([near, far], axis=1)[..., index_row : index_row + cap, 0]
     places = places.astype(jnp.int32).reshape(-1)

time: 58 us -> 57.1 us (0.984)
  starting transfers between devices: 23.7 us -> 23 us
    ppermute x16, starting transfers between devices: 20 us -> 19.2 us  [swap(): return lax.ppermute(value, axis, [(i, i ^ offset) for i in range(size)])]
where the time goes in v4:
time: 57.1 us; the launch traced here: 56.9 us
  waiting for transfers between devices  24.7 us (43%)
  starting transfers between devices  23 us (40%)
  Pallas kernels  7.49 us (13%)
  between operations  0.99 us (2%)
    ppermute x16, waiting for transfers between devices, swap(): return lax.ppermute(value, axis, [(i, i ^ offset) for i in range(size)])  24.7 us
    ppermute x16, starting transfers between devices, swap(): return lax.ppermute(value, axis, [(i, i ^ offset) for i in range(size)])  19.2 us
    pallas_call x5, Pallas kernels, call(): pl.pallas_call(kernel, out_shape=[space(shape, dtype) for space, shape, d...  7.49 us
    ppermute x1, starting transfers between devices, swap_both(): return lax.ppermute(value, ('patch', 'mp'), pairs)  2.58 us
    ppermute x2, starting transfers between devices, spread(): return lax.ppermute(value, ('patch', 'mp'), pairs)  1.21 us
  transfers between devices with their start and end apart: 19, of which 11 were waited for; matrix products, arithmetic and copies ran while one was open for 1% of the time, Pallas kernels for 5%

profile of v4, /device:TPU:0, one launch (start us, length us, event | category | flops | bytes accessed | tf_op | source)
XLA Modules:
  0.0 56.9 jit_solution(7680059511005952966)
XLA Ops:
  0.6 1.1 %term.1 = (f32[2,128,128]{2,1,0:T(8,128)S(1)}, f32[2,128,128]{2,1,0:T(8,128)S(1)}, bf16[128,128]{1,0:T(8,128)(2,1)S(1)}) custom-call(bf16[128,128]{1,0:T(8,128)(2,1)} %cotangent_hbm.1, bf16[512,128]{1,0:T(8,128)(2,1)} %second.1), custom_call_target="tpu_custom_call" | custom-call | tf_op jit(solution)/shard_map/term/pallas_call | solution.py:26
  1.8 0.5 collective-permute-start
  2.3 1.6 %pack.1 = bf16[2,272,128]{2,1,0:T(8,128)(2,1)S(1)} custom-call(s32[12]{0:T(128)} %source_hbm.1, s32[12]{0:T(128)} %live_hbm.1, bf16[12,128,128]{2,1,0:T(8,128)(2,1)} %weight_hbm.1), custom_call_target="tpu_custom_call" | custom-call | tf_op jit(solution)/shard_map/pack/pallas_call | solution.py:26
  3.9 0.0 copy-start
  3.9 0.0 collective-permute-done
  4.0 2.4 %collective-permute-start.1 = (bf16[128,128]{1,0:T(8,128)(2,1)S(1)}, bf16[128,128]{1,0:T(8,128)(2,1)S(1)}, u32[]{:S(2)}, u32[]{:S(2)}) collective-permute-start(bf16[128,128]{1,0:T(8,128)(2,1)S(1)} %get-tuple-element.42), channel_id=1, source_target_pairs={{0,2},{1,3},{2,0},{3,1},{4,6},{5,7},{6,4},{7,5},{8,10},{9,11},{10,... | collective-permute-start | bytes 98312 | tf_op jit(solution)/shard_map/ppermute | solution.py:59
  6.3 2.6 %collective-permute-start.6 = (bf16[128,128]{1,0:T(8,128)(2,1)S(1)}, bf16[128,128]{1,0:T(8,128)(2,1)S(1)}, u32[]{:S(2)}, u32[]{:S(2)}) collective-permute-start(bf16[128,128]{1,0:T(8,128)(2,1)S(1)} %get-tuple-element.42), channel_id=1, source_target_pairs={{0,18},{1,19},{2,16},{3,17},{4,22},{5,23},{6,20},{7,21},{8,26},{9,... | collective-permute-start | bytes 98312 | tf_op jit(solution)/shard_map/ppermute | solution.py:79
  8.9 0.0 collective-permute-done.1
  8.9 0.0 copy-start.2
  8.9 2.5 %collective-permute-start.5 = (bf16[256,128]{1,0:T(8,128)(2,1)S(1)}, bf16[256,128]{1,0:T(8,128)(2,1)S(1)}, u32[]{:S(2)}, u32[]{:S(2)}) collective-permute-start(bf16[256,128]{1,0:T(8,128)(2,1)S(1)} %get-tuple-element.44), channel_id=1, source_target_pairs={{0,16},{4,20},{8,24},{12,28},{16,0},{20,4},{24,8},{28,12},{1,17},{... | collective-permute-start | bytes 196616 | tf_op jit(solution)/shard_map/ppermute | solution.py:59
  11.5 0.7 %collective-permute-start.2 = (bf16[272,128]{1,0:T(8,128)(2,1)S(1)}, bf16[272,128]{1,0:T(8,128)(2,1)S(1)}, u32[]{:S(2)}, u32[]{:S(2)}) collective-permute-start(bf16[272,128]{1,0:T(8,128)(2,1)S(1)} %get-tuple-element.39), channel_id=1, source_target_pairs={{0,0},{1,5},{2,10},{3,15},{4,4},{5,1},{6,14},{7,11},{8,8},{9,13},{... | collective-permute-start | bytes 208904 | tf_op jit(solution)/shard_map/ppermute | solution.py:69
  12.2 0.5 collective-permute-start.3
  12.7 2.9 %collective-permute-done.5 = bf16[256,128]{1,0:T(8,128)(2,1)S(1)} collective-permute-done((bf16[256,128]{1,0:T(8,128)(2,1)S(1)}, bf16[256,128]{1,0:T(8,128)(2,1)S(1)}, u32[]{:S(2)}, u32[]{:S(2)}) %collective-permute-start.5) | collective-permute-done | bytes 65568 | tf_op jit(solution)/shard_map/ppermute | solution.py:59
  15.6 0.0 collective-permute-done.6
  15.6 0.0 copy-start.3
  15.6 1.5 %collective-permute-start.7 = (bf16[2,256,128]{2,1,0:T(8,128)(2,1)S(1)}, bf16[2,256,128]{2,1,0:T(8,128)(2,1)S(1)}, u32[]{:S(2)}, u32[]{:S(2)}) collective-permute-start(bf16[2,256,128]{2,1,0:T(8,128)(2,1)S(1)} %pad_maximum_fusion.1), channel_id=1, source_target_pairs={{0,4},{4,0},{8,12},{12,8},{16,20},{20,16},{24,28},{28,24},{1,5},{5... | collective-permute-start | bytes 393224 | tf_op jit(solution)/shard_map/ppermute | solution.py:59
  17.1 0.2 collective-permute-start.8
  17.4 1.8 %collective-permute-start.9 = (bf16[2,256,128]{2,1,0:T(8,128)(2,1)S(1)}, bf16[2,256,128]{2,1,0:T(8,128)(2,1)S(1)}, u32[]{:S(2)}, u32[]{:S(2)}) collective-permute-start(bf16[2,256,128]{2,1,0:T(8,128)(2,1)S(1)} %pad_maximum_fusion.1), channel_id=1, source_target_pairs={{0,12},{4,8},{8,4},{12,0},{16,28},{20,24},{24,20},{28,16},{1,13},{... | collective-permute-start | bytes 393224 | tf_op jit(solution)/shard_map/ppermute | solution.py:59
  19.2 0.0 copy-done
  19.2 0.0 copy-done.2
  19.2 0.0 copy-done.3
  19.2 1.5 %local.1 = (bf16[1024,512]{1,0:T(8,128)(2,1)S(1)}, bf16[1024,128]{1,0:T(8,128)(2,1)S(1)}, f32[128,1024]{1,0:T(8,128)S(1)}) custom-call(bf16[1024,512]{1,0:T(8,128)(2,1)S(1)} %copy-done, bf16[512,512]{1,0:T(8,128)(2,1)S(1)} %copy-done.2, bf16[512,128]{1,0:T(8,128)(2,1)S(1)} %copy-done.3), custom_call_target="tpu_custom_call" | custom-call | tf_op jit(solution)/shard_map/local/pallas_call | solution.py:26
  20.8 0.0 copy-start.1
  20.8 0.0 collective-permute-done.2
  20.8 0.0 collective-permute-done.3
  20.8 2.7 %collective-permute-start.4 = (bf16[1,2,272,128]{3,2,1,0:T(8,128)(2,1)S(1)}, bf16[1,2,272,128]{3,2,1,0:T(8,128)(2,1)S(1)}, u32[]{:S(2)}, u32[]{:S(2)}) collective-permute-start(bf16[1,2,272,128]{3,2,1,0:T(8,128)(2,1)S(1)} %maximum_bitcast_fusion), channel_id=1, source_target_pairs={{0,2},{1,3},{2,0},{3,1},{4,6},{5,7},{6,4},{7,5},{8,10},{9,11},{10,... | collective-permute-start | bytes 417800 | tf_op jit(solution)/shard_map/ppermute | solution.py:59
  23.6 0.0 collective-permute-done.7
  23.6 0.0 collective-permute-done.8
  23.6 1.3 %collective-permute-done.9 = bf16[2,256,128]{2,1,0:T(8,128)(2,1)S(1)} collective-permute-done((bf16[2,256,128]{2,1,0:T(8,128)(2,1)S(1)}, bf16[2,256,128]{2,1,0:T(8,128)(2,1)S(1)}, u32[]{:S(2)}, u32[]{:S(2)}) %collective-permute-start.9) | collective-permute-done | bytes 131104 | tf_op jit(solution)/shard_map/ppermute | solution.py:59
  24.9 0.0 copy-done.1
  24.9 1.6 %collective-permute-done.4 = bf16[1,2,272,128]{3,2,1,0:T(8,128)(2,1)S(1)} collective-permute-done((bf16[1,2,272,128]{3,2,1,0:T(8,128)(2,1)S(1)}, bf16[1,2,272,128]{3,2,1,0:T(8,128)(2,1)S(1)}, u32[]{:S(2)}, u32[]{:S(2)}) %collective-permute-start.4) | collective-permute-done | bytes 139296 | tf_op jit(solution)/shard_map/ppermute | solution.py:59
  26.6 0.1 collective-permute-start.10
  26.7 1.5 %collective-permute-done.10.far = bf16[2,2,272,128]{3,2,1,0:T(8,128)(2,1)S(1)} collective-permute-done((bf16[2,2,272,128]{3,2,1,0:T(8,128)(2,1)S(1)}, bf16[2,2,272,128]{3,2,1,0:T(8,128)(2,1)S(1)}, u32[]{:S(2)}, u32[]{:S(2)}) %collective-permute-start.10) | collective-permute-done | bytes 278560 | tf_op jit(solution)/shard_map/ppermute | solution.py:59
  28.3 0.1 copy.12
  28.4 0.1 reshape.11.places
  28.5 2.4 %gradients.1 = (bf16[768,128]{1,0:T(8,128)(2,1)S(1)}, f32[256,128]{1,0:T(8,128)S(1)}, f32[512,128]{1,0:T(8,128)S(1)}, bf16[256,128]{1,0:T(8,128)(2,1)S(1)}, f32[256,128]{1,0:T(8,128)S(1)}) custom-call(s32[16]{0:T(128)S(1)} %reshape.11.places, bf16[2,2,272,128]{3,2,1,0:T(8,128)(2,1)S(1)} %get-tuple-element.27.near, ...), custom_call_target="tpu_custom_call" | custom-call | tf_op jit(solution)/shard_map/gradients/pallas_call | solution.py:26
  30.9 1.5 %collective-permute-start.15 = (bf16[256,128]{1,0:T(8,128)(2,1)S(1)}, bf16[256,128]{1,0:T(8,128)(2,1)S(1)}, u32[]{:S(2)}, u32[]{:S(2)}) collective-permute-start(bf16[256,128]{1,0:T(8,128)(2,1)S(1)} %get-tuple-element.34), channel_id=1, source_target_pairs={{0,4},{4,0},{8,12},{12,8},{16,20},{20,16},{24,28},{28,24},{1,5},{5... | collective-permute-start | bytes 196616 | tf_op jit(solution)/shard_map/ppermute | solution.py:59
  32.4 0.0 collective-permute-start.11
  32.4 2.9 %collective-permute-done.15 = bf16[256,128]{1,0:T(8,128)(2,1)S(1)} collective-permute-done((bf16[256,128]{1,0:T(8,128)(2,1)S(1)}, bf16[256,128]{1,0:T(8,128)(2,1)S(1)}, u32[]{:S(2)}, u32[]{:S(2)}) %collective-permute-start.15) | collective-permute-done | bytes 65568 | tf_op jit(solution)/shard_map/ppermute | solution.py:59
  35.2 0.1 collective-permute-start.16
  35.3 4.4 %collective-permute-done.11 = bf16[768,128]{1,0:T(8,128)(2,1)S(1)} collective-permute-done((bf16[768,128]{1,0:T(8,128)(2,1)S(1)}, bf16[768,128]{1,0:T(8,128)(2,1)S(1)}, u32[]{:S(2)}, u32[]{:S(2)}) %collective-permute-start.11) | collective-permute-done | bytes 196640 | tf_op jit(solution)/shard_map/ppermute | solution.py:59
  39.9 0.7 %collective-permute-start.12 = (bf16[512,128]{1,0:T(8,128)(2,1)S(1)}, bf16[512,128]{1,0:T(8,128)(2,1)S(1)}, u32[]{:S(2)}, u32[]{:S(2)}) collective-permute-start(bf16[512,128]{1,0:T(8,128)(2,1)S(1)} %pad_maximum_fusion.2), channel_id=1, source_target_pairs={{0,4},{4,0},{8,12},{12,8},{16,20},{20,16},{24,28},{28,24},{1,5},{5... | collective-permute-start | bytes 393224 | tf_op jit(solution)/shard_map/ppermute | solution.py:59
  40.5 0.0 collective-permute-done.16
  40.6 1.7 %collective-permute-start.17 = (bf16[256,128]{1,0:T(8,128)(2,1)S(1)}, bf16[256,128]{1,0:T(8,128)(2,1)S(1)}, u32[]{:S(2)}, u32[]{:S(2)}) collective-permute-start(bf16[256,128]{1,0:T(8,128)(2,1)S(1)} %add_convert_fusion.1), channel_id=1, source_target_pairs={{0,16},{4,20},{8,24},{12,28},{16,0},{20,4},{24,8},{28,12},{1,17},{... | collective-permute-start | bytes 196616 | tf_op jit(solution)/shard_map/ppermute | solution.py:59
  42.3 2.6 %collective-permute-done.12 = bf16[512,128]{1,0:T(8,128)(2,1)S(1)} collective-permute-done((bf16[512,128]{1,0:T(8,128)(2,1)S(1)}, bf16[512,128]{1,0:T(8,128)(2,1)S(1)}, u32[]{:S(2)}, u32[]{:S(2)}) %collective-permute-start.12) | collective-permute-done | bytes 131104 | tf_op jit(solution)/shard_map/ppermute | solution.py:59
  45.0 1.8 %collective-permute-start.13 = (bf16[384,128]{1,0:T(8,128)(2,1)S(1)}, bf16[384,128]{1,0:T(8,128)(2,1)S(1)}, u32[]{:S(2)}, u32[]{:S(2)}) collective-permute-start(bf16[384,128]{1,0:T(8,128)(2,1)S(1)} %pad_maximum_fusion.3), channel_id=1, source_target_pairs={{0,16},{4,20},{8,24},{12,28},{16,0},{20,4},{24,8},{28,12},{1,17},{... | collective-permute-start | bytes 294920 | tf_op jit(solution)/shard_map/ppermute | solution.py:59
  46.8 1.3 %collective-permute-done.17 = bf16[256,128]{1,0:T(8,128)(2,1)S(1)} collective-permute-done((bf16[256,128]{1,0:T(8,128)(2,1)S(1)}, bf16[256,128]{1,0:T(8,128)(2,1)S(1)}, u32[]{:S(2)}, u32[]{:S(2)}) %collective-permute-start.17) | collective-permute-done | bytes 65568 | tf_op jit(solution)/shard_map/ppermute | solution.py:59
  48.1 1.6 %collective-permute-start.18 = (bf16[256,128]{1,0:T(8,128)(2,1)S(1)}, bf16[256,128]{1,0:T(8,128)(2,1)S(1)}, u32[]{:S(2)}, u32[]{:S(2)}) collective-permute-start(bf16[256,128]{1,0:T(8,128)(2,1)S(1)} %add_convert_fusion.own_first), channel_id=1, source_target_pairs={{0,4},{4,0},{8,12},{12,8},{16,20},{20,16},{24,28},{28,24},{1,5},{5... | collective-permute-start | bytes 196616 | tf_op jit(solution)/shard_map/ppermute | solution.py:59
  49.7 1.9 %collective-permute-done.13 = bf16[384,128]{1,0:T(8,128)(2,1)S(1)} collective-permute-done((bf16[384,128]{1,0:T(8,128)(2,1)S(1)}, bf16[384,128]{1,0:T(8,128)(2,1)S(1)}, u32[]{:S(2)}, u32[]{:S(2)}) %collective-permute-start.13) | collective-permute-done | bytes 98336 | tf_op jit(solution)/shard_map/ppermute | solution.py:59
  51.7 0.0 copy-start.4
  51.7 0.1 collective-permute-start.14
  51.8 0.7 %collective-permute-done.18.got_first = bf16[256,128]{1,0:T(8,128)(2,1)S(1)} collective-permute-done((bf16[256,128]{1,0:T(8,128)(2,1)S(1)}, bf16[256,128]{1,0:T(8,128)(2,1)S(1)}, u32[]{:S(2)}, u32[]{:S(2)}) %collective-permute-start.18) | collective-permute-done | bytes 65568 | tf_op jit(solution)/shard_map/ppermute | solution.py:59
  52.5 3.6 %collective-permute-done.14.got_second = bf16[256,128]{1,0:T(8,128)(2,1)S(1)} collective-permute-done((bf16[256,128]{1,0:T(8,128)(2,1)S(1)}, bf16[256,128]{1,0:T(8,128)(2,1)S(1)}, u32[]{:S(2)}, u32[]{:S(2)}) %collective-permute-start.14) | collective-permute-done | bytes 65568 | tf_op jit(solution)/shard_map/ppermute | solution.py:59
  56.1 0.0 copy-done.4
  56.1 0.9 %finish.1 = (bf16[128,128]{1,0:T(8,128)(2,1)}, f32[512,128]{1,0:T(8,128)}, f32[512,128]{1,0:T(8,128)}) custom-call(bf16[128,128]{1,0:T(8,128)(2,1)S(1)} %copy-done.4, f32[128,128]{1,0:T(8,128)S(1)} %slice_add_fusion.5.forward, bf16[256,128]{1,0:T(8,128)(2,1)S(1)} %fusion.own_second, bf16[256,128]{1,0:T(8,128)(2,1)S(1)} %collective-permute-done.14.got_second, ...), custom_call_target="tpu_custom_call" | custom-call | tf_op jit(solution)/shard_map/finish/pallas_call | solution.py:26
  (32 shorter events, 0.5 us)
Async XLA Ops:
  1.8 2.1 %collective-permute-start = (f32[2,128,128]{2,1,0:T(8,128)S(1)}, f32[2,128,128]{2,1,0:T(8,128)S(1)}, u32[]{:S(2)}, u32[]{:S(2)}) collective-permute-start(f32[2,128,128]{2,1,0:T(8,128)S(1)} %get-tuple-element.21), channel_id=1, source_target_pairs={{0,1},{1,0},{2,3},{3,2},{4,5},{5,4},{6,7},{7,6},{8,9},{9,8},{10,11... | collective-permute-start | bytes 393224 | tf_op jit(solution)/shard_map/ppermute | solution.py:59
  3.9 15.3 %copy-start = (bf16[1024,512]{1,0:T(8,128)(2,1)S(1)}, bf16[1024,512]{1,0:T(8,128)(2,1)}, u32[]{:S(2)}) copy-start(bf16[1024,512]{1,0:T(8,128)(2,1)} %latent.1) | copy-start | bytes 3145732
  4.0 4.9 %collective-permute-start.1 = (bf16[128,128]{1,0:T(8,128)(2,1)S(1)}, bf16[128,128]{1,0:T(8,128)(2,1)S(1)}, u32[]{:S(2)}, u32[]{:S(2)}) collective-permute-start(bf16[128,128]{1,0:T(8,128)(2,1)S(1)} %get-tuple-element.42), channel_id=1, source_target_pairs={{0,2},{1,3},{2,0},{3,1},{4,6},{5,7},{6,4},{7,5},{8,10},{9,11},{10,... | collective-permute-start | bytes 98312 | tf_op jit(solution)/shard_map/ppermute | solution.py:59
  6.3 9.3 %collective-permute-start.6 = (bf16[128,128]{1,0:T(8,128)(2,1)S(1)}, bf16[128,128]{1,0:T(8,128)(2,1)S(1)}, u32[]{:S(2)}, u32[]{:S(2)}) collective-permute-start(bf16[128,128]{1,0:T(8,128)(2,1)S(1)} %get-tuple-element.42), channel_id=1, source_target_pairs={{0,18},{1,19},{2,16},{3,17},{4,22},{5,23},{6,20},{7,21},{8,26},{9,... | collective-permute-start | bytes 98312 | tf_op jit(solution)/shard_map/ppermute | solution.py:79
  8.9 10.3 %copy-start.2 = (bf16[512,512]{1,0:T(8,128)(2,1)S(1)}, bf16[512,512]{1,0:T(8,128)(2,1)}, u32[]{:S(2)}) copy-start(bf16[512,512]{1,0:T(8,128)(2,1)} %first.1) | copy-start | bytes 1572868
  8.9 6.6 %collective-permute-start.5 = (bf16[256,128]{1,0:T(8,128)(2,1)S(1)}, bf16[256,128]{1,0:T(8,128)(2,1)S(1)}, u32[]{:S(2)}, u32[]{:S(2)}) collective-permute-start(bf16[256,128]{1,0:T(8,128)(2,1)S(1)} %get-tuple-element.44), channel_id=1, source_target_pairs={{0,16},{4,20},{8,24},{12,28},{16,0},{20,4},{24,8},{28,12},{1,17},{... | collective-permute-start | bytes 196616 | tf_op jit(solution)/shard_map/ppermute | solution.py:59
  11.5 9.3 %collective-permute-start.2 = (bf16[272,128]{1,0:T(8,128)(2,1)S(1)}, bf16[272,128]{1,0:T(8,128)(2,1)S(1)}, u32[]{:S(2)}, u32[]{:S(2)}) collective-permute-start(bf16[272,128]{1,0:T(8,128)(2,1)S(1)} %get-tuple-element.39), channel_id=1, source_target_pairs={{0,0},{1,5},{2,10},{3,15},{4,4},{5,1},{6,14},{7,11},{8,8},{9,13},{... | collective-permute-start | bytes 208904 | tf_op jit(solution)/shard_map/ppermute | solution.py:69
  12.2 8.7 %collective-permute-start.3 = (bf16[272,128]{1,0:T(8,128)(2,1)S(1)}, bf16[272,128]{1,0:T(8,128)(2,1)S(1)}, u32[]{:S(2)}, u32[]{:S(2)}) collective-permute-start(bf16[272,128]{1,0:T(8,128)(2,1)S(1)} %get-tuple-element.40), channel_id=1, source_target_pairs={{0,16},{1,21},{2,26},{3,31},{4,20},{5,17},{6,30},{7,27},{8,24},{9,... | collective-permute-start | bytes 208904 | tf_op jit(solution)/shard_map/ppermute | solution.py:69
  15.6 3.6 %copy-start.3 = (bf16[512,128]{1,0:T(8,128)(2,1)S(1)}, bf16[512,128]{1,0:T(8,128)(2,1)}, u32[]{:S(2)}) copy-start(bf16[512,128]{1,0:T(8,128)(2,1)} %second.1) | copy-start | bytes 393220
  15.6 7.9 %collective-permute-start.7 = (bf16[2,256,128]{2,1,0:T(8,128)(2,1)S(1)}, bf16[2,256,128]{2,1,0:T(8,128)(2,1)S(1)}, u32[]{:S(2)}, u32[]{:S(2)}) collective-permute-start(bf16[2,256,128]{2,1,0:T(8,128)(2,1)S(1)} %pad_maximum_fusion.1), channel_id=1, source_target_pairs={{0,4},{4,0},{8,12},{12,8},{16,20},{20,16},{24,28},{28,24},{1,5},{5... | collective-permute-start | bytes 393224 | tf_op jit(solution)/shard_map/ppermute | solution.py:59
  17.1 6.4 %collective-permute-start.8 = (bf16[2,256,128]{2,1,0:T(8,128)(2,1)S(1)}, bf16[2,256,128]{2,1,0:T(8,128)(2,1)S(1)}, u32[]{:S(2)}, u32[]{:S(2)}) collective-permute-start(bf16[2,256,128]{2,1,0:T(8,128)(2,1)S(1)} %pad_maximum_fusion.1), channel_id=1, source_target_pairs={{0,8},{4,12},{8,0},{12,4},{16,24},{20,28},{24,16},{28,20},{1,9},{5... | collective-permute-start | bytes 393224 | tf_op jit(solution)/shard_map/ppermute | solution.py:59
  17.4 7.5 %collective-permute-start.9 = (bf16[2,256,128]{2,1,0:T(8,128)(2,1)S(1)}, bf16[2,256,128]{2,1,0:T(8,128)(2,1)S(1)}, u32[]{:S(2)}, u32[]{:S(2)}) collective-permute-start(bf16[2,256,128]{2,1,0:T(8,128)(2,1)S(1)} %pad_maximum_fusion.1), channel_id=1, source_target_pairs={{0,12},{4,8},{8,4},{12,0},{16,28},{20,24},{24,20},{28,16},{1,13},{... | collective-permute-start | bytes 393224 | tf_op jit(solution)/shard_map/ppermute | solution.py:59
  20.8 4.2 %copy-start.1 = (f32[128,1024]{1,0:T(8,128)}, f32[128,1024]{1,0:T(8,128)S(1)}, u32[]{:S(2)}) copy-start(f32[128,1024]{1,0:T(8,128)S(1)} %get-tuple-element.29.slope_hbm) | copy-start | bytes 1572868
  20.8 5.8 %collective-permute-start.4 = (bf16[1,2,272,128]{3,2,1,0:T(8,128)(2,1)S(1)}, bf16[1,2,272,128]{3,2,1,0:T(8,128)(2,1)S(1)}, u32[]{:S(2)}, u32[]{:S(2)}) collective-permute-start(bf16[1,2,272,128]{3,2,1,0:T(8,128)(2,1)S(1)} %maximum_bitcast_fusion), channel_id=1, source_target_pairs={{0,2},{1,3},{2,0},{3,1},{4,6},{5,7},{6,4},{7,5},{8,10},{9,11},{10,... | collective-permute-start | bytes 417800 | tf_op jit(solution)/shard_map/ppermute | solution.py:59
  26.6 1.6 %collective-permute-start.10 = (bf16[2,2,272,128]{3,2,1,0:T(8,128)(2,1)S(1)}, bf16[2,2,272,128]{3,2,1,0:T(8,128)(2,1)S(1)}, u32[]{:S(2)}, u32[]{:S(2)}) collective-permute-start(bf16[2,2,272,128]{3,2,1,0:T(8,128)(2,1)S(1)} %get-tuple-element.27.near), channel_id=1, source_target_pairs={{0,1},{1,0},{2,3},{3,2},{4,5},{5,4},{6,7},{7,6},{8,9},{9,8},{10,11... | collective-permute-start | bytes 835592 | tf_op jit(solution)/shard_map/ppermute | solution.py:59
  30.9 4.3 %collective-permute-start.15 = (bf16[256,128]{1,0:T(8,128)(2,1)S(1)}, bf16[256,128]{1,0:T(8,128)(2,1)S(1)}, u32[]{:S(2)}, u32[]{:S(2)}) collective-permute-start(bf16[256,128]{1,0:T(8,128)(2,1)S(1)} %get-tuple-element.34), channel_id=1, source_target_pairs={{0,4},{4,0},{8,12},{12,8},{16,20},{20,16},{24,28},{28,24},{1,5},{5... | collective-permute-start | bytes 196616 | tf_op jit(solution)/shard_map/ppermute | solution.py:59
  32.4 7.4 %collective-permute-start.11 = (bf16[768,128]{1,0:T(8,128)(2,1)S(1)}, bf16[768,128]{1,0:T(8,128)(2,1)S(1)}, u32[]{:S(2)}, u32[]{:S(2)}) collective-permute-start(bf16[768,128]{1,0:T(8,128)(2,1)S(1)} %get-tuple-element.31), channel_id=1, source_target_pairs={{0,8},{4,12},{8,0},{12,4},{16,24},{20,28},{24,16},{28,20},{1,9},{5... | collective-permute-start | bytes 589832 | tf_op jit(solution)/shard_map/ppermute | solution.py:59
  35.2 5.3 %collective-permute-start.16 = (bf16[256,128]{1,0:T(8,128)(2,1)S(1)}, bf16[256,128]{1,0:T(8,128)(2,1)S(1)}, u32[]{:S(2)}, u32[]{:S(2)}) collective-permute-start(bf16[256,128]{1,0:T(8,128)(2,1)S(1)} %add_convert_fusion.2), channel_id=1, source_target_pairs={{0,8},{4,12},{8,0},{12,4},{16,24},{20,28},{24,16},{28,20},{1,9},{5... | collective-permute-start | bytes 196616 | tf_op jit(solution)/shard_map/ppermute | solution.py:59
  39.9 5.0 %collective-permute-start.12 = (bf16[512,128]{1,0:T(8,128)(2,1)S(1)}, bf16[512,128]{1,0:T(8,128)(2,1)S(1)}, u32[]{:S(2)}, u32[]{:S(2)}) collective-permute-start(bf16[512,128]{1,0:T(8,128)(2,1)S(1)} %pad_maximum_fusion.2), channel_id=1, source_target_pairs={{0,4},{4,0},{8,12},{12,8},{16,20},{20,16},{24,28},{28,24},{1,5},{5... | collective-permute-start | bytes 393224 | tf_op jit(solution)/shard_map/ppermute | solution.py:59
  40.6 7.6 %collective-permute-start.17 = (bf16[256,128]{1,0:T(8,128)(2,1)S(1)}, bf16[256,128]{1,0:T(8,128)(2,1)S(1)}, u32[]{:S(2)}, u32[]{:S(2)}) collective-permute-start(bf16[256,128]{1,0:T(8,128)(2,1)S(1)} %add_convert_fusion.1), channel_id=1, source_target_pairs={{0,16},{4,20},{8,24},{12,28},{16,0},{20,4},{24,8},{28,12},{1,17},{... | collective-permute-start | bytes 196616 | tf_op jit(solution)/shard_map/ppermute | solution.py:59
  45.0 6.7 %collective-permute-start.13 = (bf16[384,128]{1,0:T(8,128)(2,1)S(1)}, bf16[384,128]{1,0:T(8,128)(2,1)S(1)}, u32[]{:S(2)}, u32[]{:S(2)}) collective-permute-start(bf16[384,128]{1,0:T(8,128)(2,1)S(1)} %pad_maximum_fusion.3), channel_id=1, source_target_pairs={{0,16},{4,20},{8,24},{12,28},{16,0},{20,4},{24,8},{28,12},{1,17},{... | collective-permute-start | bytes 294920 | tf_op jit(solution)/shard_map/ppermute | solution.py:59
  48.1 4.3 %collective-permute-start.18 = (bf16[256,128]{1,0:T(8,128)(2,1)S(1)}, bf16[256,128]{1,0:T(8,128)(2,1)S(1)}, u32[]{:S(2)}, u32[]{:S(2)}) collective-permute-start(bf16[256,128]{1,0:T(8,128)(2,1)S(1)} %add_convert_fusion.own_first), channel_id=1, source_target_pairs={{0,4},{4,0},{8,12},{12,8},{16,20},{20,16},{24,28},{28,24},{1,5},{5... | collective-permute-start | bytes 196616 | tf_op jit(solution)/shard_map/ppermute | solution.py:59
  51.7 4.3 %copy-start.4 = (bf16[128,128]{1,0:T(8,128)(2,1)S(1)}, bf16[128,128]{1,0:T(8,128)(2,1)}, u32[]{:S(2)}) copy-start(bf16[128,128]{1,0:T(8,128)(2,1)} %mesh_latent.1) | copy-start | bytes 98308
  51.7 4.3 %collective-permute-start.14 = (bf16[256,128]{1,0:T(8,128)(2,1)S(1)}, bf16[256,128]{1,0:T(8,128)(2,1)S(1)}, u32[]{:S(2)}, u32[]{:S(2)}) collective-permute-start(bf16[256,128]{1,0:T(8,128)(2,1)S(1)} %fusion.own_second), channel_id=1, source_target_pairs={{0,8},{4,12},{8,0},{12,4},{16,24},{20,28},{24,16},{28,20},{1,9},{5... | collective-permute-start | bytes 196616 | tf_op jit(solution)/shard_map/ppermute | solution.py:59

commit v5 on v4

--- a/solution.py
+++ b/solution.py
@@ -267,39 +267,28 @@
         ].astype(BF16)
 
 
-def finish_kernel(
-    second_offset,
-    first_offset,
-    mesh_latent,
-    forward,
-    own_second,
-    got_second,
-    own_first,
-    got_first,
-    mesh_hbm,
-    first_hbm,
-    second_hbm,
-    mesh,
-    first,
-    second,
-    departures,
+def lay(offset, own, got, whole, target, departure):
+    half = own.shape[0]
+    upper = (lax.axis_index("patch") // offset) % 2
+    whole[pl.ds(pl.multiple_of(upper * half, half), half)] = own[...].astype(F32)
+    whole[pl.ds(pl.multiple_of((1 - upper) * half, half), half)] = got[...].astype(F32)
+    copy = pltpu.make_async_copy(whole, target, departure)
+    copy.start()
+    return copy
+
+
+def finish_first_kernel(
+    offset, mesh_latent, forward, own, got, mesh_hbm, first_hbm, mesh, first, departures
 ):
     mesh[...] = (mesh_latent[...].astype(F32) + forward[...]).astype(BF16)
-    copies = []
-    for place, offset, own, got, whole, target in (
-        (0, second_offset, own_second, got_second, second, second_hbm),
-        (1, first_offset, own_first, got_first, first, first_hbm),
-    ):
-        half = own.shape[0]
-        upper = (lax.axis_index("patch") // offset) % 2
-        whole[pl.ds(pl.multiple_of(upper * half, half), half)] = own[...].astype(F32)
-        whole[pl.ds(pl.multiple_of((1 - upper) * half, half), half)] = got[...].astype(F32)
-        copies.append(pltpu.make_async_copy(whole, target, departures.at[place]))
-        copies[-1].start()
-    copies.append(pltpu.make_async_copy(mesh, mesh_hbm, departures.at[2]))
-    copies[-1].start()
-    for copy in copies:
-        copy.wait()
+    out = pltpu.make_async_copy(mesh, mesh_hbm, departures.at[0])
+    out.start()
+    lay(offset, own, got, first, first_hbm, departures.at[1]).wait()
+    out.wait()
+
+
+def finish_second_kernel(offset, own, got, second_hbm, second, departures):
+    lay(offset, own, got, second, second_hbm, departures.at[0]).wait()
 
 
 def per_device(
@@ -458,28 +447,28 @@
             kept_second = sent_second[:split].astype(F32)
             kept_first = sent_first.astype(F32)
     second = second.astype(BF16)
-    mesh_out, first, second = call(
-        functools.partial(finish_kernel, second_order[0], first_order[0]),
-        "finish",
+    mesh_out, first = call(
+        functools.partial(finish_first_kernel, first_order[0]),
+        "finish_first",
         [
             (VMEM, mesh_latent),
             (VMEM, forward),
-            (VMEM, second),
-            (VMEM, swap(second, "patch", second_order[0])),
             (VMEM, sent_first),
             (VMEM, swap(sent_first, "patch", first_order[0])),
         ],
-        [
-            (HBM, (rows, width), BF16),
-            (HBM, (depth, hidden_local), F32),
-            (HBM, (hidden_width, width), F32),
-        ],
+        [(HBM, (rows, width), BF16), (HBM, (depth, hidden_local), F32)],
         scratch=[
             VMEM((rows, width), BF16),
             VMEM((depth, hidden_local), F32),
-            VMEM((hidden_width, width), F32),
-            pltpu.SemaphoreType.DMA((3,)),
-        ],
+            pltpu.SemaphoreType.DMA((2,)),
+        ],
+    )
+    (second,) = call(
+        functools.partial(finish_second_kernel, second_order[0]),
+        "finish_second",
+        [(VMEM, second), (VMEM, swap(second, "patch", second_order[0]))],
+        [(HBM, (hidden_width, width), F32)],
+        scratch=[VMEM((hidden_width, width), F32), pltpu.SemaphoreType.DMA((1,))],
     )
     return (mesh_out, first, second)
 

time: 57.1 us -> 57 us (level)
  waiting for transfers between devices: 24.7 us -> 24.1 us
    ppermute x16, waiting for transfers between devices: 24.7 us -> 24.1 us  [swap(): return lax.ppermute(value, axis, [(i, i ^ offset) for i in range(size)])]
    pallas_call x5 -> x6, Pallas kernels: 7.49 us -> 7.93 us  [call(): pl.pallas_call(kernel, out_shape=[space(shape, dtype) for space, shape, d...]
  transfers between devices with their start and end apart: 19 -> 19, of which waited for: 11 -> 12; matrix products, arithmetic and copies ran while one was open for 1% -> 1% of each run, Pallas kernels for 5% -> 6%
where the time goes in v5:
time: 57 us; the launch traced here: 56.8 us
  waiting for transfers between devices  24.1 us (42%)
  starting transfers between devices  22.9 us (40%)
  Pallas kernels  7.93 us (14%)
  between operations  1 us (2%)
    ppermute x16, waiting for transfers between devices, swap(): return lax.ppermute(value, axis, [(i, i ^ offset) for i in range(size)])  24.1 us
    ppermute x16, starting transfers between devices, swap(): return lax.ppermute(value, axis, [(i, i ^ offset) for i in range(size)])  19.2 us
    pallas_call x6, Pallas kernels, call(): pl.pallas_call(kernel, out_shape=[space(shape, dtype) for space, shape, d...  7.93 us
    ppermute x1, starting transfers between devices, swap_both(): return lax.ppermute(value, ('patch', 'mp'), pairs)  2.54 us
    ppermute x2, starting transfers between devices, spread(): return lax.ppermute(value, ('patch', 'mp'), pairs)  1.21 us
  transfers between devices with their start and end apart: 19, of which 12 were waited for; matrix products, arithmetic and copies ran while one was open for 1% of the time, Pallas kernels for 6%

profile of v5, /device:TPU:0, one launch (start us, length us, event | category | flops | bytes accessed | tf_op | source)
XLA Modules:
  0.0 56.8 jit_solution(3106533359722695766)
XLA Ops:
  0.6 1.1 %term.1 = (f32[2,128,128]{2,1,0:T(8,128)S(1)}, f32[2,128,128]{2,1,0:T(8,128)S(1)}, bf16[128,128]{1,0:T(8,128)(2,1)S(1)}) custom-call(bf16[128,128]{1,0:T(8,128)(2,1)} %cotangent_hbm.1, bf16[512,128]{1,0:T(8,128)(2,1)} %second.1), custom_call_target="tpu_custom_call" | custom-call | tf_op jit(solution)/shard_map/term/pallas_call | solution.py:26
  1.8 0.5 collective-permute-start
  2.3 1.4 %pack.1 = bf16[2,272,128]{2,1,0:T(8,128)(2,1)S(1)} custom-call(s32[12]{0:T(128)} %source_hbm.1, s32[12]{0:T(128)} %live_hbm.1, bf16[12,128,128]{2,1,0:T(8,128)(2,1)} %weight_hbm.1), custom_call_target="tpu_custom_call" | custom-call | tf_op jit(solution)/shard_map/pack/pallas_call | solution.py:26
  3.7 0.0 copy-start
  3.7 0.0 collective-permute-done
  3.8 2.5 %collective-permute-start.1 = (bf16[128,128]{1,0:T(8,128)(2,1)S(1)}, bf16[128,128]{1,0:T(8,128)(2,1)S(1)}, u32[]{:S(2)}, u32[]{:S(2)}) collective-permute-start(bf16[128,128]{1,0:T(8,128)(2,1)S(1)} %get-tuple-element.46), channel_id=1, source_target_pairs={{0,2},{1,3},{2,0},{3,1},{4,6},{5,7},{6,4},{7,5},{8,10},{9,11},{10,... | collective-permute-start | bytes 98312 | tf_op jit(solution)/shard_map/ppermute | solution.py:59
  6.3 2.5 %collective-permute-start.6 = (bf16[128,128]{1,0:T(8,128)(2,1)S(1)}, bf16[128,128]{1,0:T(8,128)(2,1)S(1)}, u32[]{:S(2)}, u32[]{:S(2)}) collective-permute-start(bf16[128,128]{1,0:T(8,128)(2,1)S(1)} %get-tuple-element.46), channel_id=1, source_target_pairs={{0,18},{1,19},{2,16},{3,17},{4,22},{5,23},{6,20},{7,21},{8,26},{9,... | collective-permute-start | bytes 98312 | tf_op jit(solution)/shard_map/ppermute | solution.py:79
  8.9 0.0 collective-permute-done.1
  8.9 0.0 copy-start.2
  8.9 2.5 %collective-permute-start.5 = (bf16[256,128]{1,0:T(8,128)(2,1)S(1)}, bf16[256,128]{1,0:T(8,128)(2,1)S(1)}, u32[]{:S(2)}, u32[]{:S(2)}) collective-permute-start(bf16[256,128]{1,0:T(8,128)(2,1)S(1)} %get-tuple-element.48), channel_id=1, source_target_pairs={{0,16},{4,20},{8,24},{12,28},{16,0},{20,4},{24,8},{28,12},{1,17},{... | collective-permute-start | bytes 196616 | tf_op jit(solution)/shard_map/ppermute | solution.py:59
  11.5 0.7 %collective-permute-start.2 = (bf16[272,128]{1,0:T(8,128)(2,1)S(1)}, bf16[272,128]{1,0:T(8,128)(2,1)S(1)}, u32[]{:S(2)}, u32[]{:S(2)}) collective-permute-start(bf16[272,128]{1,0:T(8,128)(2,1)S(1)} %get-tuple-element.43), channel_id=1, source_target_pairs={{0,0},{1,5},{2,10},{3,15},{4,4},{5,1},{6,14},{7,11},{8,8},{9,13},{... | collective-permute-start | bytes 208904 | tf_op jit(solution)/shard_map/ppermute | solution.py:69
  12.1 0.5 collective-permute-start.3
  12.7 2.9 %collective-permute-done.5 = bf16[256,128]{1,0:T(8,128)(2,1)S(1)} collective-permute-done((bf16[256,128]{1,0:T(8,128)(2,1)S(1)}, bf16[256,128]{1,0:T(8,128)(2,1)S(1)}, u32[]{:S(2)}, u32[]{:S(2)}) %collective-permute-start.5) | collective-permute-done | bytes 65568 | tf_op jit(solution)/shard_map/ppermute | solution.py:59
  15.6 0.0 collective-permute-done.6
  15.6 0.0 copy-start.3
  15.6 1.5 %collective-permute-start.7 = (bf16[2,256,128]{2,1,0:T(8,128)(2,1)S(1)}, bf16[2,256,128]{2,1,0:T(8,128)(2,1)S(1)}, u32[]{:S(2)}, u32[]{:S(2)}) collective-permute-start(bf16[2,256,128]{2,1,0:T(8,128)(2,1)S(1)} %pad_maximum_fusion.1), channel_id=1, source_target_pairs={{0,4},{4,0},{8,12},{12,8},{16,20},{20,16},{24,28},{28,24},{1,5},{5... | collective-permute-start | bytes 393224 | tf_op jit(solution)/shard_map/ppermute | solution.py:59
  17.2 0.2 collective-permute-start.8
  17.4 1.8 %collective-permute-start.9 = (bf16[2,256,128]{2,1,0:T(8,128)(2,1)S(1)}, bf16[2,256,128]{2,1,0:T(8,128)(2,1)S(1)}, u32[]{:S(2)}, u32[]{:S(2)}) collective-permute-start(bf16[2,256,128]{2,1,0:T(8,128)(2,1)S(1)} %pad_maximum_fusion.1), channel_id=1, source_target_pairs={{0,12},{4,8},{8,4},{12,0},{16,28},{20,24},{24,20},{28,16},{1,13},{... | collective-permute-start | bytes 393224 | tf_op jit(solution)/shard_map/ppermute | solution.py:59
  19.2 0.0 copy-done
  19.2 0.0 copy-done.2
  19.2 0.0 copy-done.3
  19.2 1.5 %local.1 = (bf16[1024,512]{1,0:T(8,128)(2,1)S(1)}, bf16[1024,128]{1,0:T(8,128)(2,1)S(1)}, f32[128,1024]{1,0:T(8,128)S(1)}) custom-call(bf16[1024,512]{1,0:T(8,128)(2,1)S(1)} %copy-done, bf16[512,512]{1,0:T(8,128)(2,1)S(1)} %copy-done.2, bf16[512,128]{1,0:T(8,128)(2,1)S(1)} %copy-done.3), custom_call_target="tpu_custom_call" | custom-call | tf_op jit(solution)/shard_map/local/pallas_call | solution.py:26
  20.8 0.0 copy-start.1
  20.8 0.0 collective-permute-done.2
  20.8 0.0 collective-permute-done.3
  20.8 2.6 %collective-permute-start.4 = (bf16[1,2,272,128]{3,2,1,0:T(8,128)(2,1)S(1)}, bf16[1,2,272,128]{3,2,1,0:T(8,128)(2,1)S(1)}, u32[]{:S(2)}, u32[]{:S(2)}) collective-permute-start(bf16[1,2,272,128]{3,2,1,0:T(8,128)(2,1)S(1)} %maximum_bitcast_fusion), channel_id=1, source_target_pairs={{0,2},{1,3},{2,0},{3,1},{4,6},{5,7},{6,4},{7,5},{8,10},{9,11},{10,... | collective-permute-start | bytes 417800 | tf_op jit(solution)/shard_map/ppermute | solution.py:59
  23.4 0.0 collective-permute-done.7
  23.4 0.0 collective-permute-done.8
  23.4 1.5 %collective-permute-done.9 = bf16[2,256,128]{2,1,0:T(8,128)(2,1)S(1)} collective-permute-done((bf16[2,256,128]{2,1,0:T(8,128)(2,1)S(1)}, bf16[2,256,128]{2,1,0:T(8,128)(2,1)S(1)}, u32[]{:S(2)}, u32[]{:S(2)}) %collective-permute-start.9) | collective-permute-done | bytes 131104 | tf_op jit(solution)/shard_map/ppermute | solution.py:59
  24.9 0.0 copy-done.1
  24.9 1.5 %collective-permute-done.4 = bf16[1,2,272,128]{3,2,1,0:T(8,128)(2,1)S(1)} collective-permute-done((bf16[1,2,272,128]{3,2,1,0:T(8,128)(2,1)S(1)}, bf16[1,2,272,128]{3,2,1,0:T(8,128)(2,1)S(1)}, u32[]{:S(2)}, u32[]{:S(2)}) %collective-permute-start.4) | collective-permute-done | bytes 139296 | tf_op jit(solution)/shard_map/ppermute | solution.py:59
  26.5 0.1 collective-permute-start.10
  26.5 1.5 %collective-permute-done.10.far = bf16[2,2,272,128]{3,2,1,0:T(8,128)(2,1)S(1)} collective-permute-done((bf16[2,2,272,128]{3,2,1,0:T(8,128)(2,1)S(1)}, bf16[2,2,272,128]{3,2,1,0:T(8,128)(2,1)S(1)}, u32[]{:S(2)}, u32[]{:S(2)}) %collective-permute-start.10) | collective-permute-done | bytes 278560 | tf_op jit(solution)/shard_map/ppermute | solution.py:59
  28.1 0.1 copy.12
  28.2 0.1 reshape.11.places
  28.3 2.4 %gradients.1 = (bf16[768,128]{1,0:T(8,128)(2,1)S(1)}, f32[256,128]{1,0:T(8,128)S(1)}, f32[512,128]{1,0:T(8,128)S(1)}, bf16[256,128]{1,0:T(8,128)(2,1)S(1)}, f32[256,128]{1,0:T(8,128)S(1)}) custom-call(s32[16]{0:T(128)S(1)} %reshape.11.places, bf16[2,2,272,128]{3,2,1,0:T(8,128)(2,1)S(1)} %get-tuple-element.29.near, ...), custom_call_target="tpu_custom_call" | custom-call | tf_op jit(solution)/shard_map/gradients/pallas_call | solution.py:26
  30.7 1.8 %collective-permute-start.14 = (bf16[256,128]{1,0:T(8,128)(2,1)S(1)}, bf16[256,128]{1,0:T(8,128)(2,1)S(1)}, u32[]{:S(2)}, u32[]{:S(2)}) collective-permute-start(bf16[256,128]{1,0:T(8,128)(2,1)S(1)} %get-tuple-element.36), channel_id=1, source_target_pairs={{0,4},{4,0},{8,12},{12,8},{16,20},{20,16},{24,28},{28,24},{1,5},{5... | collective-permute-start | bytes 196616 | tf_op jit(solution)/shard_map/ppermute | solution.py:59
  32.5 0.0 collective-permute-start.11
  32.5 2.5 %collective-permute-done.14 = bf16[256,128]{1,0:T(8,128)(2,1)S(1)} collective-permute-done((bf16[256,128]{1,0:T(8,128)(2,1)S(1)}, bf16[256,128]{1,0:T(8,128)(2,1)S(1)}, u32[]{:S(2)}, u32[]{:S(2)}) %collective-permute-start.14) | collective-permute-done | bytes 65568 | tf_op jit(solution)/shard_map/ppermute | solution.py:59
  35.1 0.1 collective-permute-start.15
  35.1 4.8 %collective-permute-done.11 = bf16[768,128]{1,0:T(8,128)(2,1)S(1)} collective-permute-done((bf16[768,128]{1,0:T(8,128)(2,1)S(1)}, bf16[768,128]{1,0:T(8,128)(2,1)S(1)}, u32[]{:S(2)}, u32[]{:S(2)}) %collective-permute-start.11) | collective-permute-done | bytes 196640 | tf_op jit(solution)/shard_map/ppermute | solution.py:59
  40.0 0.4 collective-permute-start.12
  40.5 0.1 collective-permute-done.15
  40.6 1.6 %collective-permute-start.16 = (bf16[256,128]{1,0:T(8,128)(2,1)S(1)}, bf16[256,128]{1,0:T(8,128)(2,1)S(1)}, u32[]{:S(2)}, u32[]{:S(2)}) collective-permute-start(bf16[256,128]{1,0:T(8,128)(2,1)S(1)} %add_convert_fusion.1), channel_id=1, source_target_pairs={{0,16},{4,20},{8,24},{12,28},{16,0},{20,4},{24,8},{28,12},{1,17},{... | collective-permute-start | bytes 196616 | tf_op jit(solution)/shard_map/ppermute | solution.py:59
  42.3 2.8 %collective-permute-done.12 = bf16[512,128]{1,0:T(8,128)(2,1)S(1)} collective-permute-done((bf16[512,128]{1,0:T(8,128)(2,1)S(1)}, bf16[512,128]{1,0:T(8,128)(2,1)S(1)}, u32[]{:S(2)}, u32[]{:S(2)}) %collective-permute-start.12) | collective-permute-done | bytes 131104 | tf_op jit(solution)/shard_map/ppermute | solution.py:59
  45.2 1.6 %collective-permute-start.13 = (bf16[384,128]{1,0:T(8,128)(2,1)S(1)}, bf16[384,128]{1,0:T(8,128)(2,1)S(1)}, u32[]{:S(2)}, u32[]{:S(2)}) collective-permute-start(bf16[384,128]{1,0:T(8,128)(2,1)S(1)} %pad_maximum_fusion.3), channel_id=1, source_target_pairs={{0,16},{4,20},{8,24},{12,28},{16,0},{20,4},{24,8},{28,12},{1,17},{... | collective-permute-start | bytes 294920 | tf_op jit(solution)/shard_map/ppermute | solution.py:59
  46.8 1.2 %collective-permute-done.16 = bf16[256,128]{1,0:T(8,128)(2,1)S(1)} collective-permute-done((bf16[256,128]{1,0:T(8,128)(2,1)S(1)}, bf16[256,128]{1,0:T(8,128)(2,1)S(1)}, u32[]{:S(2)}, u32[]{:S(2)}) %collective-permute-start.16) | collective-permute-done | bytes 65568 | tf_op jit(solution)/shard_map/ppermute | solution.py:59
  48.0 1.7 %collective-permute-start.17 = (bf16[256,128]{1,0:T(8,128)(2,1)S(1)}, bf16[256,128]{1,0:T(8,128)(2,1)S(1)}, u32[]{:S(2)}, u32[]{:S(2)}) collective-permute-start(bf16[256,128]{1,0:T(8,128)(2,1)S(1)} %add_convert_fusion.own), channel_id=1, source_target_pairs={{0,4},{4,0},{8,12},{12,8},{16,20},{20,16},{24,28},{28,24},{1,5},{5... | collective-permute-start | bytes 196616 | tf_op jit(solution)/shard_map/ppermute | solution.py:59
  49.7 2.0 %collective-permute-done.13 = bf16[384,128]{1,0:T(8,128)(2,1)S(1)} collective-permute-done((bf16[384,128]{1,0:T(8,128)(2,1)S(1)}, bf16[384,128]{1,0:T(8,128)(2,1)S(1)}, u32[]{:S(2)}, u32[]{:S(2)}) %collective-permute-start.13) | collective-permute-done | bytes 98336 | tf_op jit(solution)/shard_map/ppermute | solution.py:59
  51.7 0.0 copy-start.4
  51.8 0.1 collective-permute-start.18
  51.9 0.5 collective-permute-done.17.got
  52.4 0.1 copy-done.4
  52.5 0.7 %finish_first.1 = (bf16[128,128]{1,0:T(8,128)(2,1)}, f32[512,128]{1,0:T(8,128)}) custom-call(bf16[128,128]{1,0:T(8,128)(2,1)S(1)} %copy-done.4, f32[128,128]{1,0:T(8,128)S(1)} %slice_add_fusion.5.forward, bf16[256,128]{1,0:T(8,128)(2,1)S(1)} %add_convert_fusion.own, bf16[256,128]{1,0:T(8,128)(2,1)S(1)} %collective-permute-done.17.got), custom_call_target="tpu_custom_call" | custom-call | tf_op jit(solution)/shard_map/finish_first/pallas_call | solution.py:26
  53.3 2.8 %collective-permute-done.18.got = bf16[256,128]{1,0:T(8,128)(2,1)S(1)} collective-permute-done((bf16[256,128]{1,0:T(8,128)(2,1)S(1)}, bf16[256,128]{1,0:T(8,128)(2,1)S(1)}, u32[]{:S(2)}, u32[]{:S(2)}) %collective-permute-start.18) | collective-permute-done | bytes 65568 | tf_op jit(solution)/shard_map/ppermute | solution.py:59
  56.1 0.7 %finish_second.1 = f32[512,128]{1,0:T(8,128)} custom-call(bf16[256,128]{1,0:T(8,128)(2,1)S(1)} %fusion.own, bf16[256,128]{1,0:T(8,128)(2,1)S(1)} %collective-permute-done.18.got), custom_call_target="tpu_custom_call" | custom-call | tf_op jit(solution)/shard_map/finish_second/pallas_call | solution.py:26
  (32 shorter events, 0.5 us)
Async XLA Ops:
  1.8 1.9 %collective-permute-start = (f32[2,128,128]{2,1,0:T(8,128)S(1)}, f32[2,128,128]{2,1,0:T(8,128)S(1)}, u32[]{:S(2)}, u32[]{:S(2)}) collective-permute-start(f32[2,128,128]{2,1,0:T(8,128)S(1)} %get-tuple-element.23), channel_id=1, source_target_pairs={{0,1},{1,0},{2,3},{3,2},{4,5},{5,4},{6,7},{7,6},{8,9},{9,8},{10,11... | collective-permute-start | bytes 393224 | tf_op jit(solution)/shard_map/ppermute | solution.py:59
  3.7 15.5 %copy-start = (bf16[1024,512]{1,0:T(8,128)(2,1)S(1)}, bf16[1024,512]{1,0:T(8,128)(2,1)}, u32[]{:S(2)}) copy-start(bf16[1024,512]{1,0:T(8,128)(2,1)} %latent.1) | copy-start | bytes 3145732
  3.8 5.1 %collective-permute-start.1 = (bf16[128,128]{1,0:T(8,128)(2,1)S(1)}, bf16[128,128]{1,0:T(8,128)(2,1)S(1)}, u32[]{:S(2)}, u32[]{:S(2)}) collective-permute-start(bf16[128,128]{1,0:T(8,128)(2,1)S(1)} %get-tuple-element.46), channel_id=1, source_target_pairs={{0,2},{1,3},{2,0},{3,1},{4,6},{5,7},{6,4},{7,5},{8,10},{9,11},{10,... | collective-permute-start | bytes 98312 | tf_op jit(solution)/shard_map/ppermute | solution.py:59
  6.3 9.2 %collective-permute-start.6 = (bf16[128,128]{1,0:T(8,128)(2,1)S(1)}, bf16[128,128]{1,0:T(8,128)(2,1)S(1)}, u32[]{:S(2)}, u32[]{:S(2)}) collective-permute-start(bf16[128,128]{1,0:T(8,128)(2,1)S(1)} %get-tuple-element.46), channel_id=1, source_target_pairs={{0,18},{1,19},{2,16},{3,17},{4,22},{5,23},{6,20},{7,21},{8,26},{9,... | collective-permute-start | bytes 98312 | tf_op jit(solution)/shard_map/ppermute | solution.py:79
  8.9 10.3 %copy-start.2 = (bf16[512,512]{1,0:T(8,128)(2,1)S(1)}, bf16[512,512]{1,0:T(8,128)(2,1)}, u32[]{:S(2)}) copy-start(bf16[512,512]{1,0:T(8,128)(2,1)} %first.1) | copy-start | bytes 1572868
  8.9 6.6 %collective-permute-start.5 = (bf16[256,128]{1,0:T(8,128)(2,1)S(1)}, bf16[256,128]{1,0:T(8,128)(2,1)S(1)}, u32[]{:S(2)}, u32[]{:S(2)}) collective-permute-start(bf16[256,128]{1,0:T(8,128)(2,1)S(1)} %get-tuple-element.48), channel_id=1, source_target_pairs={{0,16},{4,20},{8,24},{12,28},{16,0},{20,4},{24,8},{28,12},{1,17},{... | collective-permute-start | bytes 196616 | tf_op jit(solution)/shard_map/ppermute | solution.py:59
  11.5 9.3 %collective-permute-start.2 = (bf16[272,128]{1,0:T(8,128)(2,1)S(1)}, bf16[272,128]{1,0:T(8,128)(2,1)S(1)}, u32[]{:S(2)}, u32[]{:S(2)}) collective-permute-start(bf16[272,128]{1,0:T(8,128)(2,1)S(1)} %get-tuple-element.43), channel_id=1, source_target_pairs={{0,0},{1,5},{2,10},{3,15},{4,4},{5,1},{6,14},{7,11},{8,8},{9,13},{... | collective-permute-start | bytes 208904 | tf_op jit(solution)/shard_map/ppermute | solution.py:69
  12.1 8.7 %collective-permute-start.3 = (bf16[272,128]{1,0:T(8,128)(2,1)S(1)}, bf16[272,128]{1,0:T(8,128)(2,1)S(1)}, u32[]{:S(2)}, u32[]{:S(2)}) collective-permute-start(bf16[272,128]{1,0:T(8,128)(2,1)S(1)} %get-tuple-element.44), channel_id=1, source_target_pairs={{0,16},{1,21},{2,26},{3,31},{4,20},{5,17},{6,30},{7,27},{8,24},{9,... | collective-permute-start | bytes 208904 | tf_op jit(solution)/shard_map/ppermute | solution.py:69
  15.6 3.6 %copy-start.3 = (bf16[512,128]{1,0:T(8,128)(2,1)S(1)}, bf16[512,128]{1,0:T(8,128)(2,1)}, u32[]{:S(2)}) copy-start(bf16[512,128]{1,0:T(8,128)(2,1)} %second.1) | copy-start | bytes 393220
  15.6 7.8 %collective-permute-start.7 = (bf16[2,256,128]{2,1,0:T(8,128)(2,1)S(1)}, bf16[2,256,128]{2,1,0:T(8,128)(2,1)S(1)}, u32[]{:S(2)}, u32[]{:S(2)}) collective-permute-start(bf16[2,256,128]{2,1,0:T(8,128)(2,1)S(1)} %pad_maximum_fusion.1), channel_id=1, source_target_pairs={{0,4},{4,0},{8,12},{12,8},{16,20},{20,16},{24,28},{28,24},{1,5},{5... | collective-permute-start | bytes 393224 | tf_op jit(solution)/shard_map/ppermute | solution.py:59
  17.2 6.3 %collective-permute-start.8 = (bf16[2,256,128]{2,1,0:T(8,128)(2,1)S(1)}, bf16[2,256,128]{2,1,0:T(8,128)(2,1)S(1)}, u32[]{:S(2)}, u32[]{:S(2)}) collective-permute-start(bf16[2,256,128]{2,1,0:T(8,128)(2,1)S(1)} %pad_maximum_fusion.1), channel_id=1, source_target_pairs={{0,8},{4,12},{8,0},{12,4},{16,24},{20,28},{24,16},{28,20},{1,9},{5... | collective-permute-start | bytes 393224 | tf_op jit(solution)/shard_map/ppermute | solution.py:59
  17.4 7.5 %collective-permute-start.9 = (bf16[2,256,128]{2,1,0:T(8,128)(2,1)S(1)}, bf16[2,256,128]{2,1,0:T(8,128)(2,1)S(1)}, u32[]{:S(2)}, u32[]{:S(2)}) collective-permute-start(bf16[2,256,128]{2,1,0:T(8,128)(2,1)S(1)} %pad_maximum_fusion.1), channel_id=1, source_target_pairs={{0,12},{4,8},{8,4},{12,0},{16,28},{20,24},{24,20},{28,16},{1,13},{... | collective-permute-start | bytes 393224 | tf_op jit(solution)/shard_map/ppermute | solution.py:59
  20.8 4.2 %copy-start.1 = (f32[128,1024]{1,0:T(8,128)}, f32[128,1024]{1,0:T(8,128)S(1)}, u32[]{:S(2)}) copy-start(f32[128,1024]{1,0:T(8,128)S(1)} %get-tuple-element.31.slope_hbm) | copy-start | bytes 1572868
  20.8 5.6 %collective-permute-start.4 = (bf16[1,2,272,128]{3,2,1,0:T(8,128)(2,1)S(1)}, bf16[1,2,272,128]{3,2,1,0:T(8,128)(2,1)S(1)}, u32[]{:S(2)}, u32[]{:S(2)}) collective-permute-start(bf16[1,2,272,128]{3,2,1,0:T(8,128)(2,1)S(1)} %maximum_bitcast_fusion), channel_id=1, source_target_pairs={{0,2},{1,3},{2,0},{3,1},{4,6},{5,7},{6,4},{7,5},{8,10},{9,11},{10,... | collective-permute-start | bytes 417800 | tf_op jit(solution)/shard_map/ppermute | solution.py:59
  26.5 1.6 %collective-permute-start.10 = (bf16[2,2,272,128]{3,2,1,0:T(8,128)(2,1)S(1)}, bf16[2,2,272,128]{3,2,1,0:T(8,128)(2,1)S(1)}, u32[]{:S(2)}, u32[]{:S(2)}) collective-permute-start(bf16[2,2,272,128]{3,2,1,0:T(8,128)(2,1)S(1)} %get-tuple-element.29.near), channel_id=1, source_target_pairs={{0,1},{1,0},{2,3},{3,2},{4,5},{5,4},{6,7},{7,6},{8,9},{9,8},{10,11... | collective-permute-start | bytes 835592 | tf_op jit(solution)/shard_map/ppermute | solution.py:59
  30.7 4.3 %collective-permute-start.14 = (bf16[256,128]{1,0:T(8,128)(2,1)S(1)}, bf16[256,128]{1,0:T(8,128)(2,1)S(1)}, u32[]{:S(2)}, u32[]{:S(2)}) collective-permute-start(bf16[256,128]{1,0:T(8,128)(2,1)S(1)} %get-tuple-element.36), channel_id=1, source_target_pairs={{0,4},{4,0},{8,12},{12,8},{16,20},{20,16},{24,28},{28,24},{1,5},{5... | collective-permute-start | bytes 196616 | tf_op jit(solution)/shard_map/ppermute | solution.py:59
  32.5 7.4 %collective-permute-start.11 = (bf16[768,128]{1,0:T(8,128)(2,1)S(1)}, bf16[768,128]{1,0:T(8,128)(2,1)S(1)}, u32[]{:S(2)}, u32[]{:S(2)}) collective-permute-start(bf16[768,128]{1,0:T(8,128)(2,1)S(1)} %get-tuple-element.33), channel_id=1, source_target_pairs={{0,8},{4,12},{8,0},{12,4},{16,24},{20,28},{24,16},{28,20},{1,9},{5... | collective-permute-start | bytes 589832 | tf_op jit(solution)/shard_map/ppermute | solution.py:59
  35.1 5.6 %collective-permute-start.15 = (bf16[256,128]{1,0:T(8,128)(2,1)S(1)}, bf16[256,128]{1,0:T(8,128)(2,1)S(1)}, u32[]{:S(2)}, u32[]{:S(2)}) collective-permute-start(bf16[256,128]{1,0:T(8,128)(2,1)S(1)} %add_convert_fusion.2), channel_id=1, source_target_pairs={{0,8},{4,12},{8,0},{12,4},{16,24},{20,28},{24,16},{28,20},{1,9},{5... | collective-permute-start | bytes 196616 | tf_op jit(solution)/shard_map/ppermute | solution.py:59
  40.0 5.0 %collective-permute-start.12 = (bf16[512,128]{1,0:T(8,128)(2,1)S(1)}, bf16[512,128]{1,0:T(8,128)(2,1)S(1)}, u32[]{:S(2)}, u32[]{:S(2)}) collective-permute-start(bf16[512,128]{1,0:T(8,128)(2,1)S(1)} %pad_maximum_fusion.2), channel_id=1, source_target_pairs={{0,4},{4,0},{8,12},{12,8},{16,20},{20,16},{24,28},{28,24},{1,5},{5... | collective-permute-start | bytes 393224 | tf_op jit(solution)/shard_map/ppermute | solution.py:59
  40.6 7.4 %collective-permute-start.16 = (bf16[256,128]{1,0:T(8,128)(2,1)S(1)}, bf16[256,128]{1,0:T(8,128)(2,1)S(1)}, u32[]{:S(2)}, u32[]{:S(2)}) collective-permute-start(bf16[256,128]{1,0:T(8,128)(2,1)S(1)} %add_convert_fusion.1), channel_id=1, source_target_pairs={{0,16},{4,20},{8,24},{12,28},{16,0},{20,4},{24,8},{28,12},{1,17},{... | collective-permute-start | bytes 196616 | tf_op jit(solution)/shard_map/ppermute | solution.py:59
  45.2 6.5 %collective-permute-start.13 = (bf16[384,128]{1,0:T(8,128)(2,1)S(1)}, bf16[384,128]{1,0:T(8,128)(2,1)S(1)}, u32[]{:S(2)}, u32[]{:S(2)}) collective-permute-start(bf16[384,128]{1,0:T(8,128)(2,1)S(1)} %pad_maximum_fusion.3), channel_id=1, source_target_pairs={{0,16},{4,20},{8,24},{12,28},{16,0},{20,4},{24,8},{28,12},{1,17},{... | collective-permute-start | bytes 294920 | tf_op jit(solution)/shard_map/ppermute | solution.py:59
  48.0 4.3 %collective-permute-start.17 = (bf16[256,128]{1,0:T(8,128)(2,1)S(1)}, bf16[256,128]{1,0:T(8,128)(2,1)S(1)}, u32[]{:S(2)}, u32[]{:S(2)}) collective-permute-start(bf16[256,128]{1,0:T(8,128)(2,1)S(1)} %add_convert_fusion.own), channel_id=1, source_target_pairs={{0,4},{4,0},{8,12},{12,8},{16,20},{20,16},{24,28},{28,24},{1,5},{5... | collective-permute-start | bytes 196616 | tf_op jit(solution)/shard_map/ppermute | solution.py:59
  51.7 0.8 %copy-start.4 = (bf16[128,128]{1,0:T(8,128)(2,1)S(1)}, bf16[128,128]{1,0:T(8,128)(2,1)}, u32[]{:S(2)}) copy-start(bf16[128,128]{1,0:T(8,128)(2,1)} %mesh_latent.1) | copy-start | bytes 98308
  51.8 4.3 %collective-permute-start.18 = (bf16[256,128]{1,0:T(8,128)(2,1)S(1)}, bf16[256,128]{1,0:T(8,128)(2,1)S(1)}, u32[]{:S(2)}, u32[]{:S(2)}) collective-permute-start(bf16[256,128]{1,0:T(8,128)(2,1)S(1)} %fusion.own), channel_id=1, source_target_pairs={{0,8},{4,12},{8,0},{12,4},{16,24},{20,28},{24,16},{28,20},{1,9},{5... | collective-permute-start | bytes 196616 | tf_op jit(solution)/shard_map/ppermute | solution.py:59
